TPU v7x, 128 devices: a whole 4x4x4 slice. The times are simulated.
128 devices in a mesh: prow: 16 (over y, x_hi, core), pcol: 8 (over z, x_lo).
Axes of the slice: x: 4 (x_hi: 2, x_lo: 2; x = x_hi * 2 + x_lo), y: 4, z: 4, core: 2. Of those that a mesh axis runs over, the one named last changes fastest.
Arguments:
- sigma_anc: bfloat16 [8192, 8192], P('prow', 'pcol'), as said below
- lower_blocks: bfloat16 [32, 16, 256, 256], P('pcol', None, 'prow'), may hold values from -0.09375 to 0.09375
- row_blocks: int32 [32, 16], replicated, may hold values from 0 to 31, as said below
- slot_of: int32 [32], replicated, may hold values from 0 to 31, each once
- inv_diag: float32 [32, 256, 256], P('pcol', 'prow'), as said below
Outputs:
- sigma_off: bfloat16 [8192, 8192], P('prow', 'pcol')
- sigma_diag: float32 [32, 256, 256], P('pcol', 'prow')
Inputs may be any that keep to these rules, and one draw needn't show every extreme that they name: `row_blocks`: each row holds 16 distinct ancestor indices in increasing order. `sigma_anc`: symmetric. `inv_diag`: symmetric.
All inputs are finite; a program needn't handle non-finite values.
Results may differ from a plain program's by a relative error of at most 0.015.
Values may be sent and summed in bfloat16 or wider, within the bound.
No kernel may reach another device: no remote copies, remote signals or barrier semaphores. Data moves between devices by JAX's collectives and lax.ppermute only.
A program may use at most 128 MiB of HBM per device.

v0:
```python
import jax
import jax.numpy as jnp
from jax import lax
from jax.sharding import PartitionSpec as P


def per_device(sigma_anc, lower_blocks, row_blocks, slot_of, inv_diag):
    row_index = lax.axis_index("prow")
    col_index = lax.axis_index("pcol")
    sup_dev = lower_blocks.shape[0]
    width = lower_blocks.shape[3]
    ancestors = slot_of.shape[0]
    rows_here = sigma_anc.shape[0]
    blocks_here = rows_here // width
    full_blocks = lax.all_gather(lower_blocks, "prow", axis=2, tiled=True)
    my_rows = lax.dynamic_slice_in_dim(row_blocks, col_index * sup_dev, sup_dev, 0)
    order = jnp.arange(ancestors, dtype=jnp.int32)
    slots = jnp.sum(
        jnp.where(my_rows[:, :, None] == order[None, None, :], slot_of[None, None, :], 0), axis=2
    )
    picks = (slots[:, :, None] == order[None, None, :]).astype(jnp.bfloat16)
    panel = jnp.einsum("kca,kcij->aikj", picks, full_blocks, preferred_element_type=jnp.float32)
    panel = panel.astype(jnp.bfloat16).reshape(ancestors * width, sup_dev * width)
    live = jnp.sum(picks.astype(jnp.float32), axis=1).T
    column_panel = lax.all_to_all(panel, "pcol", split_axis=0, concat_axis=1, tiled=True)
    partial_value = jnp.dot(sigma_anc, column_panel, preferred_element_type=jnp.float32)
    product = lax.psum_scatter(partial_value, "pcol", scatter_dimension=1, tiled=True)
    my_live = lax.dynamic_slice_in_dim(live, row_index * blocks_here, blocks_here, 0)
    shaped = product.reshape(blocks_here, width, sup_dev, width)
    offdiag = (-shaped * my_live[:, None, :, None]).astype(jnp.bfloat16)
    sigma_off = offdiag.reshape(rows_here, sup_dev * width)
    my_panel = lax.dynamic_slice_in_dim(panel, row_index * rows_here, rows_here, 0)
    quad = jnp.einsum(
        "rki,rkj->kij",
        my_panel.reshape(rows_here, sup_dev, width),
        sigma_off.reshape(rows_here, sup_dev, width),
        preferred_element_type=jnp.float32,
    )
    band = inv_diag.shape[1]
    total = lax.psum(quad.astype(jnp.bfloat16), "prow").astype(jnp.float32)
    mirrored = 0.5 * (total + jnp.swapaxes(total, 1, 2))
    mine = lax.dynamic_slice_in_dim(mirrored, row_index * band, band, 1)
    sigma_diag = inv_diag - mine
    return (sigma_off, sigma_diag)


def solution(mesh):
    in_specs = (P("prow", "pcol"), P("pcol", None, "prow", None), P(), P(), P("pcol", "prow", None))
    out_specs = (P("prow", "pcol"), P("pcol", "prow", None))
    return jax.shard_map(
        per_device, mesh=mesh, in_specs=in_specs, out_specs=out_specs, check_vma=False
    )
```

profile of v0, /device:TPU:0, one launch (start us, length us, event | category | flops | bytes accessed | tf_op | source)
XLA Modules:
  0.0 851.6 jit_solution(7170376953875848717)
XLA Ops:
  7.2 0.0 copy-start
  7.2 0.0 all-gather.2.cloned.1.call-start
  7.2 2.1 copy.29
  9.3 0.0 all-gather.2.cloned.1.call-update
  9.3 0.0 reduce-scatter.2.cloned.1.call-start
  9.4 0.8 constant_dynamic-slice_fusion.1
  10.2 0.1 copy.28
  10.2 0.9 select_reduce_fusion
  11.1 75.3 %all-gather.2.cloned.1.call-done = bf16[4,16,256,256]{3,1,2,0:T(8,128)(2,1)} async-done(((bf16[4,16,16,256]{3,1,2,0:T(8,128)(2,1)}), bf16[4,16,256,256]{3,1,2,0:T(8,128)(2,1)}) %all-gather.2.cloned.1.call-update) | async-done | bytes 8388624 | tf_op jit(solution)/shard_map/all_gather | solution.py:15
  86.4 10.3 %convert_bitcast_fusion = bf16[32,256,4,256]{3,0,1,2:T(8,128)(2,1)} fusion(bf16[4,16,256,256]{3,1,2,0:T(8,128)(2,1)} %all-gather.2.cloned.1.call-done, s32[4,16]{1,0:T(4,128)S(1)} %select_reduce_fusion), kind=kOutput, calls=%fused_computation | convolution fusion | flops 276826112 | bytes 25166080 | tf_op jit(solution)/shard_map/kca,kcij->aikj/dot_general | solution.py:22
  96.8 30.6 %copy.30 = bf16[32,256,4,256]{1,0,3,2:T(8,128)(2,1)} copy(bf16[32,256,4,256]{3,0,1,2:T(8,128)(2,1)} %convert_bitcast_fusion) | data formatting | bytes 33554432 | tf_op jit(solution)/shard_map/convert_element_type | solution.py:23
  127.4 26.7 %all_to_all.14 = bf16[8,1024,1024]{1,0,2:T(8,128)(2,1)} reshape(bf16[32,256,4,256]{1,0,3,2:T(8,128)(2,1)} %copy.30) | data formatting | bytes 33554432 | tf_op jit(solution)/shard_map/all_to_all | solution.py:25
  154.0 15.6 %copy.31 = bf16[8,1024,1024]{1,2,0:T(8,128)(2,1)S(1)} copy(bf16[8,1024,1024]{1,0,2:T(8,128)(2,1)} %all_to_all.14) | data formatting | bytes 33554432 | tf_op jit(solution)/shard_map/all_to_all | solution.py:25
  169.7 188.9 %all_to_all.19 = bf16[8,1024,1024]{1,2,0:T(8,128)(2,1)S(1)} all-to-all(bf16[8,1024,1024]{1,2,0:T(8,128)(2,1)S(1)} %copy.31), channel_id=1, replica_groups=mesh['prow'=16,'pcol'=8] {'pcol'}, dimensions={0} | all-to-all | bytes 33554432 | tf_op jit(solution)/shard_map/all_to_all | solution.py:25
  358.6 0.0 copy-done
  358.6 12.1 %convolution_bitcast_fusion = f32[512,8192]{0,1:T(8,128)} fusion(bf16[1024,8192]{0,1:T(8,128)(2,1)S(1)} %bitcast.42, bf16[512,1024]{1,0:T(8,128)(2,1)S(1)} %copy-done), kind=kOutput, calls=%fused_computation.1 | convolution fusion | flops 8589934592 | bytes 34603008 | tf_op jit(solution)/shard_map/dot_general | solution.py:26
  370.6 0.0 reduce-scatter.2.cloned.1.call-update
  370.6 0.2 all-reduce.2.cloned.1.call-start
  370.9 0.1 convert_reduce_fusion
  371.0 0.1 dynamic-slice_bitcast_fusion
  371.0 0.1 broadcast_bitcast_fusion
  371.1 0.6 mul.40
  371.7 0.2 copy.37
  371.9 15.8 %copy.38 = bf16[128,8,32,256]{3,1,2,0:T(8,128)(2,1)S(1)} copy(bf16[128,8,32,256]{3,2,1,0:T(8,128)(2,1)} %bitcast.40) | data formatting | bytes 33554432
  387.7 1.1 constant_dynamic-slice_fusion
  388.8 305.1 %reduce-scatter.2.cloned.1.call-done = f32[512,1024]{0,1:T(8,128)} async-done(((f32[512,8192]{0,1:T(8,128)}), f32[512,1024]{0,1:T(8,128)}) %reduce-scatter.2.cloned.1.call-update) | async-done | bytes 2097168 | tf_op jit(solution)/shard_map/reduce_scatter | solution.py:27
  693.9 0.0 copy-start.1
  693.9 3.9 fusion.7
  697.8 0.0 copy-start.2
  697.8 2.0 copy.33
  699.8 2.6 convolution_convert_fusion
  702.4 0.0 all-reduce.2.cloned.1.call-update
  702.4 2.3 copy.35
  704.6 137.4 %all-reduce.2.cloned.1.call-done = bf16[4,256,256]{2,1,0:T(8,128)(2,1)} async-done(((bf16[4,256,256]{2,1,0:T(8,128)(2,1)}), bf16[4,256,256]{2,1,0:T(8,128)(2,1)}) %all-reduce.2.cloned.1.call-update) | async-done | bytes 524304 | tf_op jit(solution)/shard_map/psum | solution.py:40
  842.0 1.2 copy.34
  843.3 1.1 convert_element_type.32
  844.4 0.0 copy-done.2
  844.4 0.7 fusion.2
  845.1 0.0 copy-done.1
  (1 shorter events, 0.0 us)
Async XLA Ops:
  7.2 351.4 %copy-start = (bf16[512,1024]{1,0:T(8,128)(2,1)S(1)}, bf16[512,1024]{1,0:T(8,128)(2,1)}, u32[]{:S(2)}) copy-start(bf16[512,1024]{1,0:T(8,128)(2,1)} %param.5) | copy-start | bytes 3145732
  7.2 79.2 %all-gather.2.cloned.1.call-start = ((), (), s32[]{:S(2)}) async-start(), calls=%async_computation.2 | async-start | bytes 8912896 | tf_op jit(solution)/shard_map/all_gather | solution.py:15
  9.3 684.6 %reduce-scatter.2.cloned.1.call-start = ((), (), s32[]{:S(2)}) async-start(), calls=%async_computation.3 | async-start | bytes 18874368 | tf_op jit(solution)/shard_map/reduce_scatter | solution.py:27
  370.6 471.4 %all-reduce.2.cloned.1.call-start = ((), (), s32[]{:S(2)}) async-start(), calls=%async_computation.4 | async-start | bytes 1048576 | tf_op jit(solution)/shard_map/psum | solution.py:40
  693.9 151.2 %copy-start.1 = (bf16[512,1024]{1,0:T(8,128)(2,1)S(1)}, bf16[512,1024]{1,0:T(8,128)(2,1)}, u32[]{:S(2)}) copy-start(bf16[512,1024]{1,0:T(8,128)(2,1)} %param.5) | copy-start | bytes 3145732
  697.8 146.6 %copy-start.2 = (f32[4,16,256]{2,1,0:T(8,128)S(1)}, f32[4,16,256]{2,1,0:T(8,128)}, u32[]{:S(2)}) copy-start(f32[4,16,256]{2,1,0:T(8,128)} %param.9) | copy-start | bytes 196612
Sparse Core Ops, SparseCore 0:
  11.1 75.3 all-gather.1
  370.8 323.1 reduce-scatter.1
  702.5 139.4 all-reduce.1
where the time goes:
time: 854 us; the launch traced here: 852 us
  waiting for transfers between devices  518 us (61%)
  blocking collectives  189 us (22%)
  local copies, waits for them, and re-layouts  99.2 us (12%)
  matrix products  25 us (3%)
  between operations  13.8 us (2%)
    reduce_scatter x1, waiting for transfers between devices, per_device(): lax.psum_scatter(partial_value, 'pcol', scatter_dimension=1, tiled=True)  305 us
    all_to_all x1, blocking collectives, per_device(): lax.all_to_all(panel, 'pcol', split_axis=0, concat_axis=1, tiled=True)  189 us
    psum x1, waiting for transfers between devices, per_device(): total = lax.psum(quad.astype(jnp.bfloat16), 'prow').astype(jnp.float32)  137 us
    all_gather x1, waiting for transfers between devices, per_device(): full_blocks = lax.all_gather(lower_blocks, 'prow', axis=2, tiled=True)  75.3 us
    all_to_all x2, local copies, waits for them, and re-layouts, per_device(): lax.all_to_all(panel, 'pcol', split_axis=0, concat_axis=1, tiled=True)  42.3 us
    convert_element_type x1, local copies, waits for them, and re-layouts, per_device(): panel.astype(jnp.bfloat16).reshape(ancestors * width, sup_dev * width)  30.6 us
    unnamed x12, local copies, waits for them, and re-layouts  20.4 us
  transfers between devices with their start and end apart: 3, of which 3 were waited for; matrix products, arithmetic and copies ran while one was open for 3% of the time, Pallas kernels for 0%

commit v1 on v0

v1 whole, which is shorter than its diff:
```python
import jax
import jax.numpy as jnp
from jax import lax
from jax.experimental import pallas as pl
from jax.experimental.pallas import tpu as pltpu
from jax.sharding import PartitionSpec as P

B = 256
NR = 16
SUP = 4
NA = 32
VMEM_LIMIT = 48 * 1024 * 1024


def row_perm(fn):
    pairs = []
    for y in range(4):
        for h in range(2):
            for co in range(2):
                ty, th, tc = fn(y, h, co)
                pairs.append((y * 4 + h * 2 + co, (ty % 4) * 4 + (th % 2) * 2 + tc % 2))
    return pairs


def col_perm(fn):
    pairs = []
    for z in range(4):
        for w in range(2):
            tz, tw = fn(z, w)
            pairs.append((z * 2 + w, (tz % 4) * 2 + tw % 2))
    return pairs


def move_y(x, step):
    return lax.ppermute(x, "prow", row_perm(lambda y, h, co: (y + step, h, co)))


def swap_h(x):
    return lax.ppermute(x, "prow", row_perm(lambda y, h, co: (y, h + 1, co)))


def swap_core(x):
    return lax.ppermute(x, "prow", row_perm(lambda y, h, co: (y, h, co + 1)))


def move_z(x, step):
    return lax.ppermute(x, "pcol", col_perm(lambda z, w: (z + step, w)))


def swap_w(x):
    return lax.ppermute(x, "pcol", col_perm(lambda z, w: (z, w + 1)))


def first_kernel(inv_ref, place_ref, s0, s1, s2, s3, s4, s5, a0, a1, a2, a3, b0, b1, b2, b3,
                 acc_out, l_out, sv, lv, acc, s_sem, l_sem, o_sem):
    loads = []
    for p, src in enumerate((s0, s1, s2, s3, s4, s5)):
        for j in range(4):
            n = p * 4 + j
            loads.append(pltpu.make_async_copy(src.at[:, pl.ds(j * B, B)], sv.at[n], s_sem.at[n]))
    n = 0
    for part in (a0, a1, a2, a3, b0, b1, b2, b3):
        for h in range(2):
            row = pl.multiple_of(place_ref[n], 16)
            loads.append(pltpu.make_async_copy(part.at[h], lv.at[:, :, pl.ds(row, 16), :], l_sem.at[n]))
            n += 1
    for load in loads:
        load.start()
    acc[...] = jnp.zeros_like(acc)
    for load in loads:
        load.wait()
    keep = pltpu.make_async_copy(lv, l_out, o_sem.at[0])
    keep.start()

    def step(pos, carry):
        for k in range(SUP):
            c = inv_ref[k, pos]

            @pl.when(c >= 0)
            def _():
                acc[k] += jnp.dot(sv[pos], lv[k, c], preferred_element_type=jnp.float32)
        return carry

    lax.fori_loop(0, 24, step, 0)
    done = pltpu.make_async_copy(acc, acc_out, o_sem.at[1])
    done.start()
    done.wait()
    keep.wait()


def last_kernel(inv_ref, own_ref, core_ref, up, down, acc_in, l_in, off_out, keep_out, send_out,
                sv, lv, acc, tq, s_sem, l_sem):
    loads = []
    for p in range(2):
        for j in range(4):
            n = p * 4 + j
            loads.append(pltpu.make_async_copy(up.at[p, :, pl.ds(j * B, B)], sv.at[n, pl.ds(0, B)], s_sem.at[2 * n]))
            loads.append(pltpu.make_async_copy(down.at[p, :, pl.ds(j * B, B)], sv.at[n, pl.ds(B, B)], s_sem.at[2 * n + 1]))
    loads.append(pltpu.make_async_copy(acc_in, acc, l_sem.at[0]))
    loads.append(pltpu.make_async_copy(l_in, lv, l_sem.at[1]))
    for load in loads:
        load.start()
    for load in loads:
        load.wait()

    def step(pos, carry):
        for k in range(SUP):
            c = inv_ref[k, pos + 24]

            @pl.when(c >= 0)
            def _():
                acc[k] += jnp.dot(sv[pos], lv[k, c], preferred_element_type=jnp.float32)
        return carry

    lax.fori_loop(0, 8, step, 0)
    core = core_ref[0]
    for k in range(SUP):
        tq[...] = jnp.zeros_like(tq)
        for t in range(2):
            c = own_ref[k, t]

            @pl.when(c >= 0)
            def _():
                off = (-acc[k, pl.ds(t * B, B)]).astype(jnp.bfloat16)
                off_out[pl.ds(t * B, B), pl.ds(k * B, B)] = off
                tq[...] += lax.dot_general(lv[k, c], off, (((0,), (0,)), ((), ())),
                                           preferred_element_type=jnp.float32)

            @pl.when(c < 0)
            def _():
                off_out[pl.ds(t * B, B), pl.ds(k * B, B)] = jnp.zeros((B, B), jnp.bfloat16)
        total = tq[...]
        tq[...] = 0.5 * (total + total.T)
        for g in range(8):
            mine = pl.multiple_of((g * 2 + core) * 16, 16)
            other = pl.multiple_of((g * 2 + 1 - core) * 16, 16)
            keep_out[k, g] = tq[pl.ds(mine, 16), :]
            send_out[k, g] = tq[pl.ds(other, 16), :].astype(jnp.bfloat16)


def per_device(sigma_anc, lower_blocks, row_blocks, slot_of, inv_diag):
    row = lax.axis_index("prow")
    col = lax.axis_index("pcol")
    y, h, core = row // 4, (row // 2) % 2, row % 2
    z, w = col // 2, col % 2

    s = sigma_anc
    s_zm = move_z(s, 1)
    s_zp = move_z(s, -1)
    s_w = swap_w(s)
    l_h = swap_h(lower_blocks)
    pair = jnp.stack([lower_blocks, l_h])
    p_ym = move_y(pair, 1)
    p_yp = move_y(pair, -1)
    p_y2 = move_y(pair, 2)
    s_wzm = move_z(s_w, 1)
    s_wzp = move_z(s_w, -1)
    mine = (pair, p_ym, p_yp, p_y2)
    theirs = tuple(swap_core(x) for x in mine)
    half = s.shape[0] // 2
    up = move_z(jnp.stack([s_zm[:half], s_wzm[:half]]), 1)
    down = move_z(jnp.stack([s_zp[half:], s_wzp[half:]]), -1)

    my_rows = lax.dynamic_slice_in_dim(row_blocks, col * SUP, SUP, 0)
    order = jnp.arange(NA, dtype=jnp.int32)
    slots = jnp.sum(jnp.where(my_rows[:, :, None] == order, slot_of, 0), axis=2)
    sc = slots // 4
    dz = (sc // 2 - z) % 4
    group = jnp.where(dz == 0, 0, jnp.where(dz == 3, 1, jnp.where(dz == 1, 2, 3)))
    pos = (group * 2 + (sc % 2 + w) % 2) * 4 + slots % 4
    number = jnp.arange(1, NR + 1, dtype=jnp.int32)[None, :, None]
    inv = jnp.sum(jnp.where(pos[:, :, None] == order, number, 0), axis=1) - 1
    ours = row * 2 + jnp.arange(2, dtype=jnp.int32)
    own = jnp.sum(jnp.where(slots[:, :, None] == ours, number, 0), axis=1) - 1
    ys = jnp.stack([y, (y + 3) % 4, (y + 1) % 4, (y + 2) % 4])
    hs = jnp.stack([h, 1 - h])
    cs = jnp.stack([core, 1 - core])
    place = ((ys[None, :, None] * 2 + hs[None, None, :]) * 2 + cs[:, None, None]).reshape(-1) * 16
    place = place.astype(jnp.int32)

    hbm = pl.BlockSpec(memory_space=pl.ANY)
    smem = pl.BlockSpec(memory_space=pltpu.SMEM)
    vmem = pl.BlockSpec(memory_space=pltpu.VMEM)
    acc, blocks = pl.pallas_call(
        first_kernel,
        out_shape=(
            jax.ShapeDtypeStruct((SUP, 2 * B, B), jnp.float32),
            jax.ShapeDtypeStruct((SUP, NR, B, B), jnp.bfloat16),
        ),
        in_specs=[smem] * 2 + [hbm] * 14,
        out_specs=(hbm, hbm),
        scratch_shapes=[
            pltpu.VMEM((24, 2 * B, B), jnp.bfloat16),
            pltpu.VMEM((SUP, NR, B, B), jnp.bfloat16),
            pltpu.VMEM((SUP, 2 * B, B), jnp.float32),
            pltpu.SemaphoreType.DMA((24,)),
            pltpu.SemaphoreType.DMA((16,)),
            pltpu.SemaphoreType.DMA((2,)),
        ],
        compiler_params=pltpu.CompilerParams(vmem_limit_bytes=VMEM_LIMIT),
    )(inv, place, s, s_w, s_zm, s_wzm, s_zp, s_wzp, *mine, *theirs)

    sigma_off, keep, send = pl.pallas_call(
        last_kernel,
        out_shape=(
            jax.ShapeDtypeStruct((2 * B, SUP * B), jnp.bfloat16),
            jax.ShapeDtypeStruct((SUP, 8, 16, B), jnp.float32),
            jax.ShapeDtypeStruct((SUP, 8, 16, B), jnp.bfloat16),
        ),
        in_specs=[smem] * 3 + [hbm] * 4,
        out_specs=(vmem, vmem, vmem),
        scratch_shapes=[
            pltpu.VMEM((8, 2 * B, B), jnp.bfloat16),
            pltpu.VMEM((SUP, NR, B, B), jnp.bfloat16),
            pltpu.VMEM((SUP, 2 * B, B), jnp.float32),
            pltpu.VMEM((B, B), jnp.float32),
            pltpu.SemaphoreType.DMA((16,)),
            pltpu.SemaphoreType.DMA((2,)),
        ],
        compiler_params=pltpu.CompilerParams(vmem_limit_bytes=VMEM_LIMIT),
    )(inv, own, core.reshape(1).astype(jnp.int32), up, down, acc, blocks)

    one = keep + swap_core(send).astype(jnp.float32)
    one = one.reshape(SUP, 4, 2, 16, B)
    kept = lax.dynamic_index_in_dim(one, h, 2, keepdims=False)
    sent = lax.dynamic_index_in_dim(one, 1 - h, 2, keepdims=False).astype(jnp.bfloat16)
    two = kept + swap_h(sent).astype(jnp.float32)
    total = lax.dynamic_index_in_dim(two, y, 1, keepdims=False)
    narrow = two.astype(jnp.bfloat16)
    for step in (1, -1, 2):
        part = lax.dynamic_index_in_dim(narrow, (y + step) % 4, 1, keepdims=False)
        total = total + move_y(part, step).astype(jnp.float32)
    return sigma_off, inv_diag - total


def solution(mesh):
    in_specs = (P("prow", "pcol"), P("pcol", None, "prow", None), P(), P(), P("pcol", "prow", None))
    out_specs = (P("prow", "pcol"), P("pcol", "prow", None))
    return jax.shard_map(
        per_device, mesh=mesh, in_specs=in_specs, out_specs=out_specs, check_vma=False
    )
```

time: 854 us -> 154 us (0.18)
  waiting for transfers between devices: 518 us -> 84.6 us
  blocking collectives: 189 us -> 0 us
  local copies, waits for them, and re-layouts: 99.2 us -> 5.61 us
  Pallas kernels: 0 us -> 30.1 us
  starting transfers between devices: 0.3 us -> 26.4 us
  matrix products: 25 us -> 0 us
  between operations: 13.8 us -> 0.82 us
    reduce_scatter x1 -> x0, waiting for transfers between devices: 305 us -> none  [per_device(): lax.psum_scatter(partial_value, 'pcol', scatter_dimension=1, tiled=True)]
    all_to_all x1 -> x0, blocking collectives: 189 us -> none  [per_device(): lax.all_to_all(panel, 'pcol', split_axis=0, concat_axis=1, tiled=True)]
    psum x1 -> x0, waiting for transfers between devices: 137 us -> none  [per_device(): total = lax.psum(quad.astype(jnp.bfloat16), 'prow').astype(jnp.float32)]
    ppermute x0 -> x20, waiting for transfers between devices: none -> 84.6 us  [the longest x6 44.4 us: move_y(): return lax.ppermute(x, 'prow', row_perm(lambda y, h, co: (y + step, h, co)))]
    all_gather x1 -> x0, waiting for transfers between devices: 75.3 us -> none  [per_device(): full_blocks = lax.all_gather(lower_blocks, 'prow', axis=2, tiled=True)]
    all_to_all x2 -> x0, local copies, waits for them, and re-layouts: 42.3 us -> none  [per_device(): lax.all_to_all(panel, 'pcol', split_axis=0, concat_axis=1, tiled=True)]
    convert_element_type x2 -> x1, local copies, waits for them, and re-layouts: 31.9 us -> 0.03 us  [per_device(): lax.dynamic_index_in_dim(one, 1 - h, 2, keepdims=False).astype(jnp.bfloat16)]
    pallas_call x0 -> x2, Pallas kernels: none -> 30.1 us  [the longest x1 18.4 us: per_device(): pl.pallas_call(first_kernel, out_shape=(jax.ShapeDtypeStruct((SUP, 2 * B,...]
  transfers between devices with their start and end apart: 3 -> 20, of which waited for: 3 -> 9; matrix products, arithmetic and copies ran while one was open for 3% -> 4% of each run, Pallas kernels for 0% -> 12%
where the time goes in v1:
time: 154 us; the launch traced here: 153 us
  waiting for transfers between devices  84.6 us (55%)
  Pallas kernels  30.1 us (20%)
  starting transfers between devices  26.4 us (17%)
  other arithmetic  5.92 us (4%)
  local copies, waits for them, and re-layouts  5.61 us (4%)
    ppermute x6, waiting for transfers between devices, move_y(): return lax.ppermute(x, 'prow', row_perm(lambda y, h, co: (y + step, h, co)))  44.4 us
    ppermute x2, waiting for transfers between devices, swap_h(): return lax.ppermute(x, 'prow', row_perm(lambda y, h, co: (y, h + 1, co)))  37.2 us
    pallas_call x1, Pallas kernels, per_device(): pl.pallas_call(first_kernel, out_shape=(jax.ShapeDtypeStruct((SUP, 2 * B,...  18.4 us
    ppermute x6, starting transfers between devices, move_z(): return lax.ppermute(x, 'pcol', col_perm(lambda z, w: (z + step, w)))  12.1 us
    pallas_call x1, Pallas kernels, per_device(): pl.pallas_call(last_kernel, out_shape=(jax.ShapeDtypeStruct((2 * B, SUP *...  11.7 us
    ppermute x6, starting transfers between devices, move_y(): return lax.ppermute(x, 'prow', row_perm(lambda y, h, co: (y + step, h, co)))  9.02 us
    unnamed x14, local copies, waits for them, and re-layouts  4.06 us
  transfers between devices with their start and end apart: 20, of which 9 were waited for; matrix products, arithmetic and copies ran while one was open for 4% of the time, Pallas kernels for 12%

profile of v1, /device:TPU:0, one launch (start us, length us, event | category | flops | bytes accessed | tf_op | source)
XLA Modules:
  0.0 153.4 jit_solution(8857697751949223620)
XLA Ops:
  0.6 0.0 copy-start
  0.7 1.7 %collective-permute-start.1 = (bf16[512,1024]{1,0:T(8,128)(2,1)}, bf16[512,1024]{1,0:T(8,128)(2,1)S(1)}, u32[]{:S(2)}, u32[]{:S(2)}) collective-permute-start(bf16[512,1024]{1,0:T(8,128)(2,1)} %s0.1), channel_id=1, source_target_pairs={{0,1},{1,0},{2,3},{3,2},{4,5},{5,4},{6,7},{7,6},{8,9},{9,8},{10,11... | collective-permute-start | bytes 3145736 | tf_op jit(solution)/shard_map/ppermute | solution.py:51
  2.3 1.9 %collective-permute-start = (bf16[512,1024]{1,0:T(8,128)(2,1)}, bf16[512,1024]{1,0:T(8,128)(2,1)S(1)}, u32[]{:S(2)}, u32[]{:S(2)}) collective-permute-start(bf16[512,1024]{1,0:T(8,128)(2,1)} %s0.1), channel_id=1, source_target_pairs={{0,2},{1,3},{2,4},{3,5},{4,6},{5,7},{6,0},{7,1},{8,10},{9,11},{10,... | collective-permute-start | bytes 3145736 | tf_op jit(solution)/shard_map/ppermute | solution.py:47
  4.2 2.7 %collective-permute-start.7 = (bf16[4,16,16,256]{3,2,1,0:T(8,128)(2,1)}, bf16[4,16,16,256]{3,2,1,0:T(8,128)(2,1)S(1)}, u32[]{:S(2)}, u32[]{:S(2)}) collective-permute-start(bf16[4,16,16,256]{3,2,1,0:T(8,128)(2,1)} %param.6), channel_id=1, source_target_pairs={{0,16},{8,24},{16,0},{24,8},{32,48},{40,56},{48,32},{56,40},{64,80... | collective-permute-start | bytes 1572872 | tf_op jit(solution)/shard_map/ppermute | solution.py:39
  7.0 2.1 %collective-permute-start.4 = (bf16[512,1024]{1,0:T(8,128)(2,1)}, bf16[512,1024]{1,0:T(8,128)(2,1)S(1)}, u32[]{:S(2)}, u32[]{:S(2)}) collective-permute-start(bf16[512,1024]{1,0:T(8,128)(2,1)} %s0.1), channel_id=1, source_target_pairs={{0,6},{1,7},{2,0},{3,1},{4,2},{5,3},{6,4},{7,5},{8,14},{9,15},{10,... | collective-permute-start | bytes 3145736 | tf_op jit(solution)/shard_map/ppermute | solution.py:47
  9.1 30.3 %collective-permute-done.7 = bf16[4,16,16,256]{3,2,1,0:T(8,128)(2,1)S(1)} collective-permute-done((bf16[4,16,16,256]{3,2,1,0:T(8,128)(2,1)}, bf16[4,16,16,256]{3,2,1,0:T(8,128)(2,1)S(1)}, u32[]{:S(2)}, u32[]{:S(2)}) %collective-permute-start.7) | collective-permute-done | bytes 524320 | tf_op jit(solution)/shard_map/ppermute | solution.py:39
  39.4 2.1 %pad_maximum_fusion.2.a0 = bf16[2,4,16,16,256]{4,3,2,1,0:T(8,128)(2,1)} fusion(bf16[1,4,16,16,256]{4,3,2,1,0:T(8,128)(2,1)S(1)} %bitcast.41, bf16[1,4,16,16,256]{4,3,2,1,0:T(8,128)(2,1)} %bitcast.40), kind=kLoop, calls=%fused_computation.2 | loop fusion | flops 524288 | bytes 2097152 | tf_op jit(solution)/shard_map/stack | solution.py:152
  41.5 1.6 %collective-permute-start.8 = (bf16[2,4,16,16,256]{4,3,2,1,0:T(8,128)(2,1)}, bf16[2,4,16,16,256]{4,3,2,1,0:T(8,128)(2,1)}, u32[]{:S(2)}, u32[]{:S(2)}) collective-permute-start(bf16[2,4,16,16,256]{4,3,2,1,0:T(8,128)(2,1)} %pad_maximum_fusion.2.a0), channel_id=1, source_target_pairs={{0,32},{8,40},{16,48},{24,56},{32,64},{40,72},{48,80},{56,88},{64,... | collective-permute-start | bytes 3145736 | tf_op jit(solution)/shard_map/ppermute | solution.py:35
  43.1 0.1 add_multiply_fusion.2
  43.1 0.1 pad_add_fusion
  43.2 1.7 %collective-permute-start.9 = (bf16[2,4,16,16,256]{4,3,2,1,0:T(8,128)(2,1)}, bf16[2,4,16,16,256]{4,3,2,1,0:T(8,128)(2,1)}, u32[]{:S(2)}, u32[]{:S(2)}) collective-permute-start(bf16[2,4,16,16,256]{4,3,2,1,0:T(8,128)(2,1)} %pad_maximum_fusion.2.a0), channel_id=1, source_target_pairs={{0,96},{8,104},{16,112},{24,120},{32,0},{40,8},{48,16},{56,24},{64... | collective-permute-start | bytes 3145736 | tf_op jit(solution)/shard_map/ppermute | solution.py:35
  44.9 0.0 collective-permute-done.1.s1
  44.9 2.0 %collective-permute-start.10 = (bf16[2,4,16,16,256]{4,3,2,1,0:T(8,128)(2,1)}, bf16[2,4,16,16,256]{4,3,2,1,0:T(8,128)(2,1)}, u32[]{:S(2)}, u32[]{:S(2)}) collective-permute-start(bf16[2,4,16,16,256]{4,3,2,1,0:T(8,128)(2,1)} %pad_maximum_fusion.2.a0), channel_id=1, source_target_pairs={{0,64},{8,72},{16,80},{24,88},{32,96},{40,104},{48,112},{56,120},{... | collective-permute-start | bytes 3145736 | tf_op jit(solution)/shard_map/ppermute | solution.py:35
  46.9 0.0 collective-permute-done.s2
  46.9 1.9 %collective-permute-start.2 = (bf16[512,1024]{1,0:T(8,128)(2,1)}, bf16[512,1024]{1,0:T(8,128)(2,1)S(1)}, u32[]{:S(2)}, u32[]{:S(2)}) collective-permute-start(bf16[512,1024]{1,0:T(8,128)(2,1)} %copy-done.3), channel_id=1, source_target_pairs={{0,2},{1,3},{2,4},{3,5},{4,6},{5,7},{6,0},{7,1},{8,10},{9,11},{10,... | collective-permute-start | bytes 3145736 | tf_op jit(solution)/shard_map/ppermute | solution.py:47
  48.8 0.1 add_multiply_fusion.1
  48.9 0.1 add_multiply_fusion
  48.9 0.0 collective-permute-done.4.s4
  48.9 2.1 %collective-permute-start.5 = (bf16[512,1024]{1,0:T(8,128)(2,1)}, bf16[512,1024]{1,0:T(8,128)(2,1)}, u32[]{:S(2)}, u32[]{:S(2)}) collective-permute-start(bf16[512,1024]{1,0:T(8,128)(2,1)} %copy-done.3), channel_id=1, source_target_pairs={{0,6},{1,7},{2,0},{3,1},{4,2},{5,3},{6,4},{7,5},{8,14},{9,15},{10,... | collective-permute-start | bytes 3145736 | tf_op jit(solution)/shard_map/ppermute | solution.py:47
  51.1 0.1 constant_dynamic-slice_fusion
  51.1 16.8 %collective-permute-done.8.a1 = bf16[2,4,16,16,256]{4,3,2,1,0:T(8,128)(2,1)} collective-permute-done((bf16[2,4,16,16,256]{4,3,2,1,0:T(8,128)(2,1)}, bf16[2,4,16,16,256]{4,3,2,1,0:T(8,128)(2,1)}, u32[]{:S(2)}, u32[]{:S(2)}) %collective-permute-start.8) | collective-permute-done | bytes 1048608 | tf_op jit(solution)/shard_map/ppermute | solution.py:35
  68.0 0.0 collective-permute-start.11
  68.1 1.6 %collective-permute-done.9.a2 = bf16[2,4,16,16,256]{4,3,2,1,0:T(8,128)(2,1)} collective-permute-done((bf16[2,4,16,16,256]{4,3,2,1,0:T(8,128)(2,1)}, bf16[2,4,16,16,256]{4,3,2,1,0:T(8,128)(2,1)}, u32[]{:S(2)}, u32[]{:S(2)}) %collective-permute-start.9) | collective-permute-done | bytes 1048608 | tf_op jit(solution)/shard_map/ppermute | solution.py:35
  69.6 0.0 collective-permute-start.12
  69.6 21.1 %collective-permute-done.10.a3 = bf16[2,4,16,16,256]{4,3,2,1,0:T(8,128)(2,1)} collective-permute-done((bf16[2,4,16,16,256]{4,3,2,1,0:T(8,128)(2,1)}, bf16[2,4,16,16,256]{4,3,2,1,0:T(8,128)(2,1)}, u32[]{:S(2)}, u32[]{:S(2)}) %collective-permute-start.10) | collective-permute-done | bytes 1048608 | tf_op jit(solution)/shard_map/ppermute | solution.py:35
  90.7 0.0 collective-permute-start.13
  90.7 0.0 collective-permute-done.2.s3
  90.7 0.5 collective-permute-start.14
  91.3 1.1 pad_maximum_fusion
  92.4 0.0 collective-permute-done.5.s5
  92.4 1.9 %collective-permute-start.3 = (bf16[2,256,1024]{2,1,0:T(8,128)(2,1)}, bf16[2,256,1024]{2,1,0:T(8,128)(2,1)}, u32[]{:S(2)}, u32[]{:S(2)}) collective-permute-start(bf16[2,256,1024]{2,1,0:T(8,128)(2,1)} %pad_maximum_fusion), channel_id=1, source_target_pairs={{0,2},{1,3},{2,4},{3,5},{4,6},{5,7},{6,0},{7,1},{8,10},{9,11},{10,... | collective-permute-start | bytes 3145736 | tf_op jit(solution)/shard_map/ppermute | solution.py:47
  94.3 1.1 slice_bitcast_fusion
  95.4 1.1 pad_maximum_fusion.1
  96.4 0.0 collective-permute-done.11.b0
  96.5 2.1 %collective-permute-start.6 = (bf16[2,256,1024]{2,1,0:T(8,128)(2,1)}, bf16[2,256,1024]{2,1,0:T(8,128)(2,1)}, u32[]{:S(2)}, u32[]{:S(2)}) collective-permute-start(bf16[2,256,1024]{2,1,0:T(8,128)(2,1)} %pad_maximum_fusion.1), channel_id=1, source_target_pairs={{0,6},{1,7},{2,0},{3,1},{4,2},{5,3},{6,4},{7,5},{8,14},{9,15},{10,... | collective-permute-start | bytes 3145736 | tf_op jit(solution)/shard_map/ppermute | solution.py:47
  98.6 0.1 mul.50.place_ref
  98.7 0.1 copy.9
  98.7 0.2 select_reduce_fusion.1
  99.0 0.2 select_reduce_fusion.2
  99.2 0.1 copy.10
  99.3 0.1 select_reduce_fusion
  99.4 0.0 collective-permute-done.12.b1
  99.4 0.0 collective-permute-done.13.b2
  99.5 0.0 collective-permute-done.14.b3
  99.5 0.0 copy-start.2
  99.5 1.2 copy-done.2
  100.7 1.2 copy-done.4
  101.9 18.4 %shard_map.68 = (f32[4,512,256]{2,1,0:T(8,128)}, bf16[4,16,256,256]{3,2,1,0:T(8,128)(2,1)}) custom-call(s32[4,32]{1,0:T(4,128)S(1)} %broadcast_add_fusion.1.inv_ref, s32[16]{0:T(128)S(1)} %mul.50.place_ref, bf16[512,1024]{1,0:T(8,128)(2,1)S(1)} %copy-done.2, bf16[512,1024]{1,0:T(8,128)(2,1)S(1)} %copy-done.4, bf16[512,1024]{1,0:T(8,128)(2,1)S(1)} %collective-permute-done.s2, ...), custom_call_target="tpu_custom_call" | custom-call | tf_op jit(solution)/shard_map/pallas_call | solution.py:184
  120.3 0.0 collective-permute-done.3.up
  120.3 1.4 collective-permute-done.6.down
  121.7 1.6 %copy-done.1 = f32[4,512,256]{2,1,0:T(8,128)S(1)} copy-done((f32[4,512,256]{2,1,0:T(8,128)S(1)}, f32[4,512,256]{2,1,0:T(8,128)}, u32[]{:S(2)}) %copy-start.1) | copy-done | bytes 2097176
  123.3 11.7 %shard_map.69 = (bf16[512,1024]{1,0:T(8,128)(2,1)}, f32[4,8,16,256]{3,2,1,0:T(8,128)S(1)}, bf16[4,8,16,256]{3,2,1,0:T(8,128)(2,1)S(1)}) custom-call(s32[4,32]{1,0:T(4,128)S(1)} %broadcast_add_fusion.1.inv_ref, s32[4,2]{1,0:T(4,128)S(1)} %broadcast_add_fusion.own_ref, s32[1]{0:T(128)} %bitcast.core_ref, bf16[2,256,1024]{2,1,0:T(8,128)(2,1)} %collective-permute-done.3.up, ...), custom_call_target="tpu_custom_call" | custom-call | tf_op jit(solution)/shard_map/pallas_call | solution.py:203
  135.0 0.1 collective-permute-start.15
  135.2 1.5 collective-permute-done.15
  136.7 0.1 convert_add_fusion
  136.8 0.2 collective-permute-start.16
  137.0 6.9 %collective-permute-done.16 = bf16[4,4,16,256]{3,2,1,0:T(8,128)(2,1)S(1)} collective-permute-done((bf16[4,4,16,256]{3,2,1,0:T(8,128)(2,1)S(1)}, bf16[4,4,16,256]{3,2,1,0:T(8,128)(2,1)S(1)}, u32[]{:S(2)}, u32[]{:S(2)}) %collective-permute-start.16) | collective-permute-done | bytes 131104 | tf_op jit(solution)/shard_map/ppermute | solution.py:39
  144.0 0.3 collective-permute-start.17
  144.3 3.0 %collective-permute-start.18 = (bf16[4,16,256]{2,1,0:T(8,128)(2,1)S(1)}, bf16[4,16,256]{2,1,0:T(8,128)(2,1)S(1)}, u32[]{:S(2)}, u32[]{:S(2)}) collective-permute-start(bf16[4,16,256]{2,1,0:T(8,128)(2,1)S(1)} %get-tuple-element.16), channel_id=1, source_target_pairs={{0,96},{8,104},{16,112},{24,120},{32,0},{40,8},{48,16},{56,24},{64... | collective-permute-start | bytes 98312 | tf_op jit(solution)/shard_map/ppermute | solution.py:35
  147.3 0.5 collective-permute-start.19
  147.8 1.4 collective-permute-done.17
  149.2 0.0 collective-permute-done.18
  149.2 3.5 %collective-permute-done.19 = bf16[4,16,256]{2,1,0:T(8,128)(2,1)S(1)} collective-permute-done((bf16[4,16,256]{2,1,0:T(8,128)(2,1)S(1)}, bf16[4,16,256]{2,1,0:T(8,128)(2,1)S(1)}, u32[]{:S(2)}, u32[]{:S(2)}) %collective-permute-start.19) | collective-permute-done | bytes 32800 | tf_op jit(solution)/shard_map/ppermute | solution.py:35
  152.7 0.7 fusion.3
  (20 shorter events, 0.3 us)
Async XLA Ops:
  0.6 50.4 %copy-start = (s32[32,16]{0,1:T(8,128)S(1)}, s32[32,16]{0,1:T(8,128)}, u32[]{:S(2)}) copy-start(s32[32,16]{0,1:T(8,128)} %param.7) | copy-start | bytes 6148
  0.6 98.1 %copy-start.6 = (s32[32]{0:T(128)S(1)}, s32[32]{0:T(128)}, u32[]{:S(2)}) copy-start(s32[32]{0:T(128)} %param.8) | copy-start | bytes 388
  0.7 44.2 %collective-permute-start.1 = (bf16[512,1024]{1,0:T(8,128)(2,1)}, bf16[512,1024]{1,0:T(8,128)(2,1)S(1)}, u32[]{:S(2)}, u32[]{:S(2)}) collective-permute-start(bf16[512,1024]{1,0:T(8,128)(2,1)} %s0.1), channel_id=1, source_target_pairs={{0,1},{1,0},{2,3},{3,2},{4,5},{5,4},{6,7},{7,6},{8,9},{9,8},{10,11... | collective-permute-start | bytes 3145736 | tf_op jit(solution)/shard_map/ppermute | solution.py:51
  2.3 44.6 %collective-permute-start = (bf16[512,1024]{1,0:T(8,128)(2,1)}, bf16[512,1024]{1,0:T(8,128)(2,1)S(1)}, u32[]{:S(2)}, u32[]{:S(2)}) collective-permute-start(bf16[512,1024]{1,0:T(8,128)(2,1)} %s0.1), channel_id=1, source_target_pairs={{0,2},{1,3},{2,4},{3,5},{4,6},{5,7},{6,0},{7,1},{8,10},{9,11},{10,... | collective-permute-start | bytes 3145736 | tf_op jit(solution)/shard_map/ppermute | solution.py:47
  4.2 35.1 %collective-permute-start.7 = (bf16[4,16,16,256]{3,2,1,0:T(8,128)(2,1)}, bf16[4,16,16,256]{3,2,1,0:T(8,128)(2,1)S(1)}, u32[]{:S(2)}, u32[]{:S(2)}) collective-permute-start(bf16[4,16,16,256]{3,2,1,0:T(8,128)(2,1)} %param.6), channel_id=1, source_target_pairs={{0,16},{8,24},{16,0},{24,8},{32,48},{40,56},{48,32},{56,40},{64,80... | collective-permute-start | bytes 1572872 | tf_op jit(solution)/shard_map/ppermute | solution.py:39
  7.0 42.0 %collective-permute-start.4 = (bf16[512,1024]{1,0:T(8,128)(2,1)}, bf16[512,1024]{1,0:T(8,128)(2,1)S(1)}, u32[]{:S(2)}, u32[]{:S(2)}) collective-permute-start(bf16[512,1024]{1,0:T(8,128)(2,1)} %s0.1), channel_id=1, source_target_pairs={{0,6},{1,7},{2,0},{3,1},{4,2},{5,3},{6,4},{7,5},{8,14},{9,15},{10,... | collective-permute-start | bytes 3145736 | tf_op jit(solution)/shard_map/ppermute | solution.py:47
  41.5 26.5 %collective-permute-start.8 = (bf16[2,4,16,16,256]{4,3,2,1,0:T(8,128)(2,1)}, bf16[2,4,16,16,256]{4,3,2,1,0:T(8,128)(2,1)}, u32[]{:S(2)}, u32[]{:S(2)}) collective-permute-start(bf16[2,4,16,16,256]{4,3,2,1,0:T(8,128)(2,1)} %pad_maximum_fusion.2.a0), channel_id=1, source_target_pairs={{0,32},{8,40},{16,48},{24,56},{32,64},{40,72},{48,80},{56,88},{64,... | collective-permute-start | bytes 3145736 | tf_op jit(solution)/shard_map/ppermute | solution.py:35
  43.2 26.4 %collective-permute-start.9 = (bf16[2,4,16,16,256]{4,3,2,1,0:T(8,128)(2,1)}, bf16[2,4,16,16,256]{4,3,2,1,0:T(8,128)(2,1)}, u32[]{:S(2)}, u32[]{:S(2)}) collective-permute-start(bf16[2,4,16,16,256]{4,3,2,1,0:T(8,128)(2,1)} %pad_maximum_fusion.2.a0), channel_id=1, source_target_pairs={{0,96},{8,104},{16,112},{24,120},{32,0},{40,8},{48,16},{56,24},{64... | collective-permute-start | bytes 3145736 | tf_op jit(solution)/shard_map/ppermute | solution.py:35
  44.9 2.0 %copy-start.3 = (bf16[512,1024]{1,0:T(8,128)(2,1)}, bf16[512,1024]{1,0:T(8,128)(2,1)S(1)}, u32[]{:S(2)}) copy-start(bf16[512,1024]{1,0:T(8,128)(2,1)S(1)} %collective-permute-done.1.s1) | copy-start | bytes 3145732
  44.9 45.9 %collective-permute-start.10 = (bf16[2,4,16,16,256]{4,3,2,1,0:T(8,128)(2,1)}, bf16[2,4,16,16,256]{4,3,2,1,0:T(8,128)(2,1)}, u32[]{:S(2)}, u32[]{:S(2)}) collective-permute-start(bf16[2,4,16,16,256]{4,3,2,1,0:T(8,128)(2,1)} %pad_maximum_fusion.2.a0), channel_id=1, source_target_pairs={{0,64},{8,72},{16,80},{24,88},{32,96},{40,104},{48,112},{56,120},{... | collective-permute-start | bytes 3145736 | tf_op jit(solution)/shard_map/ppermute | solution.py:35
  46.9 43.9 %collective-permute-start.2 = (bf16[512,1024]{1,0:T(8,128)(2,1)}, bf16[512,1024]{1,0:T(8,128)(2,1)S(1)}, u32[]{:S(2)}, u32[]{:S(2)}) collective-permute-start(bf16[512,1024]{1,0:T(8,128)(2,1)} %copy-done.3), channel_id=1, source_target_pairs={{0,2},{1,3},{2,4},{3,5},{4,6},{5,7},{6,0},{7,1},{8,10},{9,11},{10,... | collective-permute-start | bytes 3145736 | tf_op jit(solution)/shard_map/ppermute | solution.py:47
  48.9 43.4 %collective-permute-start.5 = (bf16[512,1024]{1,0:T(8,128)(2,1)}, bf16[512,1024]{1,0:T(8,128)(2,1)}, u32[]{:S(2)}, u32[]{:S(2)}) collective-permute-start(bf16[512,1024]{1,0:T(8,128)(2,1)} %copy-done.3), channel_id=1, source_target_pairs={{0,6},{1,7},{2,0},{3,1},{4,2},{5,3},{6,4},{7,5},{8,14},{9,15},{10,... | collective-permute-start | bytes 3145736 | tf_op jit(solution)/shard_map/ppermute | solution.py:47
  68.0 28.5 %collective-permute-start.11 = (bf16[2,4,16,16,256]{4,3,2,1,0:T(8,128)(2,1)}, bf16[2,4,16,16,256]{4,3,2,1,0:T(8,128)(2,1)}, u32[]{:S(2)}, u32[]{:S(2)}) collective-permute-start(bf16[2,4,16,16,256]{4,3,2,1,0:T(8,128)(2,1)} %pad_maximum_fusion.2.a0), channel_id=1, source_target_pairs={{0,8},{8,0},{16,24},{24,16},{32,40},{40,32},{48,56},{56,48},{64,72... | collective-permute-start | bytes 3145736 | tf_op jit(solution)/shard_map/ppermute | solution.py:43
  69.6 29.8 %collective-permute-start.12 = (bf16[2,4,16,16,256]{4,3,2,1,0:T(8,128)(2,1)}, bf16[2,4,16,16,256]{4,3,2,1,0:T(8,128)(2,1)}, u32[]{:S(2)}, u32[]{:S(2)}) collective-permute-start(bf16[2,4,16,16,256]{4,3,2,1,0:T(8,128)(2,1)} %collective-permute-done.8.a1), channel_id=1, source_target_pairs={{0,8},{8,0},{16,24},{24,16},{32,40},{40,32},{48,56},{56,48},{64,72... | collective-permute-start | bytes 3145736 | tf_op jit(solution)/shard_map/ppermute | solution.py:43
  90.7 8.7 %collective-permute-start.13 = (bf16[2,4,16,16,256]{4,3,2,1,0:T(8,128)(2,1)}, bf16[2,4,16,16,256]{4,3,2,1,0:T(8,128)(2,1)}, u32[]{:S(2)}, u32[]{:S(2)}) collective-permute-start(bf16[2,4,16,16,256]{4,3,2,1,0:T(8,128)(2,1)} %collective-permute-done.9.a2), channel_id=1, source_target_pairs={{0,8},{8,0},{16,24},{24,16},{32,40},{40,32},{48,56},{56,48},{64,72... | collective-permute-start | bytes 3145736 | tf_op jit(solution)/shard_map/ppermute | solution.py:43
  90.7 8.7 %collective-permute-start.14 = (bf16[2,4,16,16,256]{4,3,2,1,0:T(8,128)(2,1)}, bf16[2,4,16,16,256]{4,3,2,1,0:T(8,128)(2,1)}, u32[]{:S(2)}, u32[]{:S(2)}) collective-permute-start(bf16[2,4,16,16,256]{4,3,2,1,0:T(8,128)(2,1)} %collective-permute-done.10.a3), channel_id=1, source_target_pairs={{0,8},{8,0},{16,24},{24,16},{32,40},{40,32},{48,56},{56,48},{64,72... | collective-permute-start | bytes 3145736 | tf_op jit(solution)/shard_map/ppermute | solution.py:43
  92.4 27.9 %collective-permute-start.3 = (bf16[2,256,1024]{2,1,0:T(8,128)(2,1)}, bf16[2,256,1024]{2,1,0:T(8,128)(2,1)}, u32[]{:S(2)}, u32[]{:S(2)}) collective-permute-start(bf16[2,256,1024]{2,1,0:T(8,128)(2,1)} %pad_maximum_fusion), channel_id=1, source_target_pairs={{0,2},{1,3},{2,4},{3,5},{4,6},{5,7},{6,0},{7,1},{8,10},{9,11},{10,... | collective-permute-start | bytes 3145736 | tf_op jit(solution)/shard_map/ppermute | solution.py:47
  96.5 25.3 %collective-permute-start.6 = (bf16[2,256,1024]{2,1,0:T(8,128)(2,1)}, bf16[2,256,1024]{2,1,0:T(8,128)(2,1)}, u32[]{:S(2)}, u32[]{:S(2)}) collective-permute-start(bf16[2,256,1024]{2,1,0:T(8,128)(2,1)} %pad_maximum_fusion.1), channel_id=1, source_target_pairs={{0,6},{1,7},{2,0},{3,1},{4,2},{5,3},{6,4},{7,5},{8,14},{9,15},{10,... | collective-permute-start | bytes 3145736 | tf_op jit(solution)/shard_map/ppermute | solution.py:47
  99.5 1.2 copy-start.2
  100.7 1.2 copy-start.4
  101.9 50.8 %copy-start.5 = (f32[4,16,256]{2,1,0:T(8,128)S(1)}, f32[4,16,256]{2,1,0:T(8,128)}, u32[]{:S(2)}) copy-start(f32[4,16,256]{2,1,0:T(8,128)} %param.9) | copy-start | bytes 196612
  121.7 1.6 %copy-start.1 = (f32[4,512,256]{2,1,0:T(8,128)S(1)}, f32[4,512,256]{2,1,0:T(8,128)}, u32[]{:S(2)}) copy-start(f32[4,512,256]{2,1,0:T(8,128)} %get-tuple-element.7.acc_in) | copy-start | bytes 6291460
  135.0 1.6 %collective-permute-start.15 = (bf16[4,8,16,256]{3,2,1,0:T(8,128)(2,1)S(1)}, bf16[4,8,16,256]{3,2,1,0:T(8,128)(2,1)S(1)}, u32[]{:S(2)}, u32[]{:S(2)}) collective-permute-start(bf16[4,8,16,256]{3,2,1,0:T(8,128)(2,1)S(1)} %get-tuple-element.11), channel_id=1, source_target_pairs={{0,8},{8,0},{16,24},{24,16},{32,40},{40,32},{48,56},{56,48},{64,72... | collective-permute-start | bytes 786440 | tf_op jit(solution)/shard_map/ppermute | solution.py:43
  136.8 7.1 %collective-permute-start.16 = (bf16[4,4,16,256]{3,2,1,0:T(8,128)(2,1)S(1)}, bf16[4,4,16,256]{3,2,1,0:T(8,128)(2,1)S(1)}, u32[]{:S(2)}, u32[]{:S(2)}) collective-permute-start(bf16[4,4,16,256]{3,2,1,0:T(8,128)(2,1)S(1)} %fusion), channel_id=1, source_target_pairs={{0,16},{8,24},{16,0},{24,8},{32,48},{40,56},{48,32},{56,40},{64,80... | collective-permute-start | bytes 393224 | tf_op jit(solution)/shard_map/ppermute | solution.py:39
  144.0 5.2 %collective-permute-start.17 = (bf16[4,16,256]{2,1,0:T(8,128)(2,1)S(1)}, bf16[4,16,256]{2,1,0:T(8,128)(2,1)S(1)}, u32[]{:S(2)}, u32[]{:S(2)}) collective-permute-start(bf16[4,16,256]{2,1,0:T(8,128)(2,1)S(1)} %get-tuple-element.14), channel_id=1, source_target_pairs={{0,32},{8,40},{16,48},{24,56},{32,64},{40,72},{48,80},{56,88},{64,... | collective-permute-start | bytes 98312 | tf_op jit(solution)/shard_map/ppermute | solution.py:35
  144.3 4.9 %collective-permute-start.18 = (bf16[4,16,256]{2,1,0:T(8,128)(2,1)S(1)}, bf16[4,16,256]{2,1,0:T(8,128)(2,1)S(1)}, u32[]{:S(2)}, u32[]{:S(2)}) collective-permute-start(bf16[4,16,256]{2,1,0:T(8,128)(2,1)S(1)} %get-tuple-element.16), channel_id=1, source_target_pairs={{0,96},{8,104},{16,112},{24,120},{32,0},{40,8},{48,16},{56,24},{64... | collective-permute-start | bytes 98312 | tf_op jit(solution)/shard_map/ppermute | solution.py:35
  147.3 5.4 %collective-permute-start.19 = (bf16[4,16,256]{2,1,0:T(8,128)(2,1)S(1)}, bf16[4,16,256]{2,1,0:T(8,128)(2,1)S(1)}, u32[]{:S(2)}, u32[]{:S(2)}) collective-permute-start(bf16[4,16,256]{2,1,0:T(8,128)(2,1)S(1)} %get-tuple-element.15), channel_id=1, source_target_pairs={{0,64},{8,72},{16,80},{24,88},{32,96},{40,104},{48,112},{56,120},{... | collective-permute-start | bytes 98312 | tf_op jit(solution)/shard_map/ppermute | solution.py:35

commit v2 on v0

v2 whole, which is shorter than its diff:
```python
import jax
import jax.numpy as jnp
from jax import lax
from jax.experimental import pallas as pl
from jax.experimental.pallas import tpu as pltpu
from jax.sharding import PartitionSpec as P

B = 256
NR = 16
SUP = 4
NA = 32
ROWS = 2 * B
VMEM_LIMIT = 4 * 1024 * 1024
FINAL_LIMIT = 16 * 1024 * 1024
AXES = ("prow", "pcol")


def permute(x, fn):
    pairs = []
    for y in range(4):
        for h in range(2):
            for co in range(2):
                for z in range(4):
                    for w in range(2):
                        ty, th, tc, tz, tw = fn(y, h, co, z, w)
                        target = ((ty % 4) * 4 + (th % 2) * 2 + tc % 2) * 8 + (tz % 4) * 2 + tw % 2
                        pairs.append(((y * 4 + h * 2 + co) * 8 + z * 2 + w, target))
    return lax.ppermute(x, AXES, pairs)


def z_first(x):
    return permute(x, lambda y, h, co, z, w: (y, h, co, z + 1 - 2 * co, w))


def z_second(x):
    return permute(x, lambda y, h, co, z, w: (y, h, co, z - 1 + 2 * co, w))


def y_first(x):
    return permute(x, lambda y, h, co, z, w: (y + 1 - 2 * co, h, co, z, w))


def y_second(x):
    return permute(x, lambda y, h, co, z, w: (y - 1 + 2 * co, h, co, z, w))


def move_y(x, step):
    return permute(x, lambda y, h, co, z, w: (y + step, h, co, z, w))


def swap_h(x):
    return permute(x, lambda y, h, co, z, w: (y, h + 1, co, z, w))


def swap_core(x):
    return permute(x, lambda y, h, co, z, w: (y, h, co + 1, z, w))


def swap_w(x):
    return permute(x, lambda y, h, co, z, w: (y, h, co, z, w + 1))


def tie(*arrays):
    return lax.optimization_barrier(arrays)


def in_hbm(*arrays):
    return [pltpu.with_memory_space_constraint(v, pltpu.HBM) for v in arrays]


def start_wait(copies):
    for copy in copies:
        copy.start()
    for copy in copies:
        copy.wait()


def slot_copies(parts, sv, sem):
    return [pltpu.make_async_copy(part, sv.at[n], sem.at[n]) for n, part in enumerate(parts)]


def columns(src, count):
    return [src.at[:, pl.ds(j * B, B)] for j in range(count)]


def hold_kernel(s, p1, p2, p3, sw, a1, a2, far, sv, sem):
    parts = []
    for src in (s, p1, p2, p3):
        parts += columns(src, 4)
    for src in (sw, a1, a2):
        parts += columns(src, 3)
    parts += [far.at[i] for i in range(4)]
    start_wait(slot_copies(parts, sv, sem))


def row_copies(parts, first, place_ref, lv, sem):
    copies = []
    for n, part in enumerate(parts):
        row = pl.multiple_of(place_ref[first + n], 16)
        copies.append(pltpu.make_async_copy(part, lv.at[:, :, pl.ds(row, 16), :], sem.at[n]))
    return copies


def panel_kernel(place_ref, x1, lh, r1, r2, t1, t2, lv, sem):
    parts = [x1.at[i] for i in range(4)] + [lh, r1, r2]
    parts += [t1.at[i] for i in range(4)] + [t2.at[i] for i in range(3)]
    start_wait(row_copies(parts, 0, place_ref, lv, sem))


def final_kernel(slot_ref, own_ref, place_ref, sv_in, lv_in, a3, r3, t3, off_out, send_out, sv, lv,
                 acc, s_sem, l_sem):
    loads = slot_copies(columns(a3, 3), sv.at[pl.ds(29, 3)], s_sem)
    loads += row_copies([r3, t3], 14, place_ref, lv, l_sem)
    start_wait(loads)
    for k in range(SUP):
        left = jnp.concatenate([sv[slot_ref[k, i]] for i in range(NR)], axis=1)
        acc[k] = jnp.dot(left, lv[k].reshape(NR * B, B), preferred_element_type=jnp.float32)
    for k in range(SUP):
        offs, owns = [], []
        for t in range(2):
            c = own_ref[k, t]
            alive = (c >= 0).astype(jnp.float32)
            off = (acc[k, pl.ds(t * B, B)] * -alive).astype(jnp.bfloat16)
            off_out[pl.ds(t * B, B), pl.ds(k * B, B)] = off
            offs.append(off)
            owns.append(lv[k, jnp.maximum(c, 0)])
        total = lax.dot_general(jnp.concatenate(owns, axis=0), jnp.concatenate(offs, axis=0),
                                (((0,), (0,)), ((), ())), preferred_element_type=jnp.float32)
        send_out[:, k] = (0.5 * (total + total.T)).astype(jnp.bfloat16).reshape(16, 16, B)


def per_device(sigma_anc, lower_blocks, row_blocks, slot_of, inv_diag):
    row = lax.axis_index("prow")
    col = lax.axis_index("pcol")
    y, h, core = row // 4, (row // 2) % 2, row % 2
    z, w = col // 2, col % 2

    my_rows = lax.dynamic_slice_in_dim(row_blocks, col * SUP, SUP, 0)
    order = jnp.arange(NA, dtype=jnp.int32)
    slots = jnp.sum(jnp.where(my_rows[:, :, None] == order, slot_of, 0), axis=2)
    sc = slots // 4
    dz = (sc // 2 - z) % 4
    one_away = jnp.where(dz == 3, 1 + core, 2 - core)
    group = jnp.where(dz == 0, 0, jnp.where(dz == 2, 3, one_away))
    near = group * 4 + slots % 4
    far = jnp.where(slots % 4 == 3, 25 + group, jnp.where(group == 3, 29, 16 + group * 3) + slots % 4)
    pos = jnp.where(sc % 2 == w, near, far).astype(jnp.int32)
    number = jnp.arange(1, NR + 1, dtype=jnp.int32)[None, :, None]
    ours = row * 2 + jnp.arange(2, dtype=jnp.int32)
    own = jnp.sum(jnp.where(slots[:, :, None] == ours, number, 0), axis=1) - 1
    rel = jnp.array([0, 3, 1, 2, 0, 3, 1, 0, 3, 1, 2, 0, 3, 1, 2, 2], jnp.int32)
    flip = jnp.array([0, 0, 0, 0, 1, 1, 1, 0, 0, 0, 0, 1, 1, 1, 1, 1], jnp.int32)
    cross = jnp.array([0, 0, 0, 0, 0, 0, 0, 1, 1, 1, 1, 1, 1, 1, 0, 1], jnp.int32)
    cs = (core + cross) % 2
    place = ((((y + rel * (1 + 2 * cs)) % 4) * 2 + (h + flip) % 2) * 2 + cs) * 16
    place = place.astype(jnp.int32)

    s, l = sigma_anc, lower_blocks
    p1 = z_first(s)
    p2 = z_second(s)
    sw = swap_w(s[:, :3 * B])
    lh = swap_h(l)
    q1 = y_first(l)
    q2 = y_second(l)
    q3 = y_first(q1)
    p3 = z_first(p1)
    p2, sw, lh, q1, q2, q3 = tie(p2, sw, lh, q1, q2, q3)
    r1 = y_first(lh)
    r2 = y_second(lh)
    x1 = jnp.stack([l, q1, q2, q3])
    t1 = swap_core(x1)
    sw, p3 = tie(sw, p3)
    a1 = z_first(sw)
    a2 = z_second(sw)
    far = swap_w(jnp.stack([v[:, 3 * B:] for v in (s, p1, p2, p3)]))
    r3 = y_first(r1)
    t2 = swap_core(jnp.stack([lh, r1, r2]))
    a1, a2, far, r3 = tie(a1, a2, far, r3)
    a3 = z_first(a1)
    t3 = swap_core(r3)
    s, p1, p2, p3, sw, a1, a2, a3, far = in_hbm(s, p1, p2, p3, sw, a1, a2, a3, far)
    lh, r1, r2, r3, x1, t1, t2, t3 = in_hbm(lh, r1, r2, r3, x1, t1, t2, t3)

    hbm = pl.BlockSpec(memory_space=pltpu.HBM)
    smem = pl.BlockSpec(memory_space=pltpu.SMEM)
    vmem = pl.BlockSpec(memory_space=pltpu.VMEM)
    params = pltpu.CompilerParams(vmem_limit_bytes=VMEM_LIMIT)
    final_params = pltpu.CompilerParams(vmem_limit_bytes=FINAL_LIMIT)
    panel_shape = pltpu.VMEM((SUP, NR, B, B), jnp.bfloat16)
    held_shape = pltpu.VMEM((NA, ROWS, B), jnp.bfloat16)
    held = pl.pallas_call(
        hold_kernel,
        out_shape=held_shape,
        in_specs=[hbm] * 8,
        out_specs=vmem,
        scratch_shapes=[pltpu.SemaphoreType.DMA((29,))],
        compiler_params=params,
    )(s, p1, p2, p3, sw, a1, a2, far)
    held = pltpu.with_memory_space_constraint(held, pltpu.VMEM)
    blocks = pl.pallas_call(
        panel_kernel,
        out_shape=panel_shape,
        in_specs=[smem] + [hbm] * 6,
        out_specs=vmem,
        scratch_shapes=[pltpu.SemaphoreType.DMA((14,))],
        compiler_params=params,
    )(place, x1, lh, r1, r2, t1, t2)
    blocks = pltpu.with_memory_space_constraint(blocks, pltpu.VMEM)
    sigma_off, send, _, _ = pl.pallas_call(
        final_kernel,
        out_shape=(
            jax.ShapeDtypeStruct((ROWS, SUP * B), jnp.bfloat16),
            jax.ShapeDtypeStruct((16, SUP, 16, B), jnp.bfloat16),
            held_shape,
            panel_shape,
        ),
        in_specs=[smem] * 3 + [vmem] * 2 + [hbm] * 3,
        out_specs=(vmem, vmem, vmem, vmem),
        input_output_aliases={3: 2, 4: 3},
        scratch_shapes=[
            pltpu.VMEM((SUP, ROWS, B), jnp.float32),
            pltpu.SemaphoreType.DMA((3,)),
            pltpu.SemaphoreType.DMA((2,)),
        ],
        compiler_params=final_params,
    )(pos, own, place, held, blocks, a3, r3, t3)

    parts = lax.all_to_all(send, "prow", split_axis=0, concat_axis=0, tiled=True)
    total = jnp.sum(parts.astype(jnp.float32), axis=0)
    return sigma_off, inv_diag - total


def solution(mesh):
    in_specs = (P("prow", "pcol"), P("pcol", None, "prow", None), P(), P(), P("pcol", "prow", None))
    out_specs = (P("prow", "pcol"), P("pcol", "prow", None))
    return jax.shard_map(
        per_device, mesh=mesh, in_specs=in_specs, out_specs=out_specs, check_vma=False
    )
```

time: 854 us -> 119 us (0.14)
  waiting for transfers between devices: 518 us -> 52.5 us
  blocking collectives: 189 us -> 16.7 us
  local copies, waits for them, and re-layouts: 99.2 us -> 2.61 us
  starting transfers between devices: 0.3 us -> 27.5 us
  matrix products: 25 us -> 0 us
  Pallas kernels: 0 us -> 14.8 us
  between operations: 13.8 us -> 0.85 us
    reduce_scatter x1 -> x0, waiting for transfers between devices: 305 us -> none  [per_device(): lax.psum_scatter(partial_value, 'pcol', scatter_dimension=1, tiled=True)]
    all_to_all x1, blocking collectives: 189 us -> 16.7 us  [per_device(): lax.all_to_all(send, 'prow', split_axis=0, concat_axis=0, tiled=True)]
    psum x1 -> x0, waiting for transfers between devices: 137 us -> none  [per_device(): total = lax.psum(quad.astype(jnp.bfloat16), 'prow').astype(jnp.float32)]
    all_gather x1 -> x0, waiting for transfers between devices: 75.3 us -> none  [per_device(): full_blocks = lax.all_gather(lower_blocks, 'prow', axis=2, tiled=True)]
    ppermute x0 -> x18, waiting for transfers between devices: none -> 52.5 us  [permute(): return lax.ppermute(x, AXES, pairs)]
    all_to_all x2 -> x0, local copies, waits for them, and re-layouts: 42.3 us -> none  [per_device(): lax.all_to_all(panel, 'pcol', split_axis=0, concat_axis=1, tiled=True)]
    convert_element_type x2 -> x0, local copies, waits for them, and re-layouts: 31.9 us -> none  [the longest x1 30.6 us: per_device(): panel.astype(jnp.bfloat16).reshape(ancestors * width, sup_dev * width)]
    ppermute x0 -> x18, starting transfers between devices: none -> 27.5 us  [permute(): return lax.ppermute(x, AXES, pairs)]
  transfers between devices with their start and end apart: 3 -> 18, of which waited for: 3 -> 9; matrix products, arithmetic and copies ran while one was open for 3% -> 5% of each run, Pallas kernels for 0% -> 6%
where the time goes in v2:
time: 119 us
  waiting for transfers between devices  52.5 us (44%)
  starting transfers between devices  27.5 us (23%)
  blocking collectives  16.7 us (14%)
  Pallas kernels  14.8 us (12%)
  other arithmetic  4.06 us (3%)
  local copies, waits for them, and re-layouts  2.61 us (2%)
    ppermute x18, waiting for transfers between devices, permute(): return lax.ppermute(x, AXES, pairs)  52.5 us
    ppermute x18, starting transfers between devices, permute(): return lax.ppermute(x, AXES, pairs)  27.5 us
    all_to_all x1, blocking collectives, per_device(): lax.all_to_all(send, 'prow', split_axis=0, concat_axis=0, tiled=True)  16.7 us
    pallas_call x1, Pallas kernels, per_device(): pl.pallas_call(final_kernel, out_shape=(jax.ShapeDtypeStruct((ROWS, SUP *...  7.56 us
    pallas_call x1, Pallas kernels, per_device(): pl.pallas_call(panel_kernel, out_shape=panel_shape, in_specs=[smem] + [hb...  3.75 us
    pallas_call x1, Pallas kernels, per_device(): pl.pallas_call(hold_kernel, out_shape=held_shape, in_specs=[hbm] * 8, out...  3.5 us
  transfers between devices with their start and end apart: 18, of which 9 were waited for; matrix products, arithmetic and copies ran while one was open for 5% of the time, Pallas kernels for 6%

profile of v2, /device:TPU:0, one launch (start us, length us, event | category | flops | bytes accessed | tf_op | source)
XLA Modules:
  0.0 119.0 jit_solution(10443477070066300743)
XLA Ops:
  0.6 0.0 copy-start
  0.6 0.0 copy-start.9
  0.7 2.1 %collective-permute-start = (bf16[512,1024]{1,0:T(8,128)(2,1)}, bf16[512,1024]{1,0:T(8,128)(2,1)S(1)}, u32[]{:S(2)}, u32[]{:S(2)}) collective-permute-start(bf16[512,1024]{1,0:T(8,128)(2,1)} %s.1), channel_id=1, source_target_pairs={{0,2},{1,3},{2,4},{3,5},{4,6},{5,7},{6,0},{7,1},{8,14},{9,15},{10,... | collective-permute-start | bytes 3145736 | tf_op jit(solution)/shard_map/ppermute | solution.py:28
  2.7 1.6 %collective-permute-start.4 = (bf16[4,16,16,256]{3,2,1,0:T(8,128)(2,1)}, bf16[4,16,16,256]{3,2,1,0:T(8,128)(2,1)S(1)}, u32[]{:S(2)}, u32[]{:S(2)}) collective-permute-start(bf16[4,16,16,256]{3,2,1,0:T(8,128)(2,1)} %param.9), channel_id=1, source_target_pairs={{0,32},{1,33},{2,34},{3,35},{4,36},{5,37},{6,38},{7,39},{8,104},{9... | collective-permute-start | bytes 1572872 | tf_op jit(solution)/shard_map/ppermute | solution.py:28
  4.3 3.0 %collective-permute-start.3 = (bf16[4,16,16,256]{3,2,1,0:T(8,128)(2,1)}, bf16[4,16,16,256]{3,2,1,0:T(8,128)(2,1)S(1)}, u32[]{:S(2)}, u32[]{:S(2)}) collective-permute-start(bf16[4,16,16,256]{3,2,1,0:T(8,128)(2,1)} %param.9), channel_id=1, source_target_pairs={{0,16},{1,17},{2,18},{3,19},{4,20},{5,21},{6,22},{7,23},{8,24},{9,... | collective-permute-start | bytes 1572872 | tf_op jit(solution)/shard_map/ppermute | solution.py:28
  7.3 2.2 %collective-permute-start.1 = (bf16[512,1024]{1,0:T(8,128)(2,1)}, bf16[512,1024]{1,0:T(8,128)(2,1)S(1)}, u32[]{:S(2)}, u32[]{:S(2)}) collective-permute-start(bf16[512,1024]{1,0:T(8,128)(2,1)} %s.1), channel_id=1, source_target_pairs={{0,6},{1,7},{2,0},{3,1},{4,2},{5,3},{6,4},{7,5},{8,10},{9,11},{10,... | collective-permute-start | bytes 3145736 | tf_op jit(solution)/shard_map/ppermute | solution.py:28
  9.5 1.2 %slice.15 = bf16[512,768]{1,0:T(8,128)(2,1)S(1)} slice(bf16[512,1024]{1,0:T(8,128)(2,1)} %s.1), slice={[0:512], [0:768]} | slice | bytes 1572864 | tf_op jit(solution)/shard_map/slice | solution.py:161
  10.8 0.7 collective-permute-start.2
  11.4 1.9 %collective-permute-done.4 = bf16[4,16,16,256]{3,2,1,0:T(8,128)(2,1)S(1)} collective-permute-done((bf16[4,16,16,256]{3,2,1,0:T(8,128)(2,1)}, bf16[4,16,16,256]{3,2,1,0:T(8,128)(2,1)S(1)}, u32[]{:S(2)}, u32[]{:S(2)}) %collective-permute-start.4) | collective-permute-done | bytes 524320 | tf_op jit(solution)/shard_map/ppermute | solution.py:28
  13.3 1.8 %collective-permute-start.5 = (bf16[4,16,16,256]{3,2,1,0:T(8,128)(2,1)}, bf16[4,16,16,256]{3,2,1,0:T(8,128)(2,1)S(1)}, u32[]{:S(2)}, u32[]{:S(2)}) collective-permute-start(bf16[4,16,16,256]{3,2,1,0:T(8,128)(2,1)} %param.9), channel_id=1, source_target_pairs={{0,96},{1,97},{2,98},{3,99},{4,100},{5,101},{6,102},{7,103},{8,40}... | collective-permute-start | bytes 1572872 | tf_op jit(solution)/shard_map/ppermute | solution.py:28
  15.1 3.8 %collective-permute-done.3.lh = bf16[4,16,16,256]{3,2,1,0:T(8,128)(2,1)S(1)} collective-permute-done((bf16[4,16,16,256]{3,2,1,0:T(8,128)(2,1)}, bf16[4,16,16,256]{3,2,1,0:T(8,128)(2,1)S(1)}, u32[]{:S(2)}, u32[]{:S(2)}) %collective-permute-start.3) | collective-permute-done | bytes 524320 | tf_op jit(solution)/shard_map/ppermute | solution.py:28
  18.9 3.5 %collective-permute-start.6 = (bf16[4,16,16,256]{3,2,1,0:T(8,128)(2,1)S(1)}, bf16[4,16,16,256]{3,2,1,0:T(8,128)(2,1)S(1)}, u32[]{:S(2)}, u32[]{:S(2)}) collective-permute-start(bf16[4,16,16,256]{3,2,1,0:T(8,128)(2,1)S(1)} %collective-permute-done.4), channel_id=1, source_target_pairs={{0,32},{1,33},{2,34},{3,35},{4,36},{5,37},{6,38},{7,39},{8,104},{9... | collective-permute-start | bytes 1572872 | tf_op jit(solution)/shard_map/ppermute | solution.py:28
  22.3 0.0 collective-permute-done.p1
  22.4 2.0 %collective-permute-start.7 = (bf16[512,1024]{1,0:T(8,128)(2,1)S(1)}, bf16[512,1024]{1,0:T(8,128)(2,1)S(1)}, u32[]{:S(2)}, u32[]{:S(2)}) collective-permute-start(bf16[512,1024]{1,0:T(8,128)(2,1)S(1)} %collective-permute-done.p1), channel_id=1, source_target_pairs={{0,2},{1,3},{2,4},{3,5},{4,6},{5,7},{6,0},{7,1},{8,14},{9,15},{10,... | collective-permute-start | bytes 3145736 | tf_op jit(solution)/shard_map/ppermute | solution.py:28
  24.4 1.0 slice_bitcast_fusion.3
  25.4 0.0 collective-permute-done.5
  25.4 10.6 %collective-permute-done.2.sw = bf16[512,768]{1,0:T(8,128)(2,1)} collective-permute-done((bf16[512,768]{1,0:T(8,128)(2,1)S(1)}, bf16[512,768]{1,0:T(8,128)(2,1)}, u32[]{:S(2)}, u32[]{:S(2)}) %collective-permute-start.2) | collective-permute-done | bytes 786464 | tf_op jit(solution)/shard_map/ppermute | solution.py:28
  35.9 0.0 collective-permute-done.6
  35.9 0.0 collective-permute-done.1.p2
  35.9 2.7 %collective-permute-start.13 = (bf16[4,16,16,256]{3,2,1,0:T(8,128)(2,1)S(1)}, bf16[4,16,16,256]{3,2,1,0:T(8,128)(2,1)S(1)}, u32[]{:S(2)}, u32[]{:S(2)}) collective-permute-start(bf16[4,16,16,256]{3,2,1,0:T(8,128)(2,1)S(1)} %collective-permute-done.3.lh), channel_id=1, source_target_pairs={{0,96},{1,97},{2,98},{3,99},{4,100},{5,101},{6,102},{7,103},{8,40}... | collective-permute-start | bytes 1572872 | tf_op jit(solution)/shard_map/ppermute | solution.py:28
  38.7 0.2 collective-permute-start.11
  38.9 0.0 copy-done.9
  38.9 0.3 pad_maximum_fusion.x1
  39.2 0.0 copy-start.1
  39.2 1.8 %collective-permute-start.14 = (bf16[4,4,16,16,256]{4,3,2,1,0:T(8,128)(2,1)S(1)}, bf16[4,4,16,16,256]{4,3,2,1,0:T(8,128)(2,1)}, u32[]{:S(2)}, u32[]{:S(2)}) collective-permute-start(bf16[4,4,16,16,256]{4,3,2,1,0:T(8,128)(2,1)S(1)} %pad_maximum_fusion.x1), channel_id=1, source_target_pairs={{0,8},{1,9},{2,10},{3,11},{4,12},{5,13},{6,14},{7,15},{8,0},{9,1},... | collective-permute-start | bytes 6291464 | tf_op jit(solution)/shard_map/ppermute | solution.py:28
  41.0 0.0 copy-done.6
  41.1 11.9 %collective-permute-done.11.r1 = bf16[4,16,16,256]{3,2,1,0:T(8,128)(2,1)S(1)} collective-permute-done((bf16[4,16,16,256]{3,2,1,0:T(8,128)(2,1)S(1)}, bf16[4,16,16,256]{3,2,1,0:T(8,128)(2,1)S(1)}, u32[]{:S(2)}, u32[]{:S(2)}) %collective-permute-start.11) | collective-permute-done | bytes 524320 | tf_op jit(solution)/shard_map/ppermute | solution.py:28
  53.0 0.0 collective-permute-start.12
  53.0 0.0 collective-permute-done.7.p3
  53.1 1.3 %pad_maximum_fusion.2 = bf16[4,512,256]{2,1,0:T(8,128)(2,1)} fusion(bf16[1,512,256]{2,1,0:T(8,128)(2,1)S(1)} %slice_bitcast_fusion.1, bf16[1,512,256]{2,1,0:T(8,128)(2,1)S(1)} %slice_bitcast_fusion.2, bf16[1,512,256]{2,1,0:T(8,128)(2,1)S(1)} %slice_bitcast_fusion, bf16[1,512,256]{2,1,0:T(8,128)(2,1)S(1)} %slice_bitcast_fusion.3), kind=kLoop, calls=%fused_computation.2 | loop fusion | flops 1572864 | bytes 2097152 | tf_op jit(solution)/shard_map/stack | solution.py:175
  54.3 1.5 %collective-permute-start.10 = (bf16[4,512,256]{2,1,0:T(8,128)(2,1)}, bf16[4,512,256]{2,1,0:T(8,128)(2,1)}, u32[]{:S(2)}, u32[]{:S(2)}) collective-permute-start(bf16[4,512,256]{2,1,0:T(8,128)(2,1)} %pad_maximum_fusion.2), channel_id=1, source_target_pairs={{0,1},{1,0},{2,3},{3,2},{4,5},{5,4},{6,7},{7,6},{8,9},{9,8},{10,11... | collective-permute-start | bytes 3145736 | tf_op jit(solution)/shard_map/ppermute | solution.py:28
  55.8 0.0 collective-permute-done.13.r2
  55.8 0.0 copy-done.2
  55.8 1.3 %pad_maximum_fusion.1 = bf16[3,4,16,16,256]{4,3,2,1,0:T(8,128)(2,1)} fusion(bf16[1,4,16,16,256]{4,3,2,1,0:T(8,128)(2,1)S(1)} %bitcast.16, bf16[1,4,16,16,256]{4,3,2,1,0:T(8,128)(2,1)S(1)} %bitcast.17, bf16[1,4,16,16,256]{4,3,2,1,0:T(8,128)(2,1)S(1)} %bitcast.15), kind=kLoop, calls=%fused_computation.1 | loop fusion | flops 1572864 | bytes 3145728 | tf_op jit(solution)/shard_map/stack | solution.py:177
  57.2 0.0 copy-done.1
  57.2 0.0 copy-done.7
  57.2 2.3 %collective-permute-start.9 = (bf16[512,768]{1,0:T(8,128)(2,1)}, bf16[512,768]{1,0:T(8,128)(2,1)}, u32[]{:S(2)}, u32[]{:S(2)}) collective-permute-start(bf16[512,768]{1,0:T(8,128)(2,1)} %collective-permute-done.2.sw), channel_id=1, source_target_pairs={{0,6},{1,7},{2,0},{3,1},{4,2},{5,3},{6,4},{7,5},{8,10},{9,11},{10,... | collective-permute-start | bytes 2359304 | tf_op jit(solution)/shard_map/ppermute | solution.py:28
  59.5 0.0 collective-permute-start.8
  59.5 3.9 %collective-permute-done.12.r3 = bf16[4,16,16,256]{3,2,1,0:T(8,128)(2,1)S(1)} collective-permute-done((bf16[4,16,16,256]{3,2,1,0:T(8,128)(2,1)S(1)}, bf16[4,16,16,256]{3,2,1,0:T(8,128)(2,1)S(1)}, u32[]{:S(2)}, u32[]{:S(2)}) %collective-permute-start.12) | collective-permute-done | bytes 524320 | tf_op jit(solution)/shard_map/ppermute | solution.py:28
  63.4 0.0 collective-permute-start.15
  63.4 0.1 constant_dynamic-slice_fusion
  63.5 0.1 copy.13
  63.6 0.2 select_reduce_fusion
  63.8 14.1 %collective-permute-done.9.a2 = bf16[512,768]{1,0:T(8,128)(2,1)} collective-permute-done((bf16[512,768]{1,0:T(8,128)(2,1)}, bf16[512,768]{1,0:T(8,128)(2,1)}, u32[]{:S(2)}, u32[]{:S(2)}) %collective-permute-start.9) | collective-permute-done | bytes 786464 | tf_op jit(solution)/shard_map/ppermute | solution.py:28
  77.9 1.2 %collective-permute-done.8.a1 = bf16[512,768]{1,0:T(8,128)(2,1)} collective-permute-done((bf16[512,768]{1,0:T(8,128)(2,1)}, bf16[512,768]{1,0:T(8,128)(2,1)}, u32[]{:S(2)}, u32[]{:S(2)}) %collective-permute-start.8) | collective-permute-done | bytes 786464 | tf_op jit(solution)/shard_map/ppermute | solution.py:28
  79.1 1.4 %collective-permute-done.10.far = bf16[4,512,256]{2,1,0:T(8,128)(2,1)} collective-permute-done((bf16[4,512,256]{2,1,0:T(8,128)(2,1)}, bf16[4,512,256]{2,1,0:T(8,128)(2,1)}, u32[]{:S(2)}, u32[]{:S(2)}) %collective-permute-start.10) | collective-permute-done | bytes 1048608 | tf_op jit(solution)/shard_map/ppermute | solution.py:28
  80.5 0.0 collective-permute-start.16
  80.5 0.0 copy-done.13
  80.6 2.1 %collective-permute-start.17 = (bf16[4,16,16,256]{3,2,1,0:T(8,128)(2,1)S(1)}, bf16[4,16,16,256]{3,2,1,0:T(8,128)(2,1)}, u32[]{:S(2)}, u32[]{:S(2)}) collective-permute-start(bf16[4,16,16,256]{3,2,1,0:T(8,128)(2,1)S(1)} %collective-permute-done.12.r3), channel_id=1, source_target_pairs={{0,8},{1,9},{2,10},{3,11},{4,12},{5,13},{6,14},{7,15},{8,0},{9,1},... | collective-permute-start | bytes 1572872 | tf_op jit(solution)/shard_map/ppermute | solution.py:28
  82.7 0.2 select_reduce_fusion.1
  82.9 0.1 copy.14
  83.0 3.5 %shard_map.95.sv_in = bf16[32,512,256]{2,1,0:T(8,128)(2,1)S(1)} custom-call(bf16[512,1024]{1,0:T(8,128)(2,1)} %s.1, bf16[512,1024]{1,0:T(8,128)(2,1)} %copy-done.5, bf16[512,1024]{1,0:T(8,128)(2,1)} %copy-done.6, bf16[512,1024]{1,0:T(8,128)(2,1)} %copy-done.7, bf16[512,768]{1,0:T(8,128)(2,1)} %collective-permute-done.2.sw, ...), custom_call_target="tpu_custom_call" | custom-call | tf_op jit(solution)/shard_map/pallas_call | solution.py:191
  86.5 0.0 copy-done.3
  86.5 0.0 copy-done.8
  86.5 0.0 collective-permute-done.15.t2
  86.5 0.0 collective-permute-done.14.t1
  86.6 3.7 %shard_map.96.lv_in = bf16[4,16,256,256]{3,2,1,0:T(8,128)(2,1)S(1)} custom-call(s32[16]{0:T(128)S(1)} %fusion.13.place_ref, bf16[4,4,16,16,256]{4,3,2,1,0:T(8,128)(2,1)} %copy-done.1, bf16[4,16,16,256]{3,2,1,0:T(8,128)(2,1)} %copy-done.2, bf16[4,16,16,256]{3,2,1,0:T(8,128)(2,1)} %copy-done.4, bf16[4,16,16,256]{3,2,1,0:T(8,128)(2,1)} %copy-done.3, ...), custom_call_target="tpu_custom_call" | custom-call | tf_op jit(solution)/shard_map/pallas_call | solution.py:200
  90.3 0.0 copy-start.10
  90.3 0.0 collective-permute-done.17.t3
  90.3 3.7 %collective-permute-done.16.a3 = bf16[512,768]{1,0:T(8,128)(2,1)} collective-permute-done((bf16[512,768]{1,0:T(8,128)(2,1)}, bf16[512,768]{1,0:T(8,128)(2,1)}, u32[]{:S(2)}, u32[]{:S(2)}) %collective-permute-start.16) | collective-permute-done | bytes 786464 | tf_op jit(solution)/shard_map/ppermute | solution.py:28
  94.0 7.6 %shard_map.97 = (bf16[512,1024]{1,0:T(8,128)(2,1)}, bf16[16,4,16,256]{3,2,1,0:T(8,128)(2,1)S(1)}, bf16[32,512,256]{2,1,0:T(8,128)(2,1)S(1)}, bf16[4,16,256,256]{3,2,1,0:T(8,128)(2,1)S(1)}) custom-call(s32[4,16]{1,0:T(4,128)S(1)} %select_select_fusion.slot_ref, s32[4,2]{1,0:T(4,128)S(1)} %broadcast_add_fusion.own_ref, ...), custom_call_target="tpu_custom_call", output_to_operand_aliasing={{2}: (3, {}), {3}: (4, {})} | custom-call | tf_op jit(solution)/shard_map/pallas_call | solution.py:209
  101.6 16.7 %all_to_all.5 = bf16[16,4,16,256]{3,2,1,0:T(8,128)(2,1)S(1)} all-to-all(bf16[16,4,16,256]{3,2,1,0:T(8,128)(2,1)S(1)} %get-tuple-element.29), channel_id=1, replica_groups=mesh['prow'=16,'pcol'=8] {'prow'}, dimensions={0} | all-to-all | bytes 1048576 | tf_op jit(solution)/shard_map/all_to_all | solution.py:228
  118.3 0.1 convert_reduce_fusion
  118.3 0.6 sub.44
  (26 shorter events, 0.2 us)
Async XLA Ops:
  0.6 62.8 %copy-start = (s32[32,16]{0,1:T(8,128)S(1)}, s32[32,16]{0,1:T(8,128)}, u32[]{:S(2)}) copy-start(s32[32,16]{0,1:T(8,128)} %param.10) | copy-start | bytes 6148
  0.6 38.3 %copy-start.9 = (bf16[4,16,16,256]{3,2,1,0:T(8,128)(2,1)S(1)}, bf16[4,16,16,256]{3,2,1,0:T(8,128)(2,1)}, u32[]{:S(2)}) copy-start(bf16[4,16,16,256]{3,2,1,0:T(8,128)(2,1)} %param.9) | copy-start | bytes 1572868
  0.7 21.7 %collective-permute-start = (bf16[512,1024]{1,0:T(8,128)(2,1)}, bf16[512,1024]{1,0:T(8,128)(2,1)S(1)}, u32[]{:S(2)}, u32[]{:S(2)}) collective-permute-start(bf16[512,1024]{1,0:T(8,128)(2,1)} %s.1), channel_id=1, source_target_pairs={{0,2},{1,3},{2,4},{3,5},{4,6},{5,7},{6,0},{7,1},{8,14},{9,15},{10,... | collective-permute-start | bytes 3145736 | tf_op jit(solution)/shard_map/ppermute | solution.py:28
  2.7 10.6 %collective-permute-start.4 = (bf16[4,16,16,256]{3,2,1,0:T(8,128)(2,1)}, bf16[4,16,16,256]{3,2,1,0:T(8,128)(2,1)S(1)}, u32[]{:S(2)}, u32[]{:S(2)}) collective-permute-start(bf16[4,16,16,256]{3,2,1,0:T(8,128)(2,1)} %param.9), channel_id=1, source_target_pairs={{0,32},{1,33},{2,34},{3,35},{4,36},{5,37},{6,38},{7,39},{8,104},{9... | collective-permute-start | bytes 1572872 | tf_op jit(solution)/shard_map/ppermute | solution.py:28
  4.3 14.6 %collective-permute-start.3 = (bf16[4,16,16,256]{3,2,1,0:T(8,128)(2,1)}, bf16[4,16,16,256]{3,2,1,0:T(8,128)(2,1)S(1)}, u32[]{:S(2)}, u32[]{:S(2)}) collective-permute-start(bf16[4,16,16,256]{3,2,1,0:T(8,128)(2,1)} %param.9), channel_id=1, source_target_pairs={{0,16},{1,17},{2,18},{3,19},{4,20},{5,21},{6,22},{7,23},{8,24},{9,... | collective-permute-start | bytes 1572872 | tf_op jit(solution)/shard_map/ppermute | solution.py:28
  7.3 28.6 %collective-permute-start.1 = (bf16[512,1024]{1,0:T(8,128)(2,1)}, bf16[512,1024]{1,0:T(8,128)(2,1)S(1)}, u32[]{:S(2)}, u32[]{:S(2)}) collective-permute-start(bf16[512,1024]{1,0:T(8,128)(2,1)} %s.1), channel_id=1, source_target_pairs={{0,6},{1,7},{2,0},{3,1},{4,2},{5,3},{6,4},{7,5},{8,10},{9,11},{10,... | collective-permute-start | bytes 3145736 | tf_op jit(solution)/shard_map/ppermute | solution.py:28
  10.8 25.2 %collective-permute-start.2 = (bf16[512,768]{1,0:T(8,128)(2,1)S(1)}, bf16[512,768]{1,0:T(8,128)(2,1)}, u32[]{:S(2)}, u32[]{:S(2)}) collective-permute-start(bf16[512,768]{1,0:T(8,128)(2,1)S(1)} %slice.15), channel_id=1, source_target_pairs={{0,1},{1,0},{2,3},{3,2},{4,5},{5,4},{6,7},{7,6},{8,9},{9,8},{10,11... | collective-permute-start | bytes 2359304 | tf_op jit(solution)/shard_map/ppermute | solution.py:28
  13.3 12.0 %collective-permute-start.5 = (bf16[4,16,16,256]{3,2,1,0:T(8,128)(2,1)}, bf16[4,16,16,256]{3,2,1,0:T(8,128)(2,1)S(1)}, u32[]{:S(2)}, u32[]{:S(2)}) collective-permute-start(bf16[4,16,16,256]{3,2,1,0:T(8,128)(2,1)} %param.9), channel_id=1, source_target_pairs={{0,96},{1,97},{2,98},{3,99},{4,100},{5,101},{6,102},{7,103},{8,40}... | collective-permute-start | bytes 1572872 | tf_op jit(solution)/shard_map/ppermute | solution.py:28
  18.9 37.0 %copy-start.2 = (bf16[4,16,16,256]{3,2,1,0:T(8,128)(2,1)}, bf16[4,16,16,256]{3,2,1,0:T(8,128)(2,1)S(1)}, u32[]{:S(2)}) copy-start(bf16[4,16,16,256]{3,2,1,0:T(8,128)(2,1)S(1)} %collective-permute-done.3.lh) | copy-start | bytes 1572868
  18.9 17.0 %collective-permute-start.6 = (bf16[4,16,16,256]{3,2,1,0:T(8,128)(2,1)S(1)}, bf16[4,16,16,256]{3,2,1,0:T(8,128)(2,1)S(1)}, u32[]{:S(2)}, u32[]{:S(2)}) collective-permute-start(bf16[4,16,16,256]{3,2,1,0:T(8,128)(2,1)S(1)} %collective-permute-done.4), channel_id=1, source_target_pairs={{0,32},{1,33},{2,34},{3,35},{4,36},{5,37},{6,38},{7,39},{8,104},{9... | collective-permute-start | bytes 1572872 | tf_op jit(solution)/shard_map/ppermute | solution.py:28
  22.3 18.7 %copy-start.5 = (bf16[512,1024]{1,0:T(8,128)(2,1)}, bf16[512,1024]{1,0:T(8,128)(2,1)S(1)}, u32[]{:S(2)}) copy-start(bf16[512,1024]{1,0:T(8,128)(2,1)S(1)} %collective-permute-done.p1) | copy-start | bytes 3145732
  22.4 30.6 %collective-permute-start.7 = (bf16[512,1024]{1,0:T(8,128)(2,1)S(1)}, bf16[512,1024]{1,0:T(8,128)(2,1)S(1)}, u32[]{:S(2)}, u32[]{:S(2)}) collective-permute-start(bf16[512,1024]{1,0:T(8,128)(2,1)S(1)} %collective-permute-done.p1), channel_id=1, source_target_pairs={{0,2},{1,3},{2,4},{3,5},{4,6},{5,7},{6,0},{7,1},{8,14},{9,15},{10,... | collective-permute-start | bytes 3145736 | tf_op jit(solution)/shard_map/ppermute | solution.py:28
  35.9 5.1 %copy-start.6 = (bf16[512,1024]{1,0:T(8,128)(2,1)}, bf16[512,1024]{1,0:T(8,128)(2,1)S(1)}, u32[]{:S(2)}) copy-start(bf16[512,1024]{1,0:T(8,128)(2,1)S(1)} %collective-permute-done.1.p2) | copy-start | bytes 3145732
  35.9 19.9 %collective-permute-start.13 = (bf16[4,16,16,256]{3,2,1,0:T(8,128)(2,1)S(1)}, bf16[4,16,16,256]{3,2,1,0:T(8,128)(2,1)S(1)}, u32[]{:S(2)}, u32[]{:S(2)}) collective-permute-start(bf16[4,16,16,256]{3,2,1,0:T(8,128)(2,1)S(1)} %collective-permute-done.3.lh), channel_id=1, source_target_pairs={{0,96},{1,97},{2,98},{3,99},{4,100},{5,101},{6,102},{7,103},{8,40}... | collective-permute-start | bytes 1572872 | tf_op jit(solution)/shard_map/ppermute | solution.py:28
  38.7 14.3 %collective-permute-start.11 = (bf16[4,16,16,256]{3,2,1,0:T(8,128)(2,1)S(1)}, bf16[4,16,16,256]{3,2,1,0:T(8,128)(2,1)S(1)}, u32[]{:S(2)}, u32[]{:S(2)}) collective-permute-start(bf16[4,16,16,256]{3,2,1,0:T(8,128)(2,1)S(1)} %collective-permute-done.3.lh), channel_id=1, source_target_pairs={{0,32},{1,33},{2,34},{3,35},{4,36},{5,37},{6,38},{7,39},{8,104},{9... | collective-permute-start | bytes 1572872 | tf_op jit(solution)/shard_map/ppermute | solution.py:28
  39.2 18.0 %copy-start.1 = (bf16[4,4,16,16,256]{4,3,2,1,0:T(8,128)(2,1)}, bf16[4,4,16,16,256]{4,3,2,1,0:T(8,128)(2,1)S(1)}, u32[]{:S(2)}) copy-start(bf16[4,4,16,16,256]{4,3,2,1,0:T(8,128)(2,1)S(1)} %pad_maximum_fusion.x1) | copy-start | bytes 6291460
  39.2 47.4 %collective-permute-start.14 = (bf16[4,4,16,16,256]{4,3,2,1,0:T(8,128)(2,1)S(1)}, bf16[4,4,16,16,256]{4,3,2,1,0:T(8,128)(2,1)}, u32[]{:S(2)}, u32[]{:S(2)}) collective-permute-start(bf16[4,4,16,16,256]{4,3,2,1,0:T(8,128)(2,1)S(1)} %pad_maximum_fusion.x1), channel_id=1, source_target_pairs={{0,8},{1,9},{2,10},{3,11},{4,12},{5,13},{6,14},{7,15},{8,0},{9,1},... | collective-permute-start | bytes 6291464 | tf_op jit(solution)/shard_map/ppermute | solution.py:28
  53.0 4.2 %copy-start.4 = (bf16[4,16,16,256]{3,2,1,0:T(8,128)(2,1)}, bf16[4,16,16,256]{3,2,1,0:T(8,128)(2,1)S(1)}, u32[]{:S(2)}) copy-start(bf16[4,16,16,256]{3,2,1,0:T(8,128)(2,1)S(1)} %collective-permute-done.11.r1) | copy-start | bytes 1572868
  53.0 10.4 %collective-permute-start.12 = (bf16[4,16,16,256]{3,2,1,0:T(8,128)(2,1)S(1)}, bf16[4,16,16,256]{3,2,1,0:T(8,128)(2,1)S(1)}, u32[]{:S(2)}, u32[]{:S(2)}) collective-permute-start(bf16[4,16,16,256]{3,2,1,0:T(8,128)(2,1)S(1)} %collective-permute-done.11.r1), channel_id=1, source_target_pairs={{0,32},{1,33},{2,34},{3,35},{4,36},{5,37},{6,38},{7,39},{8,104},{9... | collective-permute-start | bytes 1572872 | tf_op jit(solution)/shard_map/ppermute | solution.py:28
  53.0 4.2 %copy-start.7 = (bf16[512,1024]{1,0:T(8,128)(2,1)}, bf16[512,1024]{1,0:T(8,128)(2,1)S(1)}, u32[]{:S(2)}) copy-start(bf16[512,1024]{1,0:T(8,128)(2,1)S(1)} %collective-permute-done.7.p3) | copy-start | bytes 3145732
  54.3 9.2 %copy-start.11 = (s32[32]{0:T(128)S(1)}, s32[32]{0:T(128)}, u32[]{:S(2)}) copy-start(s32[32]{0:T(128)} %param.11) | copy-start | bytes 388
  54.3 26.2 %copy-start.12 = (s32[16]{0:T(128)S(1)}, s32[16]{0:T(128)}, u32[]{:S(2)}) copy-start(s32[16]{0:T(128)} %constant.150.clone) | copy-start | bytes 196
  54.3 26.2 %copy-start.13 = (s32[16]{0:T(128)S(1)}, s32[16]{0:T(128)}, u32[]{:S(2)}) copy-start(s32[16]{0:T(128)} %constant.149.clone) | copy-start | bytes 196
  54.3 26.2 %copy-start.14 = (s32[16]{0:T(128)S(1)}, s32[16]{0:T(128)}, u32[]{:S(2)}) copy-start(s32[16]{0:T(128)} %constant.148.clone) | copy-start | bytes 196
  54.3 26.2 %collective-permute-start.10 = (bf16[4,512,256]{2,1,0:T(8,128)(2,1)}, bf16[4,512,256]{2,1,0:T(8,128)(2,1)}, u32[]{:S(2)}, u32[]{:S(2)}) collective-permute-start(bf16[4,512,256]{2,1,0:T(8,128)(2,1)} %pad_maximum_fusion.2), channel_id=1, source_target_pairs={{0,1},{1,0},{2,3},{3,2},{4,5},{5,4},{6,7},{7,6},{8,9},{9,8},{10,11... | collective-permute-start | bytes 3145736 | tf_op jit(solution)/shard_map/ppermute | solution.py:28
  55.8 30.7 %copy-start.3 = (bf16[4,16,16,256]{3,2,1,0:T(8,128)(2,1)}, bf16[4,16,16,256]{3,2,1,0:T(8,128)(2,1)S(1)}, u32[]{:S(2)}) copy-start(bf16[4,16,16,256]{3,2,1,0:T(8,128)(2,1)S(1)} %collective-permute-done.13.r2) | copy-start | bytes 1572868
  57.2 20.7 %collective-permute-start.9 = (bf16[512,768]{1,0:T(8,128)(2,1)}, bf16[512,768]{1,0:T(8,128)(2,1)}, u32[]{:S(2)}, u32[]{:S(2)}) collective-permute-start(bf16[512,768]{1,0:T(8,128)(2,1)} %collective-permute-done.2.sw), channel_id=1, source_target_pairs={{0,6},{1,7},{2,0},{3,1},{4,2},{5,3},{6,4},{7,5},{8,10},{9,11},{10,... | collective-permute-start | bytes 2359304 | tf_op jit(solution)/shard_map/ppermute | solution.py:28
  59.5 19.7 %collective-permute-start.8 = (bf16[512,768]{1,0:T(8,128)(2,1)}, bf16[512,768]{1,0:T(8,128)(2,1)}, u32[]{:S(2)}, u32[]{:S(2)}) collective-permute-start(bf16[512,768]{1,0:T(8,128)(2,1)} %collective-permute-done.2.sw), channel_id=1, source_target_pairs={{0,2},{1,3},{2,4},{3,5},{4,6},{5,7},{6,0},{7,1},{8,14},{9,15},{10,... | collective-permute-start | bytes 2359304 | tf_op jit(solution)/shard_map/ppermute | solution.py:28
  63.4 23.1 %copy-start.8 = (bf16[4,16,16,256]{3,2,1,0:T(8,128)(2,1)}, bf16[4,16,16,256]{3,2,1,0:T(8,128)(2,1)S(1)}, u32[]{:S(2)}) copy-start(bf16[4,16,16,256]{3,2,1,0:T(8,128)(2,1)S(1)} %collective-permute-done.12.r3) | copy-start | bytes 1572868
  63.4 23.2 %collective-permute-start.15 = (bf16[3,4,16,16,256]{4,3,2,1,0:T(8,128)(2,1)}, bf16[3,4,16,16,256]{4,3,2,1,0:T(8,128)(2,1)}, u32[]{:S(2)}, u32[]{:S(2)}) collective-permute-start(bf16[3,4,16,16,256]{4,3,2,1,0:T(8,128)(2,1)} %pad_maximum_fusion.1), channel_id=1, source_target_pairs={{0,8},{1,9},{2,10},{3,11},{4,12},{5,13},{6,14},{7,15},{8,0},{9,1},... | collective-permute-start | bytes 4718600 | tf_op jit(solution)/shard_map/ppermute | solution.py:28
  80.5 13.5 %collective-permute-start.16 = (bf16[512,768]{1,0:T(8,128)(2,1)}, bf16[512,768]{1,0:T(8,128)(2,1)}, u32[]{:S(2)}, u32[]{:S(2)}) collective-permute-start(bf16[512,768]{1,0:T(8,128)(2,1)} %collective-permute-done.8.a1), channel_id=1, source_target_pairs={{0,2},{1,3},{2,4},{3,5},{4,6},{5,7},{6,0},{7,1},{8,14},{9,15},{10,... | collective-permute-start | bytes 2359304 | tf_op jit(solution)/shard_map/ppermute | solution.py:28
  80.6 9.8 %collective-permute-start.17 = (bf16[4,16,16,256]{3,2,1,0:T(8,128)(2,1)S(1)}, bf16[4,16,16,256]{3,2,1,0:T(8,128)(2,1)}, u32[]{:S(2)}, u32[]{:S(2)}) collective-permute-start(bf16[4,16,16,256]{3,2,1,0:T(8,128)(2,1)S(1)} %collective-permute-done.12.r3), channel_id=1, source_target_pairs={{0,8},{1,9},{2,10},{3,11},{4,12},{5,13},{6,14},{7,15},{8,0},{9,1},... | collective-permute-start | bytes 1572872 | tf_op jit(solution)/shard_map/ppermute | solution.py:28
  90.3 28.0 %copy-start.10 = (f32[4,16,256]{2,1,0:T(8,128)S(1)}, f32[4,16,256]{2,1,0:T(8,128)}, u32[]{:S(2)}) copy-start(f32[4,16,256]{2,1,0:T(8,128)} %param.12) | copy-start | bytes 196612

commit v3 on v2

--- a/solution.py
+++ b/solution.py
@@ -85,11 +85,11 @@
 
 def hold_kernel(s, p1, p2, p3, sw, a1, a2, far, sv, sem):
     parts = []
-    for src in (s, p1, p2, p3):
+    for src in (s, p1, p2, p3, sw):
         parts += columns(src, 4)
-    for src in (sw, a1, a2):
-        parts += columns(src, 3)
-    parts += [far.at[i] for i in range(4)]
+    for i, src in enumerate((a1, a2)):
+        parts += columns(src, 3) + [far.at[i]]
+    parts.append(far.at[2])
     start_wait(slot_copies(parts, sv, sem))
 
 
@@ -101,13 +101,13 @@
     return copies
 
 
-def panel_kernel(place_ref, x1, lh, r1, r2, t1, t2, lv, sem):
-    parts = [x1.at[i] for i in range(4)] + [lh, r1, r2]
-    parts += [t1.at[i] for i in range(4)] + [t2.at[i] for i in range(3)]
+def panel_kernel(place_ref, x0, x1, lh, r1, r2, tx0, tx1, t0, t2, lv, sem):
+    parts = [x0.at[0], x0.at[1], x1.at[0], x1.at[1], lh, r1, r2]
+    parts += [tx0.at[0], tx0.at[1], tx1.at[0], tx1.at[1], t0, t2.at[0], t2.at[1]]
     start_wait(row_copies(parts, 0, place_ref, lv, sem))
 
 
-def final_kernel(slot_ref, own_ref, place_ref, sv_in, lv_in, a3, r3, t3, off_out, send_out, sv, lv,
+def final_kernel(slot_ref, own_ref, place_ref, core_ref, sv_in, lv_in, a3, r3, t3, off_out, keep_out, send_out, sv, lv,
                  acc, s_sem, l_sem):
     loads = slot_copies(columns(a3, 3), sv.at[pl.ds(29, 3)], s_sem)
     loads += row_copies([r3, t3], 14, place_ref, lv, l_sem)
@@ -115,6 +115,7 @@
     for k in range(SUP):
         left = jnp.concatenate([sv[slot_ref[k, i]] for i in range(NR)], axis=1)
         acc[k] = jnp.dot(left, lv[k].reshape(NR * B, B), preferred_element_type=jnp.float32)
+    core = core_ref[0]
     for k in range(SUP):
         offs, owns = [], []
         for t in range(2):
@@ -126,7 +127,9 @@
             owns.append(lv[k, jnp.maximum(c, 0)])
         total = lax.dot_general(jnp.concatenate(owns, axis=0), jnp.concatenate(offs, axis=0),
                                 (((0,), (0,)), ((), ())), preferred_element_type=jnp.float32)
-        send_out[:, k] = (0.5 * (total + total.T)).astype(jnp.bfloat16).reshape(16, 16, B)
+        part = (0.5 * (total + total.T)).reshape(8, 2, 16, B)
+        keep_out[:, k] = jnp.where(core == 0, part[:, 0], part[:, 1])
+        send_out[:, k] = jnp.where(core == 0, part[:, 1], part[:, 0]).astype(jnp.bfloat16)
 
 
 def per_device(sigma_anc, lower_blocks, row_blocks, slot_of, inv_diag):
@@ -143,7 +146,7 @@
     one_away = jnp.where(dz == 3, 1 + core, 2 - core)
     group = jnp.where(dz == 0, 0, jnp.where(dz == 2, 3, one_away))
     near = group * 4 + slots % 4
-    far = jnp.where(slots % 4 == 3, 25 + group, jnp.where(group == 3, 29, 16 + group * 3) + slots % 4)
+    far = jnp.where(group == 3, jnp.where(slots % 4 == 3, 28, 29 + slots % 4), 16 + group * 4 + slots % 4)
     pos = jnp.where(sc % 2 == w, near, far).astype(jnp.int32)
     number = jnp.arange(1, NR + 1, dtype=jnp.int32)[None, :, None]
     ours = row * 2 + jnp.arange(2, dtype=jnp.int32)
@@ -158,28 +161,34 @@
     s, l = sigma_anc, lower_blocks
     p1 = z_first(s)
     p2 = z_second(s)
-    sw = swap_w(s[:, :3 * B])
-    lh = swap_h(l)
+    sw = swap_w(s)
+    wa = sw[:, :3 * B]
     q1 = y_first(l)
     q2 = y_second(l)
+    p1, q1, q2 = tie(p1, q1, q2)
+    p3 = z_first(p1)
+    lh = swap_h(l)
     q3 = y_first(q1)
-    p3 = z_first(p1)
-    p2, sw, lh, q1, q2, q3 = tie(p2, sw, lh, q1, q2, q3)
+    p2, p3, wa, lh, q3 = tie(p2, p3, wa, lh, q3)
+    a1 = z_first(wa)
+    a2 = z_second(wa)
+    far = swap_w(jnp.stack([v[:, 3 * B:] for v in (p1, p2, p3)]))
     r1 = y_first(lh)
     r2 = y_second(lh)
-    x1 = jnp.stack([l, q1, q2, q3])
-    t1 = swap_core(x1)
-    sw, p3 = tie(sw, p3)
-    a1 = z_first(sw)
-    a2 = z_second(sw)
-    far = swap_w(jnp.stack([v[:, 3 * B:] for v in (s, p1, p2, p3)]))
+    r1, r2, q1, q3 = tie(r1, r2, q1, q3)
     r3 = y_first(r1)
-    t2 = swap_core(jnp.stack([lh, r1, r2]))
-    a1, a2, far, r3 = tie(a1, a2, far, r3)
+    x0 = jnp.stack([l, q1])
+    x1 = jnp.stack([q2, q3])
+    tx0 = swap_core(x0)
+    tx1 = swap_core(x1)
+    t0 = swap_core(lh)
+    t2 = swap_core(jnp.stack([r1, r2]))
+    a1, a2, far = tie(a1, a2, far)
     a3 = z_first(a1)
     t3 = swap_core(r3)
     s, p1, p2, p3, sw, a1, a2, a3, far = in_hbm(s, p1, p2, p3, sw, a1, a2, a3, far)
-    lh, r1, r2, r3, x1, t1, t2, t3 = in_hbm(lh, r1, r2, r3, x1, t1, t2, t3)
+    lh, r1, r2, r3, x0, x1 = in_hbm(lh, r1, r2, r3, x0, x1)
+    t0, tx0, tx1, t2, t3 = in_hbm(t0, tx0, tx1, t2, t3)
 
     hbm = pl.BlockSpec(memory_space=pltpu.HBM)
     smem = pl.BlockSpec(memory_space=pltpu.SMEM)
@@ -200,32 +209,35 @@
     blocks = pl.pallas_call(
         panel_kernel,
         out_shape=panel_shape,
-        in_specs=[smem] + [hbm] * 6,
+        in_specs=[smem] + [hbm] * 9,
         out_specs=vmem,
         scratch_shapes=[pltpu.SemaphoreType.DMA((14,))],
         compiler_params=params,
-    )(place, x1, lh, r1, r2, t1, t2)
+    )(place, x0, x1, lh, r1, r2, tx0, tx1, t0, t2)
     blocks = pltpu.with_memory_space_constraint(blocks, pltpu.VMEM)
-    sigma_off, send, _, _ = pl.pallas_call(
+    sigma_off, keep, send, _, _ = pl.pallas_call(
         final_kernel,
         out_shape=(
             jax.ShapeDtypeStruct((ROWS, SUP * B), jnp.bfloat16),
-            jax.ShapeDtypeStruct((16, SUP, 16, B), jnp.bfloat16),
+            jax.ShapeDtypeStruct((8, SUP, 16, B), jnp.float32),
+            jax.ShapeDtypeStruct((8, SUP, 16, B), jnp.bfloat16),
             held_shape,
             panel_shape,
         ),
-        in_specs=[smem] * 3 + [vmem] * 2 + [hbm] * 3,
-        out_specs=(vmem, vmem, vmem, vmem),
-        input_output_aliases={3: 2, 4: 3},
+        in_specs=[smem] * 4 + [vmem] * 2 + [hbm] * 3,
+        out_specs=(vmem,) * 5,
+        input_output_aliases={4: 3, 5: 4},
         scratch_shapes=[
             pltpu.VMEM((SUP, ROWS, B), jnp.float32),
             pltpu.SemaphoreType.DMA((3,)),
             pltpu.SemaphoreType.DMA((2,)),
         ],
         compiler_params=final_params,
-    )(pos, own, place, held, blocks, a3, r3, t3)
-
-    parts = lax.all_to_all(send, "prow", split_axis=0, concat_axis=0, tiled=True)
+    )(pos, own, place, core.reshape(1).astype(jnp.int32), held, blocks, a3, r3, t3)
+
+    halves = (keep + swap_core(send).astype(jnp.float32)).astype(jnp.bfloat16)
+    parts = lax.all_to_all(halves, "prow", split_axis=0, concat_axis=0, tiled=True,
+                           axis_index_groups=[list(range(c, 16, 2)) for c in range(2)])
     total = jnp.sum(parts.astype(jnp.float32), axis=0)
     return sigma_off, inv_diag - total
 

time: 119 us -> 106 us (0.89)
  waiting for transfers between devices: 52.5 us -> 44.2 us
  blocking collectives: 16.7 us -> 12 us
  other arithmetic: 4.06 us -> 7.95 us
  starting transfers between devices: 27.5 us -> 24.6 us
    ppermute x18 -> x21, waiting for transfers between devices: 52.5 us -> 44.2 us  [permute(): return lax.ppermute(x, AXES, pairs)]
    all_to_all x1, blocking collectives: 16.7 us -> 12 us  [per_device(): lax.all_to_all(halves, 'prow', split_axis=0, concat_axis=0, tiled=True, a...]
    another operation x3 -> x4, other arithmetic: 2.84 us -> 6.68 us  [the longest x1 2.72 us: per_device(): t2 = swap_core(jnp.stack([r1, r2]))]
    ppermute x18 -> x21, starting transfers between devices: 27.5 us -> 24.6 us  [permute(): return lax.ppermute(x, AXES, pairs)]
  transfers between devices with their start and end apart: 18 -> 21, of which waited for: 9 -> 11; matrix products, arithmetic and copies ran while one was open for 5% -> 8% of each run, Pallas kernels for 6% -> 7%
where the time goes in v3:
time: 106 us
  waiting for transfers between devices  44.2 us (42%)
  starting transfers between devices  24.6 us (23%)
  Pallas kernels  14.8 us (14%)
  blocking collectives  12 us (11%)
  other arithmetic  7.95 us (8%)
  local copies, waits for them, and re-layouts  1.59 us (2%)
    ppermute x21, waiting for transfers between devices, permute(): return lax.ppermute(x, AXES, pairs)  44.2 us
    ppermute x21, starting transfers between devices, permute(): return lax.ppermute(x, AXES, pairs)  24.6 us
    all_to_all x1, blocking collectives, per_device(): lax.all_to_all(halves, 'prow', split_axis=0, concat_axis=0, tiled=True, a...  12 us
    pallas_call x1, Pallas kernels, per_device(): pl.pallas_call(final_kernel, out_shape=(jax.ShapeDtypeStruct((ROWS, SUP *...  7.56 us
    pallas_call x1, Pallas kernels, per_device(): pl.pallas_call(panel_kernel, out_shape=panel_shape, in_specs=[smem] + [hb...  3.75 us
    pallas_call x1, Pallas kernels, per_device(): pl.pallas_call(hold_kernel, out_shape=held_shape, in_specs=[hbm] * 8, out...  3.5 us
    another operation x1, other arithmetic, per_device(): t2 = swap_core(jnp.stack([r1, r2]))  2.72 us
  transfers between devices with their start and end apart: 21, of which 11 were waited for; matrix products, arithmetic and copies ran while one was open for 8% of the time, Pallas kernels for 7%

profile of v3, /device:TPU:0, one launch (start us, length us, event | category | flops | bytes accessed | tf_op | source)
XLA Modules:
  0.0 106.1 jit_solution(17165843426630062412)
XLA Ops:
  0.6 0.0 copy-start
  0.6 0.0 copy-start.13
  0.7 0.0 copy-start.14
  0.7 0.0 copy-start.15
  0.7 2.1 %collective-permute-start = (bf16[512,1024]{1,0:T(8,128)(2,1)}, bf16[512,1024]{1,0:T(8,128)(2,1)S(1)}, u32[]{:S(2)}, u32[]{:S(2)}) collective-permute-start(bf16[512,1024]{1,0:T(8,128)(2,1)} %s.1), channel_id=1, source_target_pairs={{0,2},{1,3},{2,4},{3,5},{4,6},{5,7},{6,0},{7,1},{8,14},{9,15},{10,... | collective-permute-start | bytes 3145736 | tf_op jit(solution)/shard_map/ppermute | solution.py:28
  2.8 3.0 %collective-permute-start.2 = (bf16[4,16,16,256]{3,2,1,0:T(8,128)(2,1)}, bf16[4,16,16,256]{3,2,1,0:T(8,128)(2,1)S(1)}, u32[]{:S(2)}, u32[]{:S(2)}) collective-permute-start(bf16[4,16,16,256]{3,2,1,0:T(8,128)(2,1)} %param.9), channel_id=1, source_target_pairs={{0,96},{1,97},{2,98},{3,99},{4,100},{5,101},{6,102},{7,103},{8,40}... | collective-permute-start | bytes 1572872 | tf_op jit(solution)/shard_map/ppermute | solution.py:28
  5.8 0.0 collective-permute-start.1
  5.8 1.5 %collective-permute-start.5 = (bf16[512,1024]{1,0:T(8,128)(2,1)}, bf16[512,1024]{1,0:T(8,128)(2,1)S(1)}, u32[]{:S(2)}, u32[]{:S(2)}) collective-permute-start(bf16[512,1024]{1,0:T(8,128)(2,1)} %s.1), channel_id=1, source_target_pairs={{0,1},{1,0},{2,3},{3,2},{4,5},{5,4},{6,7},{7,6},{8,9},{9,8},{10,11... | collective-permute-start | bytes 3145736 | tf_op jit(solution)/shard_map/ppermute | solution.py:28
  7.3 2.2 %collective-permute-start.3 = (bf16[512,1024]{1,0:T(8,128)(2,1)}, bf16[512,1024]{1,0:T(8,128)(2,1)S(1)}, u32[]{:S(2)}, u32[]{:S(2)}) collective-permute-start(bf16[512,1024]{1,0:T(8,128)(2,1)} %s.1), channel_id=1, source_target_pairs={{0,6},{1,7},{2,0},{3,1},{4,2},{5,3},{6,4},{7,5},{8,10},{9,11},{10,... | collective-permute-start | bytes 3145736 | tf_op jit(solution)/shard_map/ppermute | solution.py:28
  9.5 8.3 %collective-permute-done.2 = bf16[4,16,16,256]{3,2,1,0:T(8,128)(2,1)S(1)} collective-permute-done((bf16[4,16,16,256]{3,2,1,0:T(8,128)(2,1)}, bf16[4,16,16,256]{3,2,1,0:T(8,128)(2,1)S(1)}, u32[]{:S(2)}, u32[]{:S(2)}) %collective-permute-start.2) | collective-permute-done | bytes 524320 | tf_op jit(solution)/shard_map/ppermute | solution.py:28
  17.7 2.0 %collective-permute-done.1 = bf16[4,16,16,256]{3,2,1,0:T(8,128)(2,1)S(1)} collective-permute-done((bf16[4,16,16,256]{3,2,1,0:T(8,128)(2,1)}, bf16[4,16,16,256]{3,2,1,0:T(8,128)(2,1)S(1)}, u32[]{:S(2)}, u32[]{:S(2)}) %collective-permute-start.1) | collective-permute-done | bytes 524320 | tf_op jit(solution)/shard_map/ppermute | solution.py:28
  19.8 3.5 %collective-permute-done.p1 = bf16[512,1024]{1,0:T(8,128)(2,1)S(1)} collective-permute-done((bf16[512,1024]{1,0:T(8,128)(2,1)}, bf16[512,1024]{1,0:T(8,128)(2,1)S(1)}, u32[]{:S(2)}, u32[]{:S(2)}) %collective-permute-start) | collective-permute-done | bytes 1048608 | tf_op jit(solution)/shard_map/ppermute | solution.py:28
  23.3 2.2 %collective-permute-start.4 = (bf16[512,1024]{1,0:T(8,128)(2,1)S(1)}, bf16[512,1024]{1,0:T(8,128)(2,1)S(1)}, u32[]{:S(2)}, u32[]{:S(2)}) collective-permute-start(bf16[512,1024]{1,0:T(8,128)(2,1)S(1)} %collective-permute-done.p1), channel_id=1, source_target_pairs={{0,2},{1,3},{2,4},{3,5},{4,6},{5,7},{6,0},{7,1},{8,14},{9,15},{10,... | collective-permute-start | bytes 3145736 | tf_op jit(solution)/shard_map/ppermute | solution.py:28
  25.5 3.3 %collective-permute-start.6 = (bf16[4,16,16,256]{3,2,1,0:T(8,128)(2,1)}, bf16[4,16,16,256]{3,2,1,0:T(8,128)(2,1)}, u32[]{:S(2)}, u32[]{:S(2)}) collective-permute-start(bf16[4,16,16,256]{3,2,1,0:T(8,128)(2,1)} %param.9), channel_id=1, source_target_pairs={{0,16},{1,17},{2,18},{3,19},{4,20},{5,21},{6,22},{7,23},{8,24},{9,... | collective-permute-start | bytes 1572872 | tf_op jit(solution)/shard_map/ppermute | solution.py:28
  28.8 2.9 %collective-permute-start.7 = (bf16[4,16,16,256]{3,2,1,0:T(8,128)(2,1)S(1)}, bf16[4,16,16,256]{3,2,1,0:T(8,128)(2,1)S(1)}, u32[]{:S(2)}, u32[]{:S(2)}) collective-permute-start(bf16[4,16,16,256]{3,2,1,0:T(8,128)(2,1)S(1)} %collective-permute-done.1), channel_id=1, source_target_pairs={{0,32},{1,33},{2,34},{3,35},{4,36},{5,37},{6,38},{7,39},{8,104},{9... | collective-permute-start | bytes 1572872 | tf_op jit(solution)/shard_map/ppermute | solution.py:28
  31.8 0.0 collective-permute-done.5.sw
  31.8 1.1 %slice.16 = bf16[512,768]{1,0:T(8,128)(2,1)} slice(bf16[512,1024]{1,0:T(8,128)(2,1)S(1)} %collective-permute-done.5.sw), slice={[0:512], [0:768]} | slice | bytes 1572864 | tf_op jit(solution)/shard_map/slice | solution.py:165
  32.9 12.3 %collective-permute-done.6.lh = bf16[4,16,16,256]{3,2,1,0:T(8,128)(2,1)} collective-permute-done((bf16[4,16,16,256]{3,2,1,0:T(8,128)(2,1)}, bf16[4,16,16,256]{3,2,1,0:T(8,128)(2,1)}, u32[]{:S(2)}, u32[]{:S(2)}) %collective-permute-start.6) | collective-permute-done | bytes 524320 | tf_op jit(solution)/shard_map/ppermute | solution.py:28
  45.2 0.0 collective-permute-done.3.p2
  45.2 0.0 collective-permute-done.7
  45.2 0.0 collective-permute-done.4.p3
  45.3 2.6 %collective-permute-start.12 = (bf16[4,16,16,256]{3,2,1,0:T(8,128)(2,1)}, bf16[4,16,16,256]{3,2,1,0:T(8,128)(2,1)S(1)}, u32[]{:S(2)}, u32[]{:S(2)}) collective-permute-start(bf16[4,16,16,256]{3,2,1,0:T(8,128)(2,1)} %collective-permute-done.6.lh), channel_id=1, source_target_pairs={{0,96},{1,97},{2,98},{3,99},{4,100},{5,101},{6,102},{7,103},{8,40}... | collective-permute-start | bytes 1572872 | tf_op jit(solution)/shard_map/ppermute | solution.py:28
  47.9 0.0 collective-permute-start.11
  47.9 0.1 slice_bitcast_fusion
  47.9 1.0 pad_maximum_fusion.3
  48.9 0.2 collective-permute-start.10
  49.1 1.7 %collective-permute-start.9 = (bf16[512,768]{1,0:T(8,128)(2,1)}, bf16[512,768]{1,0:T(8,128)(2,1)}, u32[]{:S(2)}, u32[]{:S(2)}) collective-permute-start(bf16[512,768]{1,0:T(8,128)(2,1)} %slice.16), channel_id=1, source_target_pairs={{0,6},{1,7},{2,0},{3,1},{4,2},{5,3},{6,4},{7,5},{8,10},{9,11},{10,... | collective-permute-start | bytes 2359304 | tf_op jit(solution)/shard_map/ppermute | solution.py:28
  50.8 0.3 collective-permute-start.8
  51.2 0.1 constant_dynamic-slice_fusion
  51.2 8.9 %collective-permute-done.12.r2 = bf16[4,16,16,256]{3,2,1,0:T(8,128)(2,1)S(1)} collective-permute-done((bf16[4,16,16,256]{3,2,1,0:T(8,128)(2,1)}, bf16[4,16,16,256]{3,2,1,0:T(8,128)(2,1)S(1)}, u32[]{:S(2)}, u32[]{:S(2)}) %collective-permute-start.12) | collective-permute-done | bytes 524320 | tf_op jit(solution)/shard_map/ppermute | solution.py:28
  60.1 0.0 collective-permute-start.15
  60.1 0.7 collective-permute-done.11.r1
  60.9 0.0 collective-permute-start.18
  60.9 0.1 copy-done.4
  60.9 1.3 %pad_maximum_fusion.1.x1 = bf16[2,4,16,16,256]{4,3,2,1,0:T(8,128)(2,1)S(1)} fusion(bf16[1,4,16,16,256]{4,3,2,1,0:T(8,128)(2,1)} %bitcast.17, bf16[1,4,16,16,256]{4,3,2,1,0:T(8,128)(2,1)} %bitcast.15), kind=kLoop, calls=%fused_computation.1 | loop fusion | flops 524288 | bytes 2097152 | tf_op jit(solution)/shard_map/stack | solution.py:181
  62.3 1.7 %pad_maximum_fusion.x0 = bf16[2,4,16,16,256]{4,3,2,1,0:T(8,128)(2,1)S(1)} fusion(bf16[1,4,16,16,256]{4,3,2,1,0:T(8,128)(2,1)} %bitcast.16, bf16[1,4,16,16,256]{4,3,2,1,0:T(8,128)(2,1)} %bitcast.14), kind=kLoop, calls=%fused_computation | loop fusion | flops 524288 | bytes 2097152 | tf_op jit(solution)/shard_map/stack | solution.py:180
  64.0 2.7 %pad_maximum_fusion.2 = bf16[2,4,16,16,256]{4,3,2,1,0:T(8,128)(2,1)} fusion(bf16[1,4,16,16,256]{4,3,2,1,0:T(8,128)(2,1)} %bitcast.13, bf16[1,4,16,16,256]{4,3,2,1,0:T(8,128)(2,1)} %bitcast.8), kind=kLoop, calls=%fused_computation.2 | loop fusion | flops 524288 | bytes 2097152 | tf_op jit(solution)/shard_map/stack | solution.py:185
  66.7 2.3 %collective-permute-done.10.far = bf16[3,512,256]{2,1,0:T(8,128)(2,1)} collective-permute-done((bf16[3,512,256]{2,1,0:T(8,128)(2,1)}, bf16[3,512,256]{2,1,0:T(8,128)(2,1)}, u32[]{:S(2)}, u32[]{:S(2)}) %collective-permute-start.10) | collective-permute-done | bytes 786464 | tf_op jit(solution)/shard_map/ppermute | solution.py:28
  69.0 0.7 collective-permute-start.16
  69.7 0.0 collective-permute-done.9.a2
  69.7 0.1 collective-permute-start.13
  69.8 0.5 collective-permute-done.8.a1
  70.3 0.0 collective-permute-start.14
  70.3 0.1 copy.13
  70.4 0.2 select_reduce_fusion
  70.6 0.0 collective-permute-done.15.t0
  70.6 0.1 collective-permute-start.17
  70.8 0.8 collective-permute-done.18.r3
  71.6 1.6 %collective-permute-start.19 = (bf16[4,16,16,256]{3,2,1,0:T(8,128)(2,1)}, bf16[4,16,16,256]{3,2,1,0:T(8,128)(2,1)}, u32[]{:S(2)}, u32[]{:S(2)}) collective-permute-start(bf16[4,16,16,256]{3,2,1,0:T(8,128)(2,1)} %collective-permute-done.18.r3), channel_id=1, source_target_pairs={{0,8},{1,9},{2,10},{3,11},{4,12},{5,13},{6,14},{7,15},{8,0},{9,1},... | collective-permute-start | bytes 1572872 | tf_op jit(solution)/shard_map/ppermute | solution.py:28
  73.2 0.2 select_reduce_fusion.1
  73.4 0.1 copy.14
  73.5 3.5 %shard_map.95.sv_in = bf16[32,512,256]{2,1,0:T(8,128)(2,1)S(1)} custom-call(bf16[512,1024]{1,0:T(8,128)(2,1)} %s.1, bf16[512,1024]{1,0:T(8,128)(2,1)} %copy-done.5, bf16[512,1024]{1,0:T(8,128)(2,1)} %copy-done.6, bf16[512,1024]{1,0:T(8,128)(2,1)} %copy-done.7, bf16[512,1024]{1,0:T(8,128)(2,1)} %copy-done.3, bf16[512,768]{1,0:T(8,128)(2,1)} %collective-permute-done.8.a1, ...), custom_call_target="tpu_custom_call" | custom-call | tf_op jit(solution)/shard_map/pallas_call | solution.py:200
  77.1 0.0 collective-permute-done.16.t2
  77.1 0.0 collective-permute-done.13.tx0
  77.1 0.0 collective-permute-done.14.tx1
  77.1 3.7 %shard_map.96.lv_in = bf16[4,16,256,256]{3,2,1,0:T(8,128)(2,1)S(1)} custom-call(s32[16]{0:T(128)S(1)} %fusion.13.place_ref, bf16[2,4,16,16,256]{4,3,2,1,0:T(8,128)(2,1)} %copy-done.2, bf16[2,4,16,16,256]{4,3,2,1,0:T(8,128)(2,1)} %copy-done.1, bf16[4,16,16,256]{3,2,1,0:T(8,128)(2,1)} %collective-permute-done.6.lh, ...), custom_call_target="tpu_custom_call" | custom-call | tf_op jit(solution)/shard_map/pallas_call | solution.py:209
  80.8 0.0 collective-permute-done.19.t3
  80.9 3.3 %collective-permute-done.17.a3 = bf16[512,768]{1,0:T(8,128)(2,1)} collective-permute-done((bf16[512,768]{1,0:T(8,128)(2,1)}, bf16[512,768]{1,0:T(8,128)(2,1)}, u32[]{:S(2)}, u32[]{:S(2)}) %collective-permute-start.17) | collective-permute-done | bytes 786464 | tf_op jit(solution)/shard_map/ppermute | solution.py:28
  84.2 7.6 %shard_map.97 = (bf16[512,1024]{1,0:T(8,128)(2,1)}, f32[8,4,16,256]{3,2,1,0:T(8,128)S(1)}, bf16[8,4,16,256]{3,2,1,0:T(8,128)(2,1)S(1)}, bf16[32,512,256]{2,1,0:T(8,128)(2,1)S(1)}, bf16[4,16,256,256]{3,2,1,0:T(8,128)(2,1)S(1)}) custom-call(s32[4,16]{1,0:T(4,128)S(1)} %select_select_fusion.slot_ref, ...), custom_call_target="tpu_custom_call", output_to_operand_aliasing={{3}: (4, {}), {4}: (5, {})} | custom-call | tf_op jit(solution)/shard_map/pallas_call | solution.py:218
  91.8 0.1 collective-permute-start.20
  91.9 1.5 %collective-permute-done.20 = bf16[8,4,16,256]{3,2,1,0:T(8,128)(2,1)S(1)} collective-permute-done((bf16[8,4,16,256]{3,2,1,0:T(8,128)(2,1)S(1)}, bf16[8,4,16,256]{3,2,1,0:T(8,128)(2,1)S(1)}, u32[]{:S(2)}, u32[]{:S(2)}) %collective-permute-start.20) | collective-permute-done | bytes 262176 | tf_op jit(solution)/shard_map/ppermute | solution.py:28
  93.4 0.1 add_convert_fusion
  93.5 12.0 %all_to_all.5 = bf16[8,4,16,256]{3,2,1,0:T(8,128)(2,1)S(1)} all-to-all(bf16[8,4,16,256]{3,2,1,0:T(8,128)(2,1)S(1)} %add_convert_fusion), channel_id=1, replica_groups={{0,16,32,48,64,80,96,112},{8,24,40,56,72,88,104,120},{1,17,33,49,65,81,..., dimensions={0} | all-to-all | bytes 524288 | tf_op jit(solution)/shard_map/all_to_all | solution.py:239
  105.5 0.6 sub.44
  (34 shorter events, 0.2 us)
Async XLA Ops:
  0.6 50.5 %copy-start = (s32[32,16]{0,1:T(8,128)S(1)}, s32[32,16]{0,1:T(8,128)}, u32[]{:S(2)}) copy-start(s32[32,16]{0,1:T(8,128)} %param.10) | copy-start | bytes 6148
  0.6 70.1 %copy-start.13 = (s32[16]{0:T(128)S(1)}, s32[16]{0:T(128)}, u32[]{:S(2)}) copy-start(s32[16]{0:T(128)} %constant.153.clone) | copy-start | bytes 196
  0.7 70.1 %copy-start.14 = (s32[16]{0:T(128)S(1)}, s32[16]{0:T(128)}, u32[]{:S(2)}) copy-start(s32[16]{0:T(128)} %constant.152.clone) | copy-start | bytes 196
  0.7 70.1 %copy-start.15 = (s32[16]{0:T(128)S(1)}, s32[16]{0:T(128)}, u32[]{:S(2)}) copy-start(s32[16]{0:T(128)} %constant.151.clone) | copy-start | bytes 196
  0.7 69.7 %copy-start.12 = (s32[32]{0:T(128)S(1)}, s32[32]{0:T(128)}, u32[]{:S(2)}) copy-start(s32[32]{0:T(128)} %param.11) | copy-start | bytes 388
  0.7 22.6 %collective-permute-start = (bf16[512,1024]{1,0:T(8,128)(2,1)}, bf16[512,1024]{1,0:T(8,128)(2,1)S(1)}, u32[]{:S(2)}, u32[]{:S(2)}) collective-permute-start(bf16[512,1024]{1,0:T(8,128)(2,1)} %s.1), channel_id=1, source_target_pairs={{0,2},{1,3},{2,4},{3,5},{4,6},{5,7},{6,0},{7,1},{8,14},{9,15},{10,... | collective-permute-start | bytes 3145736 | tf_op jit(solution)/shard_map/ppermute | solution.py:28
  2.8 15.0 %collective-permute-start.2 = (bf16[4,16,16,256]{3,2,1,0:T(8,128)(2,1)}, bf16[4,16,16,256]{3,2,1,0:T(8,128)(2,1)S(1)}, u32[]{:S(2)}, u32[]{:S(2)}) collective-permute-start(bf16[4,16,16,256]{3,2,1,0:T(8,128)(2,1)} %param.9), channel_id=1, source_target_pairs={{0,96},{1,97},{2,98},{3,99},{4,100},{5,101},{6,102},{7,103},{8,40}... | collective-permute-start | bytes 1572872 | tf_op jit(solution)/shard_map/ppermute | solution.py:28
  5.8 14.0 %collective-permute-start.1 = (bf16[4,16,16,256]{3,2,1,0:T(8,128)(2,1)}, bf16[4,16,16,256]{3,2,1,0:T(8,128)(2,1)S(1)}, u32[]{:S(2)}, u32[]{:S(2)}) collective-permute-start(bf16[4,16,16,256]{3,2,1,0:T(8,128)(2,1)} %param.9), channel_id=1, source_target_pairs={{0,32},{1,33},{2,34},{3,35},{4,36},{5,37},{6,38},{7,39},{8,104},{9... | collective-permute-start | bytes 1572872 | tf_op jit(solution)/shard_map/ppermute | solution.py:28
  5.8 26.0 %collective-permute-start.5 = (bf16[512,1024]{1,0:T(8,128)(2,1)}, bf16[512,1024]{1,0:T(8,128)(2,1)S(1)}, u32[]{:S(2)}, u32[]{:S(2)}) collective-permute-start(bf16[512,1024]{1,0:T(8,128)(2,1)} %s.1), channel_id=1, source_target_pairs={{0,1},{1,0},{2,3},{3,2},{4,5},{5,4},{6,7},{7,6},{8,9},{9,8},{10,11... | collective-permute-start | bytes 3145736 | tf_op jit(solution)/shard_map/ppermute | solution.py:28
  7.3 37.9 %collective-permute-start.3 = (bf16[512,1024]{1,0:T(8,128)(2,1)}, bf16[512,1024]{1,0:T(8,128)(2,1)S(1)}, u32[]{:S(2)}, u32[]{:S(2)}) collective-permute-start(bf16[512,1024]{1,0:T(8,128)(2,1)} %s.1), channel_id=1, source_target_pairs={{0,6},{1,7},{2,0},{3,1},{4,2},{5,3},{6,4},{7,5},{8,10},{9,11},{10,... | collective-permute-start | bytes 3145736 | tf_op jit(solution)/shard_map/ppermute | solution.py:28
  17.7 11.1 %copy-start.8 = (bf16[4,16,16,256]{3,2,1,0:T(8,128)(2,1)}, bf16[4,16,16,256]{3,2,1,0:T(8,128)(2,1)S(1)}, u32[]{:S(2)}) copy-start(bf16[4,16,16,256]{3,2,1,0:T(8,128)(2,1)S(1)} %collective-permute-done.2) | copy-start | bytes 1572868
  19.7 29.2 %copy-start.9 = (bf16[4,16,16,256]{3,2,1,0:T(8,128)(2,1)}, bf16[4,16,16,256]{3,2,1,0:T(8,128)(2,1)S(1)}, u32[]{:S(2)}) copy-start(bf16[4,16,16,256]{3,2,1,0:T(8,128)(2,1)S(1)} %collective-permute-done.1) | copy-start | bytes 1572868
  23.3 22.0 %copy-start.5 = (bf16[512,1024]{1,0:T(8,128)(2,1)}, bf16[512,1024]{1,0:T(8,128)(2,1)S(1)}, u32[]{:S(2)}) copy-start(bf16[512,1024]{1,0:T(8,128)(2,1)S(1)} %collective-permute-done.p1) | copy-start | bytes 3145732
  23.3 22.0 %collective-permute-start.4 = (bf16[512,1024]{1,0:T(8,128)(2,1)S(1)}, bf16[512,1024]{1,0:T(8,128)(2,1)S(1)}, u32[]{:S(2)}, u32[]{:S(2)}) collective-permute-start(bf16[512,1024]{1,0:T(8,128)(2,1)S(1)} %collective-permute-done.p1), channel_id=1, source_target_pairs={{0,2},{1,3},{2,4},{3,5},{4,6},{5,7},{6,0},{7,1},{8,14},{9,15},{10,... | collective-permute-start | bytes 3145736 | tf_op jit(solution)/shard_map/ppermute | solution.py:28
  25.5 19.7 %collective-permute-start.6 = (bf16[4,16,16,256]{3,2,1,0:T(8,128)(2,1)}, bf16[4,16,16,256]{3,2,1,0:T(8,128)(2,1)}, u32[]{:S(2)}, u32[]{:S(2)}) collective-permute-start(bf16[4,16,16,256]{3,2,1,0:T(8,128)(2,1)} %param.9), channel_id=1, source_target_pairs={{0,16},{1,17},{2,18},{3,19},{4,20},{5,21},{6,22},{7,23},{8,24},{9,... | collective-permute-start | bytes 1572872 | tf_op jit(solution)/shard_map/ppermute | solution.py:28
  28.8 16.4 %collective-permute-start.7 = (bf16[4,16,16,256]{3,2,1,0:T(8,128)(2,1)S(1)}, bf16[4,16,16,256]{3,2,1,0:T(8,128)(2,1)S(1)}, u32[]{:S(2)}, u32[]{:S(2)}) collective-permute-start(bf16[4,16,16,256]{3,2,1,0:T(8,128)(2,1)S(1)} %collective-permute-done.1), channel_id=1, source_target_pairs={{0,32},{1,33},{2,34},{3,35},{4,36},{5,37},{6,38},{7,39},{8,104},{9... | collective-permute-start | bytes 1572872 | tf_op jit(solution)/shard_map/ppermute | solution.py:28
  31.8 41.7 %copy-start.3 = (bf16[512,1024]{1,0:T(8,128)(2,1)}, bf16[512,1024]{1,0:T(8,128)(2,1)S(1)}, u32[]{:S(2)}) copy-start(bf16[512,1024]{1,0:T(8,128)(2,1)S(1)} %collective-permute-done.5.sw) | copy-start | bytes 3145732
  45.2 17.0 %copy-start.6 = (bf16[512,1024]{1,0:T(8,128)(2,1)}, bf16[512,1024]{1,0:T(8,128)(2,1)S(1)}, u32[]{:S(2)}) copy-start(bf16[512,1024]{1,0:T(8,128)(2,1)S(1)} %collective-permute-done.3.p2) | copy-start | bytes 3145732
  45.2 3.9 %copy-start.10 = (bf16[4,16,16,256]{3,2,1,0:T(8,128)(2,1)}, bf16[4,16,16,256]{3,2,1,0:T(8,128)(2,1)S(1)}, u32[]{:S(2)}) copy-start(bf16[4,16,16,256]{3,2,1,0:T(8,128)(2,1)S(1)} %collective-permute-done.7) | copy-start | bytes 1572868
  45.3 2.6 %copy-start.7 = (bf16[512,1024]{1,0:T(8,128)(2,1)}, bf16[512,1024]{1,0:T(8,128)(2,1)S(1)}, u32[]{:S(2)}) copy-start(bf16[512,1024]{1,0:T(8,128)(2,1)S(1)} %collective-permute-done.4.p3) | copy-start | bytes 3145732
  45.3 14.9 %collective-permute-start.12 = (bf16[4,16,16,256]{3,2,1,0:T(8,128)(2,1)}, bf16[4,16,16,256]{3,2,1,0:T(8,128)(2,1)S(1)}, u32[]{:S(2)}, u32[]{:S(2)}) collective-permute-start(bf16[4,16,16,256]{3,2,1,0:T(8,128)(2,1)} %collective-permute-done.6.lh), channel_id=1, source_target_pairs={{0,96},{1,97},{2,98},{3,99},{4,100},{5,101},{6,102},{7,103},{8,40}... | collective-permute-start | bytes 1572872 | tf_op jit(solution)/shard_map/ppermute | solution.py:28
  47.9 13.0 %collective-permute-start.11 = (bf16[4,16,16,256]{3,2,1,0:T(8,128)(2,1)}, bf16[4,16,16,256]{3,2,1,0:T(8,128)(2,1)}, u32[]{:S(2)}, u32[]{:S(2)}) collective-permute-start(bf16[4,16,16,256]{3,2,1,0:T(8,128)(2,1)} %collective-permute-done.6.lh), channel_id=1, source_target_pairs={{0,32},{1,33},{2,34},{3,35},{4,36},{5,37},{6,38},{7,39},{8,104},{9... | collective-permute-start | bytes 1572872 | tf_op jit(solution)/shard_map/ppermute | solution.py:28
  48.9 20.1 %collective-permute-start.10 = (bf16[3,512,256]{2,1,0:T(8,128)(2,1)}, bf16[3,512,256]{2,1,0:T(8,128)(2,1)}, u32[]{:S(2)}, u32[]{:S(2)}) collective-permute-start(bf16[3,512,256]{2,1,0:T(8,128)(2,1)} %pad_maximum_fusion.3), channel_id=1, source_target_pairs={{0,1},{1,0},{2,3},{3,2},{4,5},{5,4},{6,7},{7,6},{8,9},{9,8},{10,11... | collective-permute-start | bytes 2359304 | tf_op jit(solution)/shard_map/ppermute | solution.py:28
  49.1 20.5 %collective-permute-start.9 = (bf16[512,768]{1,0:T(8,128)(2,1)}, bf16[512,768]{1,0:T(8,128)(2,1)}, u32[]{:S(2)}, u32[]{:S(2)}) collective-permute-start(bf16[512,768]{1,0:T(8,128)(2,1)} %slice.16), channel_id=1, source_target_pairs={{0,6},{1,7},{2,0},{3,1},{4,2},{5,3},{6,4},{7,5},{8,10},{9,11},{10,... | collective-permute-start | bytes 2359304 | tf_op jit(solution)/shard_map/ppermute | solution.py:28
  50.8 19.5 %collective-permute-start.8 = (bf16[512,768]{1,0:T(8,128)(2,1)}, bf16[512,768]{1,0:T(8,128)(2,1)}, u32[]{:S(2)}, u32[]{:S(2)}) collective-permute-start(bf16[512,768]{1,0:T(8,128)(2,1)} %slice.16), channel_id=1, source_target_pairs={{0,2},{1,3},{2,4},{3,5},{4,6},{5,7},{6,0},{7,1},{8,14},{9,15},{10,... | collective-permute-start | bytes 2359304 | tf_op jit(solution)/shard_map/ppermute | solution.py:28
  60.1 0.8 copy-start.4
  60.1 10.5 %collective-permute-start.15 = (bf16[4,16,16,256]{3,2,1,0:T(8,128)(2,1)}, bf16[4,16,16,256]{3,2,1,0:T(8,128)(2,1)}, u32[]{:S(2)}, u32[]{:S(2)}) collective-permute-start(bf16[4,16,16,256]{3,2,1,0:T(8,128)(2,1)} %collective-permute-done.6.lh), channel_id=1, source_target_pairs={{0,8},{1,9},{2,10},{3,11},{4,12},{5,13},{6,14},{7,15},{8,0},{9,1},... | collective-permute-start | bytes 1572872 | tf_op jit(solution)/shard_map/ppermute | solution.py:28
  60.9 10.7 %collective-permute-start.18 = (bf16[4,16,16,256]{3,2,1,0:T(8,128)(2,1)}, bf16[4,16,16,256]{3,2,1,0:T(8,128)(2,1)}, u32[]{:S(2)}, u32[]{:S(2)}) collective-permute-start(bf16[4,16,16,256]{3,2,1,0:T(8,128)(2,1)} %collective-permute-done.11.r1), channel_id=1, source_target_pairs={{0,32},{1,33},{2,34},{3,35},{4,36},{5,37},{6,38},{7,39},{8,104},{9... | collective-permute-start | bytes 1572872 | tf_op jit(solution)/shard_map/ppermute | solution.py:28
  62.2 14.8 %copy-start.1 = (bf16[2,4,16,16,256]{4,3,2,1,0:T(8,128)(2,1)}, bf16[2,4,16,16,256]{4,3,2,1,0:T(8,128)(2,1)S(1)}, u32[]{:S(2)}) copy-start(bf16[2,4,16,16,256]{4,3,2,1,0:T(8,128)(2,1)S(1)} %pad_maximum_fusion.1.x1) | copy-start | bytes 3145732
  63.9 13.1 %copy-start.2 = (bf16[2,4,16,16,256]{4,3,2,1,0:T(8,128)(2,1)}, bf16[2,4,16,16,256]{4,3,2,1,0:T(8,128)(2,1)S(1)}, u32[]{:S(2)}) copy-start(bf16[2,4,16,16,256]{4,3,2,1,0:T(8,128)(2,1)S(1)} %pad_maximum_fusion.x0) | copy-start | bytes 3145732
  69.0 8.1 %collective-permute-start.16 = (bf16[2,4,16,16,256]{4,3,2,1,0:T(8,128)(2,1)}, bf16[2,4,16,16,256]{4,3,2,1,0:T(8,128)(2,1)}, u32[]{:S(2)}, u32[]{:S(2)}) collective-permute-start(bf16[2,4,16,16,256]{4,3,2,1,0:T(8,128)(2,1)} %pad_maximum_fusion.2), channel_id=1, source_target_pairs={{0,8},{1,9},{2,10},{3,11},{4,12},{5,13},{6,14},{7,15},{8,0},{9,1},... | collective-permute-start | bytes 3145736 | tf_op jit(solution)/shard_map/ppermute | solution.py:28
  69.7 7.4 %collective-permute-start.13 = (bf16[2,4,16,16,256]{4,3,2,1,0:T(8,128)(2,1)S(1)}, bf16[2,4,16,16,256]{4,3,2,1,0:T(8,128)(2,1)}, u32[]{:S(2)}, u32[]{:S(2)}) collective-permute-start(bf16[2,4,16,16,256]{4,3,2,1,0:T(8,128)(2,1)S(1)} %pad_maximum_fusion.x0), channel_id=1, source_target_pairs={{0,8},{1,9},{2,10},{3,11},{4,12},{5,13},{6,14},{7,15},{8,0},{9,1},... | collective-permute-start | bytes 3145736 | tf_op jit(solution)/shard_map/ppermute | solution.py:28
  70.3 6.8 %collective-permute-start.14 = (bf16[2,4,16,16,256]{4,3,2,1,0:T(8,128)(2,1)S(1)}, bf16[2,4,16,16,256]{4,3,2,1,0:T(8,128)(2,1)}, u32[]{:S(2)}, u32[]{:S(2)}) collective-permute-start(bf16[2,4,16,16,256]{4,3,2,1,0:T(8,128)(2,1)S(1)} %pad_maximum_fusion.1.x1), channel_id=1, source_target_pairs={{0,8},{1,9},{2,10},{3,11},{4,12},{5,13},{6,14},{7,15},{8,0},{9,1},... | collective-permute-start | bytes 3145736 | tf_op jit(solution)/shard_map/ppermute | solution.py:28
  70.6 13.6 %collective-permute-start.17 = (bf16[512,768]{1,0:T(8,128)(2,1)}, bf16[512,768]{1,0:T(8,128)(2,1)}, u32[]{:S(2)}, u32[]{:S(2)}) collective-permute-start(bf16[512,768]{1,0:T(8,128)(2,1)} %collective-permute-done.8.a1), channel_id=1, source_target_pairs={{0,2},{1,3},{2,4},{3,5},{4,6},{5,7},{6,0},{7,1},{8,14},{9,15},{10,... | collective-permute-start | bytes 2359304 | tf_op jit(solution)/shard_map/ppermute | solution.py:28
  71.6 9.3 %collective-permute-start.19 = (bf16[4,16,16,256]{3,2,1,0:T(8,128)(2,1)}, bf16[4,16,16,256]{3,2,1,0:T(8,128)(2,1)}, u32[]{:S(2)}, u32[]{:S(2)}) collective-permute-start(bf16[4,16,16,256]{3,2,1,0:T(8,128)(2,1)} %collective-permute-done.18.r3), channel_id=1, source_target_pairs={{0,8},{1,9},{2,10},{3,11},{4,12},{5,13},{6,14},{7,15},{8,0},{9,1},... | collective-permute-start | bytes 1572872 | tf_op jit(solution)/shard_map/ppermute | solution.py:28
  84.2 21.3 %copy-start.11 = (f32[4,16,256]{2,1,0:T(8,128)S(1)}, f32[4,16,256]{2,1,0:T(8,128)}, u32[]{:S(2)}) copy-start(f32[4,16,256]{2,1,0:T(8,128)} %param.12) | copy-start | bytes 196612
  91.8 1.6 %collective-permute-start.20 = (bf16[8,4,16,256]{3,2,1,0:T(8,128)(2,1)S(1)}, bf16[8,4,16,256]{3,2,1,0:T(8,128)(2,1)S(1)}, u32[]{:S(2)}, u32[]{:S(2)}) collective-permute-start(bf16[8,4,16,256]{3,2,1,0:T(8,128)(2,1)S(1)} %get-tuple-element.37), channel_id=1, source_target_pairs={{0,8},{1,9},{2,10},{3,11},{4,12},{5,13},{6,14},{7,15},{8,0},{9,1},... | collective-permute-start | bytes 786440 | tf_op jit(solution)/shard_map/ppermute | solution.py:28

commit v4 on v3

--- a/solution.py
+++ b/solution.py
@@ -9,9 +9,9 @@
 NR = 16
 SUP = 4
 NA = 32
+EARLY = 13
 ROWS = 2 * B
-VMEM_LIMIT = 4 * 1024 * 1024
-FINAL_LIMIT = 16 * 1024 * 1024
+VMEM_LIMIT = 16 * 1024 * 1024
 AXES = ("prow", "pcol")
 
 
@@ -89,8 +89,7 @@
         parts += columns(src, 4)
     for i, src in enumerate((a1, a2)):
         parts += columns(src, 3) + [far.at[i]]
-    parts.append(far.at[2])
-    start_wait(slot_copies(parts, sv, sem))
+    start_wait(slot_copies(parts + [far.at[2]], sv, sem))
 
 
 def row_copies(parts, first, place_ref, lv, sem):
@@ -107,29 +106,44 @@
     start_wait(row_copies(parts, 0, place_ref, lv, sem))
 
 
-def final_kernel(slot_ref, own_ref, place_ref, core_ref, sv_in, lv_in, a3, r3, t3, off_out, keep_out, send_out, sv, lv,
-                 acc, s_sem, l_sem):
-    loads = slot_copies(columns(a3, 3), sv.at[pl.ds(29, 3)], s_sem)
-    loads += row_copies([r3, t3], 14, place_ref, lv, l_sem)
-    start_wait(loads)
+def product(slot_ref, block_ref, k, first, count, sv, lv):
+    left = jnp.concatenate([sv[slot_ref[k, i]] for i in range(first, first + count)], axis=1)
+    right = jnp.concatenate([lv[k, block_ref[k, i]] for i in range(first, first + count)], axis=0)
+    return jnp.dot(left, right, preferred_element_type=jnp.float32)
+
+
+def main_kernel(slot_ref, block_ref, place_ref, sv, lv_in, r3, t3, lv, acc, sem):
+    start_wait(row_copies([r3, t3], 14, place_ref, lv, sem))
     for k in range(SUP):
-        left = jnp.concatenate([sv[slot_ref[k, i]] for i in range(NR)], axis=1)
-        acc[k] = jnp.dot(left, lv[k].reshape(NR * B, B), preferred_element_type=jnp.float32)
+        acc[k] = product(slot_ref, block_ref, k, 0, EARLY, sv, lv)
+
+
+def late_kernel(slot_ref, block_ref, own_ref, core_ref, sv_in, lv, acc_in, a3, off_out, keep_out, send_out, sv,
+                acc, off_ref, sem):
+    for j in range(3):
+        sv[29 + j] = a3[:, j * B:(j + 1) * B]
+    stores = []
     core = core_ref[0]
+    for k in range(SUP):
+        acc[k] = acc_in[k] + product(slot_ref, block_ref, k, EARLY, NR - EARLY, sv, lv)
     for k in range(SUP):
         offs, owns = [], []
         for t in range(2):
             c = own_ref[k, t]
             alive = (c >= 0).astype(jnp.float32)
             off = (acc[k, pl.ds(t * B, B)] * -alive).astype(jnp.bfloat16)
-            off_out[pl.ds(t * B, B), pl.ds(k * B, B)] = off
+            off_ref[k, pl.ds(t * B, B)] = off
             offs.append(off)
             owns.append(lv[k, jnp.maximum(c, 0)])
+        stores.append(pltpu.make_async_copy(off_ref.at[k], off_out.at[:, pl.ds(k * B, B)], sem.at[k]))
+        stores[-1].start()
         total = lax.dot_general(jnp.concatenate(owns, axis=0), jnp.concatenate(offs, axis=0),
                                 (((0,), (0,)), ((), ())), preferred_element_type=jnp.float32)
         part = (0.5 * (total + total.T)).reshape(8, 2, 16, B)
         keep_out[:, k] = jnp.where(core == 0, part[:, 0], part[:, 1])
         send_out[:, k] = jnp.where(core == 0, part[:, 1], part[:, 0]).astype(jnp.bfloat16)
+    for store in stores:
+        store.wait()
 
 
 def per_device(sigma_anc, lower_blocks, row_blocks, slot_of, inv_diag):
@@ -148,6 +162,11 @@
     near = group * 4 + slots % 4
     far = jnp.where(group == 3, jnp.where(slots % 4 == 3, 28, 29 + slots % 4), 16 + group * 4 + slots % 4)
     pos = jnp.where(sc % 2 == w, near, far).astype(jnp.int32)
+    rank = jnp.sum((pos[:, None, :] < pos[:, :, None]).astype(jnp.int32), axis=2)
+    ranked = rank[:, :, None] == jnp.arange(NR, dtype=jnp.int32)
+    index = jnp.arange(NR, dtype=jnp.int32)[None, :, None]
+    sorted_slots = jnp.sum(jnp.where(ranked, pos[:, :, None], 0), axis=1)
+    sorted_blocks = jnp.sum(jnp.where(ranked, index, 0), axis=1)
     number = jnp.arange(1, NR + 1, dtype=jnp.int32)[None, :, None]
     ours = row * 2 + jnp.arange(2, dtype=jnp.int32)
     own = jnp.sum(jnp.where(slots[:, :, None] == ours, number, 0), axis=1) - 1
@@ -186,17 +205,19 @@
     a1, a2, far = tie(a1, a2, far)
     a3 = z_first(a1)
     t3 = swap_core(r3)
-    s, p1, p2, p3, sw, a1, a2, a3, far = in_hbm(s, p1, p2, p3, sw, a1, a2, a3, far)
-    lh, r1, r2, r3, x0, x1 = in_hbm(lh, r1, r2, r3, x0, x1)
-    t0, tx0, tx1, t2, t3 = in_hbm(t0, tx0, tx1, t2, t3)
+    s, p1, p2, p3, sw, a1, a2, far = in_hbm(s, p1, p2, p3, sw, a1, a2, far)
+    a3 = pltpu.with_memory_space_constraint(a3, pltpu.VMEM)
+    lh, r1, r2, x0, x1 = in_hbm(lh, r1, r2, x0, x1)
+    t0, tx0, tx1, t2 = in_hbm(t0, tx0, tx1, t2)
+    r3, t3 = [pltpu.with_memory_space_constraint(v, pltpu.VMEM) for v in (r3, t3)]
 
     hbm = pl.BlockSpec(memory_space=pltpu.HBM)
     smem = pl.BlockSpec(memory_space=pltpu.SMEM)
     vmem = pl.BlockSpec(memory_space=pltpu.VMEM)
     params = pltpu.CompilerParams(vmem_limit_bytes=VMEM_LIMIT)
-    final_params = pltpu.CompilerParams(vmem_limit_bytes=FINAL_LIMIT)
     panel_shape = pltpu.VMEM((SUP, NR, B, B), jnp.bfloat16)
     held_shape = pltpu.VMEM((NA, ROWS, B), jnp.bfloat16)
+    acc_shape = pltpu.VMEM((SUP, ROWS, B), jnp.float32)
     held = pl.pallas_call(
         hold_kernel,
         out_shape=held_shape,
@@ -205,7 +226,6 @@
         scratch_shapes=[pltpu.SemaphoreType.DMA((29,))],
         compiler_params=params,
     )(s, p1, p2, p3, sw, a1, a2, far)
-    held = pltpu.with_memory_space_constraint(held, pltpu.VMEM)
     blocks = pl.pallas_call(
         panel_kernel,
         out_shape=panel_shape,
@@ -214,26 +234,35 @@
         scratch_shapes=[pltpu.SemaphoreType.DMA((14,))],
         compiler_params=params,
     )(place, x0, x1, lh, r1, r2, tx0, tx1, t0, t2)
-    blocks = pltpu.with_memory_space_constraint(blocks, pltpu.VMEM)
-    sigma_off, keep, send, _, _ = pl.pallas_call(
-        final_kernel,
+    held, blocks = [pltpu.with_memory_space_constraint(v, pltpu.VMEM) for v in (held, blocks)]
+    blocks, acc = pl.pallas_call(
+        main_kernel,
+        out_shape=(panel_shape, acc_shape),
+        in_specs=[smem] * 3 + [vmem] * 4,
+        out_specs=(vmem, vmem),
+        input_output_aliases={4: 0},
+        scratch_shapes=[pltpu.SemaphoreType.DMA((2,))],
+        compiler_params=params,
+    )(sorted_slots, sorted_blocks, place, held, blocks, r3, t3)
+    blocks, acc = [pltpu.with_memory_space_constraint(v, pltpu.VMEM) for v in (blocks, acc)]
+    sigma_off, keep, send, _ = pl.pallas_call(
+        late_kernel,
         out_shape=(
             jax.ShapeDtypeStruct((ROWS, SUP * B), jnp.bfloat16),
             jax.ShapeDtypeStruct((8, SUP, 16, B), jnp.float32),
             jax.ShapeDtypeStruct((8, SUP, 16, B), jnp.bfloat16),
             held_shape,
-            panel_shape,
         ),
-        in_specs=[smem] * 4 + [vmem] * 2 + [hbm] * 3,
-        out_specs=(vmem,) * 5,
-        input_output_aliases={4: 3, 5: 4},
+        in_specs=[smem] * 4 + [vmem] * 4,
+        out_specs=(hbm,) + (vmem,) * 3,
+        input_output_aliases={4: 3},
         scratch_shapes=[
             pltpu.VMEM((SUP, ROWS, B), jnp.float32),
-            pltpu.SemaphoreType.DMA((3,)),
-            pltpu.SemaphoreType.DMA((2,)),
+            pltpu.VMEM((SUP, ROWS, B), jnp.bfloat16),
+            pltpu.SemaphoreType.DMA((SUP,)),
         ],
-        compiler_params=final_params,
-    )(pos, own, place, core.reshape(1).astype(jnp.int32), held, blocks, a3, r3, t3)
+        compiler_params=params,
+    )(sorted_slots, sorted_blocks, own, core.reshape(1).astype(jnp.int32), held, blocks, acc, a3)
 
     halves = (keep + swap_core(send).astype(jnp.float32)).astype(jnp.bfloat16)
     parts = lax.all_to_all(halves, "prow", split_axis=0, concat_axis=0, tiled=True,

time: 106 us -> 103 us (0.972)
  waiting for transfers between devices: 44.2 us -> 40.5 us
    ppermute x21, waiting for transfers between devices: 44.2 us -> 40.5 us  [permute(): return lax.ppermute(x, AXES, pairs)]
    another operation x1, other arithmetic: 1.3 us -> 0.1 us  [per_device(): x1 = jnp.stack([q2, q3])]
    pallas_call x1 -> x2, Pallas kernels: 7.56 us -> 7.05 us  [the longest x1 4.45 us: per_device(): pl.pallas_call(main_kernel, out_shape=(panel_shape, acc_shape), in_specs=...]
  transfers between devices with their start and end apart: 21 -> 21, of which waited for: 11 -> 10; matrix products, arithmetic and copies ran while one was open for 8% -> 8% of each run, Pallas kernels for 7% -> 11%
where the time goes in v4:
time: 103 us
  waiting for transfers between devices  40.5 us (39%)
  starting transfers between devices  24.9 us (24%)
  Pallas kernels  14.3 us (14%)
  blocking collectives  12.5 us (12%)
  other arithmetic  7.57 us (7%)
  local copies, waits for them, and re-layouts  2.38 us (2%)
    ppermute x21, waiting for transfers between devices, permute(): return lax.ppermute(x, AXES, pairs)  40.5 us
    ppermute x21, starting transfers between devices, permute(): return lax.ppermute(x, AXES, pairs)  24.9 us
    all_to_all x1, blocking collectives, per_device(): lax.all_to_all(halves, 'prow', split_axis=0, concat_axis=0, tiled=True, a...  12.5 us
    pallas_call x1, Pallas kernels, per_device(): pl.pallas_call(main_kernel, out_shape=(panel_shape, acc_shape), in_specs=...  4.45 us
    pallas_call x1, Pallas kernels, per_device(): pl.pallas_call(panel_kernel, out_shape=panel_shape, in_specs=[smem] + [hb...  3.75 us
    pallas_call x1, Pallas kernels, per_device(): pl.pallas_call(hold_kernel, out_shape=held_shape, in_specs=[hbm] * 8, out...  3.5 us
    pallas_call x1, Pallas kernels, per_device(): pl.pallas_call(late_kernel, out_shape=(jax.ShapeDtypeStruct((ROWS, SUP *...  2.6 us
    another operation x1, other arithmetic, per_device(): t2 = swap_core(jnp.stack([r1, r2]))  2.58 us
  transfers between devices with their start and end apart: 21, of which 10 were waited for; matrix products, arithmetic and copies ran while one was open for 8% of the time, Pallas kernels for 11%

profile of v4, /device:TPU:0, one launch (start us, length us, event | category | flops | bytes accessed | tf_op | source)
XLA Modules:
  0.0 103.0 jit_solution(8460827088618735802)
XLA Ops:
  0.6 0.0 copy-start
  0.6 0.0 copy-start.9
  0.7 0.0 copy-start.10
  0.7 0.0 copy-start.11
  0.7 2.1 %collective-permute-start = (bf16[512,1024]{1,0:T(8,128)(2,1)}, bf16[512,1024]{1,0:T(8,128)(2,1)S(1)}, u32[]{:S(2)}, u32[]{:S(2)}) collective-permute-start(bf16[512,1024]{1,0:T(8,128)(2,1)} %s.1), channel_id=1, source_target_pairs={{0,2},{1,3},{2,4},{3,5},{4,6},{5,7},{6,0},{7,1},{8,14},{9,15},{10,... | collective-permute-start | bytes 3145736 | tf_op jit(solution)/shard_map/ppermute | solution.py:28
  2.8 3.0 %collective-permute-start.2 = (bf16[4,16,16,256]{3,2,1,0:T(8,128)(2,1)}, bf16[4,16,16,256]{3,2,1,0:T(8,128)(2,1)S(1)}, u32[]{:S(2)}, u32[]{:S(2)}) collective-permute-start(bf16[4,16,16,256]{3,2,1,0:T(8,128)(2,1)} %param.9), channel_id=1, source_target_pairs={{0,96},{1,97},{2,98},{3,99},{4,100},{5,101},{6,102},{7,103},{8,40}... | collective-permute-start | bytes 1572872 | tf_op jit(solution)/shard_map/ppermute | solution.py:28
  5.8 0.0 collective-permute-start.1
  5.8 1.5 %collective-permute-start.5 = (bf16[512,1024]{1,0:T(8,128)(2,1)}, bf16[512,1024]{1,0:T(8,128)(2,1)S(1)}, u32[]{:S(2)}, u32[]{:S(2)}) collective-permute-start(bf16[512,1024]{1,0:T(8,128)(2,1)} %s.1), channel_id=1, source_target_pairs={{0,1},{1,0},{2,3},{3,2},{4,5},{5,4},{6,7},{7,6},{8,9},{9,8},{10,11... | collective-permute-start | bytes 3145736 | tf_op jit(solution)/shard_map/ppermute | solution.py:28
  7.3 2.2 %collective-permute-start.3 = (bf16[512,1024]{1,0:T(8,128)(2,1)}, bf16[512,1024]{1,0:T(8,128)(2,1)S(1)}, u32[]{:S(2)}, u32[]{:S(2)}) collective-permute-start(bf16[512,1024]{1,0:T(8,128)(2,1)} %s.1), channel_id=1, source_target_pairs={{0,6},{1,7},{2,0},{3,1},{4,2},{5,3},{6,4},{7,5},{8,10},{9,11},{10,... | collective-permute-start | bytes 3145736 | tf_op jit(solution)/shard_map/ppermute | solution.py:28
  9.5 8.3 %collective-permute-done.2 = bf16[4,16,16,256]{3,2,1,0:T(8,128)(2,1)S(1)} collective-permute-done((bf16[4,16,16,256]{3,2,1,0:T(8,128)(2,1)}, bf16[4,16,16,256]{3,2,1,0:T(8,128)(2,1)S(1)}, u32[]{:S(2)}, u32[]{:S(2)}) %collective-permute-start.2) | collective-permute-done | bytes 524320 | tf_op jit(solution)/shard_map/ppermute | solution.py:28
  17.7 2.1 %collective-permute-done.1 = bf16[4,16,16,256]{3,2,1,0:T(8,128)(2,1)} collective-permute-done((bf16[4,16,16,256]{3,2,1,0:T(8,128)(2,1)}, bf16[4,16,16,256]{3,2,1,0:T(8,128)(2,1)}, u32[]{:S(2)}, u32[]{:S(2)}) %collective-permute-start.1) | collective-permute-done | bytes 524320 | tf_op jit(solution)/shard_map/ppermute | solution.py:28
  19.8 3.4 %collective-permute-done.p1 = bf16[512,1024]{1,0:T(8,128)(2,1)S(1)} collective-permute-done((bf16[512,1024]{1,0:T(8,128)(2,1)}, bf16[512,1024]{1,0:T(8,128)(2,1)S(1)}, u32[]{:S(2)}, u32[]{:S(2)}) %collective-permute-start) | collective-permute-done | bytes 1048608 | tf_op jit(solution)/shard_map/ppermute | solution.py:28
  23.3 2.2 %collective-permute-start.4 = (bf16[512,1024]{1,0:T(8,128)(2,1)S(1)}, bf16[512,1024]{1,0:T(8,128)(2,1)S(1)}, u32[]{:S(2)}, u32[]{:S(2)}) collective-permute-start(bf16[512,1024]{1,0:T(8,128)(2,1)S(1)} %collective-permute-done.p1), channel_id=1, source_target_pairs={{0,2},{1,3},{2,4},{3,5},{4,6},{5,7},{6,0},{7,1},{8,14},{9,15},{10,... | collective-permute-start | bytes 3145736 | tf_op jit(solution)/shard_map/ppermute | solution.py:28
  25.5 3.3 %collective-permute-start.6 = (bf16[4,16,16,256]{3,2,1,0:T(8,128)(2,1)}, bf16[4,16,16,256]{3,2,1,0:T(8,128)(2,1)}, u32[]{:S(2)}, u32[]{:S(2)}) collective-permute-start(bf16[4,16,16,256]{3,2,1,0:T(8,128)(2,1)} %param.9), channel_id=1, source_target_pairs={{0,16},{1,17},{2,18},{3,19},{4,20},{5,21},{6,22},{7,23},{8,24},{9,... | collective-permute-start | bytes 1572872 | tf_op jit(solution)/shard_map/ppermute | solution.py:28
  28.8 2.9 %collective-permute-start.7 = (bf16[4,16,16,256]{3,2,1,0:T(8,128)(2,1)}, bf16[4,16,16,256]{3,2,1,0:T(8,128)(2,1)S(1)}, u32[]{:S(2)}, u32[]{:S(2)}) collective-permute-start(bf16[4,16,16,256]{3,2,1,0:T(8,128)(2,1)} %collective-permute-done.1), channel_id=1, source_target_pairs={{0,32},{1,33},{2,34},{3,35},{4,36},{5,37},{6,38},{7,39},{8,104},{9... | collective-permute-start | bytes 1572872 | tf_op jit(solution)/shard_map/ppermute | solution.py:28
  31.8 0.0 collective-permute-done.5.sw
  31.8 1.0 copy-done.3
  32.7 1.0 slice.16
  33.8 11.4 %collective-permute-done.6.lh = bf16[4,16,16,256]{3,2,1,0:T(8,128)(2,1)} collective-permute-done((bf16[4,16,16,256]{3,2,1,0:T(8,128)(2,1)}, bf16[4,16,16,256]{3,2,1,0:T(8,128)(2,1)}, u32[]{:S(2)}, u32[]{:S(2)}) %collective-permute-start.6) | collective-permute-done | bytes 524320 | tf_op jit(solution)/shard_map/ppermute | solution.py:28
  45.2 0.0 collective-permute-done.3.p2
  45.2 0.0 collective-permute-done.7
  45.2 0.0 collective-permute-done.4.p3
  45.2 2.6 %collective-permute-start.12 = (bf16[4,16,16,256]{3,2,1,0:T(8,128)(2,1)}, bf16[4,16,16,256]{3,2,1,0:T(8,128)(2,1)S(1)}, u32[]{:S(2)}, u32[]{:S(2)}) collective-permute-start(bf16[4,16,16,256]{3,2,1,0:T(8,128)(2,1)} %collective-permute-done.6.lh), channel_id=1, source_target_pairs={{0,96},{1,97},{2,98},{3,99},{4,100},{5,101},{6,102},{7,103},{8,40}... | collective-permute-start | bytes 1572872 | tf_op jit(solution)/shard_map/ppermute | solution.py:28
  47.8 0.1 slice_bitcast_fusion
  47.9 1.0 pad_maximum_fusion.3
  48.9 0.2 collective-permute-start.10
  49.1 1.7 %collective-permute-start.9 = (bf16[512,768]{1,0:T(8,128)(2,1)}, bf16[512,768]{1,0:T(8,128)(2,1)}, u32[]{:S(2)}, u32[]{:S(2)}) collective-permute-start(bf16[512,768]{1,0:T(8,128)(2,1)} %slice.16), channel_id=1, source_target_pairs={{0,6},{1,7},{2,0},{3,1},{4,2},{5,3},{6,4},{7,5},{8,10},{9,11},{10,... | collective-permute-start | bytes 2359304 | tf_op jit(solution)/shard_map/ppermute | solution.py:28
  50.8 0.3 collective-permute-start.8
  51.2 0.1 constant_dynamic-slice_fusion
  51.2 0.1 copy.13
  51.3 0.9 select_reduce_fusion.2
  52.2 7.9 %collective-permute-done.12.r2 = bf16[4,16,16,256]{3,2,1,0:T(8,128)(2,1)S(1)} collective-permute-done((bf16[4,16,16,256]{3,2,1,0:T(8,128)(2,1)}, bf16[4,16,16,256]{3,2,1,0:T(8,128)(2,1)S(1)}, u32[]{:S(2)}, u32[]{:S(2)}) %collective-permute-start.12) | collective-permute-done | bytes 524320 | tf_op jit(solution)/shard_map/ppermute | solution.py:28
  60.1 0.7 collective-permute-done.11.r1
  60.8 0.0 collective-permute-start.17
  60.8 0.1 pad_maximum_fusion.1.x1
  61.0 1.7 %pad_maximum_fusion.x0 = bf16[2,4,16,16,256]{4,3,2,1,0:T(8,128)(2,1)S(1)} fusion(bf16[1,4,16,16,256]{4,3,2,1,0:T(8,128)(2,1)} %bitcast.5, bf16[1,4,16,16,256]{4,3,2,1,0:T(8,128)(2,1)} %bitcast.14), kind=kLoop, calls=%fused_computation | loop fusion | flops 524288 | bytes 2097152 | tf_op jit(solution)/shard_map/stack | solution.py:199
  62.6 2.6 %pad_maximum_fusion.2 = bf16[2,4,16,16,256]{4,3,2,1,0:T(8,128)(2,1)} fusion(bf16[1,4,16,16,256]{4,3,2,1,0:T(8,128)(2,1)S(1)} %bitcast.13, bf16[1,4,16,16,256]{4,3,2,1,0:T(8,128)(2,1)} %bitcast.8), kind=kLoop, calls=%fused_computation.2 | loop fusion | flops 524288 | bytes 2097152 | tf_op jit(solution)/shard_map/stack | solution.py:204
  65.2 3.8 %collective-permute-done.10.far = bf16[3,512,256]{2,1,0:T(8,128)(2,1)} collective-permute-done((bf16[3,512,256]{2,1,0:T(8,128)(2,1)}, bf16[3,512,256]{2,1,0:T(8,128)(2,1)}, u32[]{:S(2)}, u32[]{:S(2)}) %collective-permute-start.10) | collective-permute-done | bytes 786464 | tf_op jit(solution)/shard_map/ppermute | solution.py:28
  69.0 0.0 collective-permute-start.16
  69.0 0.0 collective-permute-done.9.a2
  69.0 0.5 collective-permute-start.13
  69.5 0.7 collective-permute-done.8.a1
  70.2 0.0 collective-permute-start.14
  70.2 0.0 collective-permute-done.15.t0
  70.3 0.1 collective-permute-start.19
  70.3 0.2 select_reduce_fusion.3
  70.6 0.1 copy.14
  70.6 0.2 convert_reduce_fusion.1
  70.9 0.6 collective-permute-done.17.r3
  71.4 2.1 %collective-permute-start.18 = (bf16[4,16,16,256]{3,2,1,0:T(8,128)(2,1)S(1)}, bf16[4,16,16,256]{3,2,1,0:T(8,128)(2,1)S(1)}, u32[]{:S(2)}, u32[]{:S(2)}) collective-permute-start(bf16[4,16,16,256]{3,2,1,0:T(8,128)(2,1)S(1)} %collective-permute-done.17.r3), channel_id=1, source_target_pairs={{0,8},{1,9},{2,10},{3,11},{4,12},{5,13},{6,14},{7,15},{8,0},{9,1},... | collective-permute-start | bytes 1572872 | tf_op jit(solution)/shard_map/ppermute | solution.py:28
  73.5 0.1 select_reduce_fusion
  73.7 3.5 %shard_map.95.sv.sv_in = bf16[32,512,256]{2,1,0:T(8,128)(2,1)S(1)} custom-call(bf16[512,1024]{1,0:T(8,128)(2,1)} %s.1, bf16[512,1024]{1,0:T(8,128)(2,1)} %copy-done.5, bf16[512,1024]{1,0:T(8,128)(2,1)} %copy-done.6, bf16[512,1024]{1,0:T(8,128)(2,1)} %copy-done.7, bf16[512,1024]{1,0:T(8,128)(2,1)} %copy-done.3, bf16[512,768]{1,0:T(8,128)(2,1)} %collective-permute-done.8.a1, ...), custom_call_target="tpu_custom_call" | custom-call | tf_op jit(solution)/shard_map/pallas_call | solution.py:221
  77.2 0.0 collective-permute-done.13.tx0
  77.2 3.7 %shard_map.96.lv_in = bf16[4,16,256,256]{3,2,1,0:T(8,128)(2,1)S(1)} custom-call(s32[16]{0:T(128)S(1)} %fusion.13.place_ref, bf16[2,4,16,16,256]{4,3,2,1,0:T(8,128)(2,1)} %copy-done.2, bf16[2,4,16,16,256]{4,3,2,1,0:T(8,128)(2,1)} %copy-done.1, bf16[4,16,16,256]{3,2,1,0:T(8,128)(2,1)} %collective-permute-done.6.lh, ...), custom_call_target="tpu_custom_call" | custom-call | tf_op jit(solution)/shard_map/pallas_call | solution.py:229
  81.0 0.0 collective-permute-done.18.t3
  81.0 4.5 %shard_map.97 = (bf16[4,16,256,256]{3,2,1,0:T(8,128)(2,1)S(1)}, f32[4,512,256]{2,1,0:T(8,128)S(1)}) custom-call(s32[4,16]{1,0:T(4,128)S(1)} %get-tuple-element.43.slot_ref, s32[4,16]{1,0:T(4,128)S(1)} %get-tuple-element.42.block_ref, s32[16]{0:T(128)S(1)} %fusion.13.place_ref, ...), custom_call_target="tpu_custom_call", output_to_operand_aliasing={{0}: (4, {})} | custom-call | tf_op jit(solution)/shard_map/pallas_call | solution.py:238
  85.5 0.0 collective-permute-done.19.a3
  85.5 0.0 copy-start.8
  85.5 2.6 %shard_map.98 = (bf16[512,1024]{1,0:T(8,128)(2,1)}, f32[8,4,16,256]{3,2,1,0:T(8,128)S(1)}, bf16[8,4,16,256]{3,2,1,0:T(8,128)(2,1)S(1)}, bf16[32,512,256]{2,1,0:T(8,128)(2,1)S(1)}) custom-call(s32[4,16]{1,0:T(4,128)S(1)} %get-tuple-element.43.slot_ref, s32[4,16]{1,0:T(4,128)S(1)} %get-tuple-element.42.block_ref, ...), custom_call_target="tpu_custom_call", output_to_operand_aliasing={{3}: (4, {})} | custom-call | tf_op jit(solution)/shard_map/pallas_call | solution.py:248
  88.1 0.1 collective-permute-start.20
  88.2 1.5 %collective-permute-done.20 = bf16[8,4,16,256]{3,2,1,0:T(8,128)(2,1)S(1)} collective-permute-done((bf16[8,4,16,256]{3,2,1,0:T(8,128)(2,1)S(1)}, bf16[8,4,16,256]{3,2,1,0:T(8,128)(2,1)S(1)}, u32[]{:S(2)}, u32[]{:S(2)}) %collective-permute-start.20) | collective-permute-done | bytes 262176 | tf_op jit(solution)/shard_map/ppermute | solution.py:28
  89.7 0.1 add_convert_fusion
  89.8 12.5 %all_to_all.5 = bf16[8,4,16,256]{3,2,1,0:T(8,128)(2,1)S(1)} all-to-all(bf16[8,4,16,256]{3,2,1,0:T(8,128)(2,1)S(1)} %add_convert_fusion), channel_id=1, replica_groups={{0,16,32,48,64,80,96,112},{8,24,40,56,72,88,104,120},{1,17,33,49,65,81,..., dimensions={0} | all-to-all | bytes 524288 | tf_op jit(solution)/shard_map/all_to_all | solution.py:268
  102.4 0.6 sub.52
  (29 shorter events, 0.2 us)
Async XLA Ops:
  0.6 50.5 %copy-start = (s32[32,16]{0,1:T(8,128)S(1)}, s32[32,16]{0,1:T(8,128)}, u32[]{:S(2)}) copy-start(s32[32,16]{0,1:T(8,128)} %param.10) | copy-start | bytes 6148
  0.6 73.0 %copy-start.9 = (s32[16]{0:T(128)S(1)}, s32[16]{0:T(128)}, u32[]{:S(2)}) copy-start(s32[16]{0:T(128)} %constant.159.clone) | copy-start | bytes 196
  0.7 73.0 %copy-start.10 = (s32[16]{0:T(128)S(1)}, s32[16]{0:T(128)}, u32[]{:S(2)}) copy-start(s32[16]{0:T(128)} %constant.158.clone) | copy-start | bytes 196
  0.7 73.0 %copy-start.11 = (s32[16]{0:T(128)S(1)}, s32[16]{0:T(128)}, u32[]{:S(2)}) copy-start(s32[16]{0:T(128)} %constant.157.clone) | copy-start | bytes 196
  0.7 22.6 %collective-permute-start = (bf16[512,1024]{1,0:T(8,128)(2,1)}, bf16[512,1024]{1,0:T(8,128)(2,1)S(1)}, u32[]{:S(2)}, u32[]{:S(2)}) collective-permute-start(bf16[512,1024]{1,0:T(8,128)(2,1)} %s.1), channel_id=1, source_target_pairs={{0,2},{1,3},{2,4},{3,5},{4,6},{5,7},{6,0},{7,1},{8,14},{9,15},{10,... | collective-permute-start | bytes 3145736 | tf_op jit(solution)/shard_map/ppermute | solution.py:28
  2.8 15.0 %collective-permute-start.2 = (bf16[4,16,16,256]{3,2,1,0:T(8,128)(2,1)}, bf16[4,16,16,256]{3,2,1,0:T(8,128)(2,1)S(1)}, u32[]{:S(2)}, u32[]{:S(2)}) collective-permute-start(bf16[4,16,16,256]{3,2,1,0:T(8,128)(2,1)} %param.9), channel_id=1, source_target_pairs={{0,96},{1,97},{2,98},{3,99},{4,100},{5,101},{6,102},{7,103},{8,40}... | collective-permute-start | bytes 1572872 | tf_op jit(solution)/shard_map/ppermute | solution.py:28
  5.8 14.1 %collective-permute-start.1 = (bf16[4,16,16,256]{3,2,1,0:T(8,128)(2,1)}, bf16[4,16,16,256]{3,2,1,0:T(8,128)(2,1)}, u32[]{:S(2)}, u32[]{:S(2)}) collective-permute-start(bf16[4,16,16,256]{3,2,1,0:T(8,128)(2,1)} %param.9), channel_id=1, source_target_pairs={{0,32},{1,33},{2,34},{3,35},{4,36},{5,37},{6,38},{7,39},{8,104},{9... | collective-permute-start | bytes 1572872 | tf_op jit(solution)/shard_map/ppermute | solution.py:28
  5.8 26.0 %collective-permute-start.5 = (bf16[512,1024]{1,0:T(8,128)(2,1)}, bf16[512,1024]{1,0:T(8,128)(2,1)S(1)}, u32[]{:S(2)}, u32[]{:S(2)}) collective-permute-start(bf16[512,1024]{1,0:T(8,128)(2,1)} %s.1), channel_id=1, source_target_pairs={{0,1},{1,0},{2,3},{3,2},{4,5},{5,4},{6,7},{7,6},{8,9},{9,8},{10,11... | collective-permute-start | bytes 3145736 | tf_op jit(solution)/shard_map/ppermute | solution.py:28
  7.3 37.9 %collective-permute-start.3 = (bf16[512,1024]{1,0:T(8,128)(2,1)}, bf16[512,1024]{1,0:T(8,128)(2,1)S(1)}, u32[]{:S(2)}, u32[]{:S(2)}) collective-permute-start(bf16[512,1024]{1,0:T(8,128)(2,1)} %s.1), channel_id=1, source_target_pairs={{0,6},{1,7},{2,0},{3,1},{4,2},{5,3},{6,4},{7,5},{8,10},{9,11},{10,... | collective-permute-start | bytes 3145736 | tf_op jit(solution)/shard_map/ppermute | solution.py:28
  23.3 22.0 %copy-start.5 = (bf16[512,1024]{1,0:T(8,128)(2,1)}, bf16[512,1024]{1,0:T(8,128)(2,1)S(1)}, u32[]{:S(2)}) copy-start(bf16[512,1024]{1,0:T(8,128)(2,1)S(1)} %collective-permute-done.p1) | copy-start | bytes 3145732
  23.3 22.0 %collective-permute-start.4 = (bf16[512,1024]{1,0:T(8,128)(2,1)S(1)}, bf16[512,1024]{1,0:T(8,128)(2,1)S(1)}, u32[]{:S(2)}, u32[]{:S(2)}) collective-permute-start(bf16[512,1024]{1,0:T(8,128)(2,1)S(1)} %collective-permute-done.p1), channel_id=1, source_target_pairs={{0,2},{1,3},{2,4},{3,5},{4,6},{5,7},{6,0},{7,1},{8,14},{9,15},{10,... | collective-permute-start | bytes 3145736 | tf_op jit(solution)/shard_map/ppermute | solution.py:28
  25.5 19.7 %collective-permute-start.6 = (bf16[4,16,16,256]{3,2,1,0:T(8,128)(2,1)}, bf16[4,16,16,256]{3,2,1,0:T(8,128)(2,1)}, u32[]{:S(2)}, u32[]{:S(2)}) collective-permute-start(bf16[4,16,16,256]{3,2,1,0:T(8,128)(2,1)} %param.9), channel_id=1, source_target_pairs={{0,16},{1,17},{2,18},{3,19},{4,20},{5,21},{6,22},{7,23},{8,24},{9,... | collective-permute-start | bytes 1572872 | tf_op jit(solution)/shard_map/ppermute | solution.py:28
  28.8 16.4 %collective-permute-start.7 = (bf16[4,16,16,256]{3,2,1,0:T(8,128)(2,1)}, bf16[4,16,16,256]{3,2,1,0:T(8,128)(2,1)S(1)}, u32[]{:S(2)}, u32[]{:S(2)}) collective-permute-start(bf16[4,16,16,256]{3,2,1,0:T(8,128)(2,1)} %collective-permute-done.1), channel_id=1, source_target_pairs={{0,32},{1,33},{2,34},{3,35},{4,36},{5,37},{6,38},{7,39},{8,104},{9... | collective-permute-start | bytes 1572872 | tf_op jit(solution)/shard_map/ppermute | solution.py:28
  31.8 1.0 copy-start.3
  45.2 2.6 %copy-start.6 = (bf16[512,1024]{1,0:T(8,128)(2,1)}, bf16[512,1024]{1,0:T(8,128)(2,1)S(1)}, u32[]{:S(2)}) copy-start(bf16[512,1024]{1,0:T(8,128)(2,1)S(1)} %collective-permute-done.3.p2) | copy-start | bytes 3145732
  45.2 2.7 %copy-start.7 = (bf16[512,1024]{1,0:T(8,128)(2,1)}, bf16[512,1024]{1,0:T(8,128)(2,1)S(1)}, u32[]{:S(2)}) copy-start(bf16[512,1024]{1,0:T(8,128)(2,1)S(1)} %collective-permute-done.4.p3) | copy-start | bytes 3145732
  45.2 14.9 %collective-permute-start.12 = (bf16[4,16,16,256]{3,2,1,0:T(8,128)(2,1)}, bf16[4,16,16,256]{3,2,1,0:T(8,128)(2,1)S(1)}, u32[]{:S(2)}, u32[]{:S(2)}) collective-permute-start(bf16[4,16,16,256]{3,2,1,0:T(8,128)(2,1)} %collective-permute-done.6.lh), channel_id=1, source_target_pairs={{0,96},{1,97},{2,98},{3,99},{4,100},{5,101},{6,102},{7,103},{8,40}... | collective-permute-start | bytes 1572872 | tf_op jit(solution)/shard_map/ppermute | solution.py:28
  47.8 13.0 %collective-permute-start.11 = (bf16[4,16,16,256]{3,2,1,0:T(8,128)(2,1)}, bf16[4,16,16,256]{3,2,1,0:T(8,128)(2,1)}, u32[]{:S(2)}, u32[]{:S(2)}) collective-permute-start(bf16[4,16,16,256]{3,2,1,0:T(8,128)(2,1)} %collective-permute-done.6.lh), channel_id=1, source_target_pairs={{0,32},{1,33},{2,34},{3,35},{4,36},{5,37},{6,38},{7,39},{8,104},{9... | collective-permute-start | bytes 1572872 | tf_op jit(solution)/shard_map/ppermute | solution.py:28
  48.9 20.1 %collective-permute-start.10 = (bf16[3,512,256]{2,1,0:T(8,128)(2,1)}, bf16[3,512,256]{2,1,0:T(8,128)(2,1)}, u32[]{:S(2)}, u32[]{:S(2)}) collective-permute-start(bf16[3,512,256]{2,1,0:T(8,128)(2,1)} %pad_maximum_fusion.3), channel_id=1, source_target_pairs={{0,1},{1,0},{2,3},{3,2},{4,5},{5,4},{6,7},{7,6},{8,9},{9,8},{10,11... | collective-permute-start | bytes 2359304 | tf_op jit(solution)/shard_map/ppermute | solution.py:28
  49.1 19.9 %collective-permute-start.9 = (bf16[512,768]{1,0:T(8,128)(2,1)}, bf16[512,768]{1,0:T(8,128)(2,1)}, u32[]{:S(2)}, u32[]{:S(2)}) collective-permute-start(bf16[512,768]{1,0:T(8,128)(2,1)} %slice.16), channel_id=1, source_target_pairs={{0,6},{1,7},{2,0},{3,1},{4,2},{5,3},{6,4},{7,5},{8,10},{9,11},{10,... | collective-permute-start | bytes 2359304 | tf_op jit(solution)/shard_map/ppermute | solution.py:28
  50.8 19.4 %collective-permute-start.8 = (bf16[512,768]{1,0:T(8,128)(2,1)}, bf16[512,768]{1,0:T(8,128)(2,1)}, u32[]{:S(2)}, u32[]{:S(2)}) collective-permute-start(bf16[512,768]{1,0:T(8,128)(2,1)} %slice.16), channel_id=1, source_target_pairs={{0,2},{1,3},{2,4},{3,5},{4,6},{5,7},{6,0},{7,1},{8,14},{9,15},{10,... | collective-permute-start | bytes 2359304 | tf_op jit(solution)/shard_map/ppermute | solution.py:28
  60.1 10.1 %copy-start.4 = (bf16[4,16,16,256]{3,2,1,0:T(8,128)(2,1)}, bf16[4,16,16,256]{3,2,1,0:T(8,128)(2,1)S(1)}, u32[]{:S(2)}) copy-start(bf16[4,16,16,256]{3,2,1,0:T(8,128)(2,1)S(1)} %collective-permute-done.12.r2) | copy-start | bytes 1572868
  60.1 10.1 %collective-permute-start.15 = (bf16[4,16,16,256]{3,2,1,0:T(8,128)(2,1)}, bf16[4,16,16,256]{3,2,1,0:T(8,128)(2,1)}, u32[]{:S(2)}, u32[]{:S(2)}) collective-permute-start(bf16[4,16,16,256]{3,2,1,0:T(8,128)(2,1)} %collective-permute-done.6.lh), channel_id=1, source_target_pairs={{0,8},{1,9},{2,10},{3,11},{4,12},{5,13},{6,14},{7,15},{8,0},{9,1},... | collective-permute-start | bytes 1572872 | tf_op jit(solution)/shard_map/ppermute | solution.py:28
  60.8 10.6 %collective-permute-start.17 = (bf16[4,16,16,256]{3,2,1,0:T(8,128)(2,1)}, bf16[4,16,16,256]{3,2,1,0:T(8,128)(2,1)S(1)}, u32[]{:S(2)}, u32[]{:S(2)}) collective-permute-start(bf16[4,16,16,256]{3,2,1,0:T(8,128)(2,1)} %collective-permute-done.11.r1), channel_id=1, source_target_pairs={{0,32},{1,33},{2,34},{3,35},{4,36},{5,37},{6,38},{7,39},{8,104},{9... | collective-permute-start | bytes 1572872 | tf_op jit(solution)/shard_map/ppermute | solution.py:28
  60.9 16.2 %copy-start.1 = (bf16[2,4,16,16,256]{4,3,2,1,0:T(8,128)(2,1)}, bf16[2,4,16,16,256]{4,3,2,1,0:T(8,128)(2,1)S(1)}, u32[]{:S(2)}) copy-start(bf16[2,4,16,16,256]{4,3,2,1,0:T(8,128)(2,1)S(1)} %pad_maximum_fusion.1.x1) | copy-start | bytes 3145732
  62.6 14.6 %copy-start.2 = (bf16[2,4,16,16,256]{4,3,2,1,0:T(8,128)(2,1)}, bf16[2,4,16,16,256]{4,3,2,1,0:T(8,128)(2,1)S(1)}, u32[]{:S(2)}) copy-start(bf16[2,4,16,16,256]{4,3,2,1,0:T(8,128)(2,1)S(1)} %pad_maximum_fusion.x0) | copy-start | bytes 3145732
  69.0 8.2 %collective-permute-start.16 = (bf16[2,4,16,16,256]{4,3,2,1,0:T(8,128)(2,1)}, bf16[2,4,16,16,256]{4,3,2,1,0:T(8,128)(2,1)}, u32[]{:S(2)}, u32[]{:S(2)}) collective-permute-start(bf16[2,4,16,16,256]{4,3,2,1,0:T(8,128)(2,1)} %pad_maximum_fusion.2), channel_id=1, source_target_pairs={{0,8},{1,9},{2,10},{3,11},{4,12},{5,13},{6,14},{7,15},{8,0},{9,1},... | collective-permute-start | bytes 3145736 | tf_op jit(solution)/shard_map/ppermute | solution.py:28
  69.0 8.2 %collective-permute-start.13 = (bf16[2,4,16,16,256]{4,3,2,1,0:T(8,128)(2,1)S(1)}, bf16[2,4,16,16,256]{4,3,2,1,0:T(8,128)(2,1)}, u32[]{:S(2)}, u32[]{:S(2)}) collective-permute-start(bf16[2,4,16,16,256]{4,3,2,1,0:T(8,128)(2,1)S(1)} %pad_maximum_fusion.x0), channel_id=1, source_target_pairs={{0,8},{1,9},{2,10},{3,11},{4,12},{5,13},{6,14},{7,15},{8,0},{9,1},... | collective-permute-start | bytes 3145736 | tf_op jit(solution)/shard_map/ppermute | solution.py:28
  70.2 7.0 %collective-permute-start.14 = (bf16[2,4,16,16,256]{4,3,2,1,0:T(8,128)(2,1)S(1)}, bf16[2,4,16,16,256]{4,3,2,1,0:T(8,128)(2,1)}, u32[]{:S(2)}, u32[]{:S(2)}) collective-permute-start(bf16[2,4,16,16,256]{4,3,2,1,0:T(8,128)(2,1)S(1)} %pad_maximum_fusion.1.x1), channel_id=1, source_target_pairs={{0,8},{1,9},{2,10},{3,11},{4,12},{5,13},{6,14},{7,15},{8,0},{9,1},... | collective-permute-start | bytes 3145736 | tf_op jit(solution)/shard_map/ppermute | solution.py:28
  70.3 15.2 %collective-permute-start.19 = (bf16[512,768]{1,0:T(8,128)(2,1)}, bf16[512,768]{1,0:T(8,128)(2,1)S(1)}, u32[]{:S(2)}, u32[]{:S(2)}) collective-permute-start(bf16[512,768]{1,0:T(8,128)(2,1)} %collective-permute-done.8.a1), channel_id=1, source_target_pairs={{0,2},{1,3},{2,4},{3,5},{4,6},{5,7},{6,0},{7,1},{8,14},{9,15},{10,... | collective-permute-start | bytes 2359304 | tf_op jit(solution)/shard_map/ppermute | solution.py:28
  71.4 9.6 %collective-permute-start.18 = (bf16[4,16,16,256]{3,2,1,0:T(8,128)(2,1)S(1)}, bf16[4,16,16,256]{3,2,1,0:T(8,128)(2,1)S(1)}, u32[]{:S(2)}, u32[]{:S(2)}) collective-permute-start(bf16[4,16,16,256]{3,2,1,0:T(8,128)(2,1)S(1)} %collective-permute-done.17.r3), channel_id=1, source_target_pairs={{0,8},{1,9},{2,10},{3,11},{4,12},{5,13},{6,14},{7,15},{8,0},{9,1},... | collective-permute-start | bytes 1572872 | tf_op jit(solution)/shard_map/ppermute | solution.py:28
  85.5 16.9 %copy-start.8 = (f32[4,16,256]{2,1,0:T(8,128)S(1)}, f32[4,16,256]{2,1,0:T(8,128)}, u32[]{:S(2)}) copy-start(f32[4,16,256]{2,1,0:T(8,128)} %param.12) | copy-start | bytes 196612
  88.1 1.6 %collective-permute-start.20 = (bf16[8,4,16,256]{3,2,1,0:T(8,128)(2,1)S(1)}, bf16[8,4,16,256]{3,2,1,0:T(8,128)(2,1)S(1)}, u32[]{:S(2)}, u32[]{:S(2)}) collective-permute-start(bf16[8,4,16,256]{3,2,1,0:T(8,128)(2,1)S(1)} %get-tuple-element.41), channel_id=1, source_target_pairs={{0,8},{1,9},{2,10},{3,11},{4,12},{5,13},{6,14},{7,15},{8,0},{9,1},... | collective-permute-start | bytes 786440 | tf_op jit(solution)/shard_map/ppermute | solution.py:28

commit v5 on v4

--- a/solution.py
+++ b/solution.py
@@ -264,10 +264,15 @@
         compiler_params=params,
     )(sorted_slots, sorted_blocks, own, core.reshape(1).astype(jnp.int32), held, blocks, acc, a3)
 
-    halves = (keep + swap_core(send).astype(jnp.float32)).astype(jnp.bfloat16)
-    parts = lax.all_to_all(halves, "prow", split_axis=0, concat_axis=0, tiled=True,
-                           axis_index_groups=[list(range(c, 16, 2)) for c in range(2)])
-    total = jnp.sum(parts.astype(jnp.float32), axis=0)
+    one = (keep + swap_core(send).astype(jnp.float32)).reshape(4, 2, SUP, 16, B)
+    kept = lax.dynamic_index_in_dim(one, h, 1, keepdims=False)
+    sent = lax.dynamic_index_in_dim(one, 1 - h, 1, keepdims=False).astype(jnp.bfloat16)
+    two = kept + swap_h(sent).astype(jnp.float32)
+    narrow = two.astype(jnp.bfloat16)
+    parts = [move_y(lax.dynamic_index_in_dim(narrow, (y + step) % 4, 0, keepdims=False), step) for step in (2, 1, -1)]
+    total = lax.dynamic_index_in_dim(two, y, 0, keepdims=False)
+    for part in parts:
+        total = total + part.astype(jnp.float32)
     return sigma_off, inv_diag - total
 
 

time: 103 us -> 104 us (level)
  blocking collectives: 12.5 us -> 0 us
  waiting for transfers between devices: 40.5 us -> 48.4 us
  starting transfers between devices: 24.9 us -> 30.5 us
    all_to_all x1 -> x0, blocking collectives: 12.5 us -> none  [per_device(): lax.all_to_all(halves, 'prow', split_axis=0, concat_axis=0, tiled=True, a...]
    ppermute x21 -> x25, waiting for transfers between devices: 40.5 us -> 48.4 us  [permute(): return lax.ppermute(x, AXES, pairs)]
    ppermute x21 -> x25, starting transfers between devices: 24.9 us -> 30.5 us  [permute(): return lax.ppermute(x, AXES, pairs)]
  transfers between devices with their start and end apart: 21 -> 25, of which waited for: 10 -> 15; matrix products, arithmetic and copies ran while one was open for 8% -> 8% of each run, Pallas kernels for 11% -> 11%
where the time goes in v5:
time: 104 us
  waiting for transfers between devices  48.4 us (47%)
  starting transfers between devices  30.5 us (29%)
  Pallas kernels  14.3 us (14%)
  other arithmetic  7.31 us (7%)
  local copies, waits for them, and re-layouts  2.47 us (2%)
    ppermute x25, waiting for transfers between devices, permute(): return lax.ppermute(x, AXES, pairs)  48.4 us
    ppermute x25, starting transfers between devices, permute(): return lax.ppermute(x, AXES, pairs)  30.5 us
    pallas_call x1, Pallas kernels, per_device(): pl.pallas_call(main_kernel, out_shape=(panel_shape, acc_shape), in_specs=...  4.45 us
    pallas_call x1, Pallas kernels, per_device(): pl.pallas_call(panel_kernel, out_shape=panel_shape, in_specs=[smem] + [hb...  3.75 us
    pallas_call x1, Pallas kernels, per_device(): pl.pallas_call(hold_kernel, out_shape=held_shape, in_specs=[hbm] * 8, out...  3.5 us
    pallas_call x1, Pallas kernels, per_device(): pl.pallas_call(late_kernel, out_shape=(jax.ShapeDtypeStruct((ROWS, SUP *...  2.61 us
    another operation x1, other arithmetic, per_device(): t2 = swap_core(jnp.stack([r1, r2]))  2.32 us
  transfers between devices with their start and end apart: 25, of which 15 were waited for; matrix products, arithmetic and copies ran while one was open for 8% of the time, Pallas kernels for 11%

profile of v5, /device:TPU:0, one launch (start us, length us, event | category | flops | bytes accessed | tf_op | source)
XLA Modules:
  0.0 103.9 jit_solution(10265788941596155488)
XLA Ops:
  0.6 0.0 copy-start
  0.6 0.0 copy-start.9
  0.7 0.0 copy-start.10
  0.7 0.0 copy-start.11
  0.7 2.1 %collective-permute-start = (bf16[512,1024]{1,0:T(8,128)(2,1)}, bf16[512,1024]{1,0:T(8,128)(2,1)S(1)}, u32[]{:S(2)}, u32[]{:S(2)}) collective-permute-start(bf16[512,1024]{1,0:T(8,128)(2,1)} %s.1), channel_id=1, source_target_pairs={{0,2},{1,3},{2,4},{3,5},{4,6},{5,7},{6,0},{7,1},{8,14},{9,15},{10,... | collective-permute-start | bytes 3145736 | tf_op jit(solution)/shard_map/ppermute | solution.py:28
  2.8 1.6 %collective-permute-start.1 = (bf16[4,16,16,256]{3,2,1,0:T(8,128)(2,1)}, bf16[4,16,16,256]{3,2,1,0:T(8,128)(2,1)}, u32[]{:S(2)}, u32[]{:S(2)}) collective-permute-start(bf16[4,16,16,256]{3,2,1,0:T(8,128)(2,1)} %param.9), channel_id=1, source_target_pairs={{0,32},{1,33},{2,34},{3,35},{4,36},{5,37},{6,38},{7,39},{8,104},{9... | collective-permute-start | bytes 1572872 | tf_op jit(solution)/shard_map/ppermute | solution.py:28
  4.3 1.7 %collective-permute-start.2 = (bf16[4,16,16,256]{3,2,1,0:T(8,128)(2,1)}, bf16[4,16,16,256]{3,2,1,0:T(8,128)(2,1)S(1)}, u32[]{:S(2)}, u32[]{:S(2)}) collective-permute-start(bf16[4,16,16,256]{3,2,1,0:T(8,128)(2,1)} %param.9), channel_id=1, source_target_pairs={{0,96},{1,97},{2,98},{3,99},{4,100},{5,101},{6,102},{7,103},{8,40}... | collective-permute-start | bytes 1572872 | tf_op jit(solution)/shard_map/ppermute | solution.py:28
  6.0 1.5 %collective-permute-start.5 = (bf16[512,1024]{1,0:T(8,128)(2,1)}, bf16[512,1024]{1,0:T(8,128)(2,1)S(1)}, u32[]{:S(2)}, u32[]{:S(2)}) collective-permute-start(bf16[512,1024]{1,0:T(8,128)(2,1)} %s.1), channel_id=1, source_target_pairs={{0,1},{1,0},{2,3},{3,2},{4,5},{5,4},{6,7},{7,6},{8,9},{9,8},{10,11... | collective-permute-start | bytes 3145736 | tf_op jit(solution)/shard_map/ppermute | solution.py:28
  7.5 2.2 %collective-permute-start.3 = (bf16[512,1024]{1,0:T(8,128)(2,1)}, bf16[512,1024]{1,0:T(8,128)(2,1)S(1)}, u32[]{:S(2)}, u32[]{:S(2)}) collective-permute-start(bf16[512,1024]{1,0:T(8,128)(2,1)} %s.1), channel_id=1, source_target_pairs={{0,6},{1,7},{2,0},{3,1},{4,2},{5,3},{6,4},{7,5},{8,10},{9,11},{10,... | collective-permute-start | bytes 3145736 | tf_op jit(solution)/shard_map/ppermute | solution.py:28
  9.7 5.9 %collective-permute-done.1 = bf16[4,16,16,256]{3,2,1,0:T(8,128)(2,1)} collective-permute-done((bf16[4,16,16,256]{3,2,1,0:T(8,128)(2,1)}, bf16[4,16,16,256]{3,2,1,0:T(8,128)(2,1)}, u32[]{:S(2)}, u32[]{:S(2)}) %collective-permute-start.1) | collective-permute-done | bytes 524320 | tf_op jit(solution)/shard_map/ppermute | solution.py:28
  15.6 2.9 %collective-permute-done.2 = bf16[4,16,16,256]{3,2,1,0:T(8,128)(2,1)S(1)} collective-permute-done((bf16[4,16,16,256]{3,2,1,0:T(8,128)(2,1)}, bf16[4,16,16,256]{3,2,1,0:T(8,128)(2,1)S(1)}, u32[]{:S(2)}, u32[]{:S(2)}) %collective-permute-start.2) | collective-permute-done | bytes 524320 | tf_op jit(solution)/shard_map/ppermute | solution.py:28
  18.5 4.8 %collective-permute-done.p1 = bf16[512,1024]{1,0:T(8,128)(2,1)S(1)} collective-permute-done((bf16[512,1024]{1,0:T(8,128)(2,1)}, bf16[512,1024]{1,0:T(8,128)(2,1)S(1)}, u32[]{:S(2)}, u32[]{:S(2)}) %collective-permute-start) | collective-permute-done | bytes 1048608 | tf_op jit(solution)/shard_map/ppermute | solution.py:28
  23.3 2.3 %collective-permute-start.4 = (bf16[512,1024]{1,0:T(8,128)(2,1)S(1)}, bf16[512,1024]{1,0:T(8,128)(2,1)S(1)}, u32[]{:S(2)}, u32[]{:S(2)}) collective-permute-start(bf16[512,1024]{1,0:T(8,128)(2,1)S(1)} %collective-permute-done.p1), channel_id=1, source_target_pairs={{0,2},{1,3},{2,4},{3,5},{4,6},{5,7},{6,0},{7,1},{8,14},{9,15},{10,... | collective-permute-start | bytes 3145736 | tf_op jit(solution)/shard_map/ppermute | solution.py:28
  25.6 3.3 %collective-permute-start.6 = (bf16[4,16,16,256]{3,2,1,0:T(8,128)(2,1)}, bf16[4,16,16,256]{3,2,1,0:T(8,128)(2,1)}, u32[]{:S(2)}, u32[]{:S(2)}) collective-permute-start(bf16[4,16,16,256]{3,2,1,0:T(8,128)(2,1)} %param.9), channel_id=1, source_target_pairs={{0,16},{1,17},{2,18},{3,19},{4,20},{5,21},{6,22},{7,23},{8,24},{9,... | collective-permute-start | bytes 1572872 | tf_op jit(solution)/shard_map/ppermute | solution.py:28
  28.9 2.9 %collective-permute-start.7 = (bf16[4,16,16,256]{3,2,1,0:T(8,128)(2,1)}, bf16[4,16,16,256]{3,2,1,0:T(8,128)(2,1)S(1)}, u32[]{:S(2)}, u32[]{:S(2)}) collective-permute-start(bf16[4,16,16,256]{3,2,1,0:T(8,128)(2,1)} %collective-permute-done.1), channel_id=1, source_target_pairs={{0,32},{1,33},{2,34},{3,35},{4,36},{5,37},{6,38},{7,39},{8,104},{9... | collective-permute-start | bytes 1572872 | tf_op jit(solution)/shard_map/ppermute | solution.py:28
  31.8 0.3 collective-permute-done.5.sw
  32.0 1.0 copy-done.3
  33.0 1.0 slice.16
  34.1 11.5 %collective-permute-done.6.lh = bf16[4,16,16,256]{3,2,1,0:T(8,128)(2,1)} collective-permute-done((bf16[4,16,16,256]{3,2,1,0:T(8,128)(2,1)}, bf16[4,16,16,256]{3,2,1,0:T(8,128)(2,1)}, u32[]{:S(2)}, u32[]{:S(2)}) %collective-permute-start.6) | collective-permute-done | bytes 524320 | tf_op jit(solution)/shard_map/ppermute | solution.py:28
  45.6 0.0 collective-permute-done.3.p2
  45.6 0.0 collective-permute-done.7
  45.6 0.5 collective-permute-start.11
  46.1 2.8 %collective-permute-start.12 = (bf16[4,16,16,256]{3,2,1,0:T(8,128)(2,1)}, bf16[4,16,16,256]{3,2,1,0:T(8,128)(2,1)S(1)}, u32[]{:S(2)}, u32[]{:S(2)}) collective-permute-start(bf16[4,16,16,256]{3,2,1,0:T(8,128)(2,1)} %collective-permute-done.6.lh), channel_id=1, source_target_pairs={{0,96},{1,97},{2,98},{3,99},{4,100},{5,101},{6,102},{7,103},{8,40}... | collective-permute-start | bytes 1572872 | tf_op jit(solution)/shard_map/ppermute | solution.py:28
  48.9 0.1 slice_bitcast_fusion
  49.0 1.0 pad_maximum_fusion.3
  50.0 0.2 collective-permute-start.10
  50.2 3.2 %collective-permute-start.9 = (bf16[512,768]{1,0:T(8,128)(2,1)}, bf16[512,768]{1,0:T(8,128)(2,1)}, u32[]{:S(2)}, u32[]{:S(2)}) collective-permute-start(bf16[512,768]{1,0:T(8,128)(2,1)} %slice.16), channel_id=1, source_target_pairs={{0,6},{1,7},{2,0},{3,1},{4,2},{5,3},{6,4},{7,5},{8,10},{9,11},{10,... | collective-permute-start | bytes 2359304 | tf_op jit(solution)/shard_map/ppermute | solution.py:28
  53.4 0.1 constant_dynamic-slice_fusion
  53.5 0.1 copy.13
  53.6 0.9 select_reduce_fusion.2
  54.5 7.0 %collective-permute-done.11.r1 = bf16[4,16,16,256]{3,2,1,0:T(8,128)(2,1)} collective-permute-done((bf16[4,16,16,256]{3,2,1,0:T(8,128)(2,1)}, bf16[4,16,16,256]{3,2,1,0:T(8,128)(2,1)}, u32[]{:S(2)}, u32[]{:S(2)}) %collective-permute-start.11) | collective-permute-done | bytes 524320 | tf_op jit(solution)/shard_map/ppermute | solution.py:28
  61.4 0.0 collective-permute-start.15
  61.4 0.0 collective-permute-done.12.r2
  61.4 0.1 collective-permute-start.17
  61.5 2.3 %pad_maximum_fusion.2 = bf16[2,4,16,16,256]{4,3,2,1,0:T(8,128)(2,1)} fusion(bf16[1,4,16,16,256]{4,3,2,1,0:T(8,128)(2,1)S(1)} %bitcast.33, bf16[1,4,16,16,256]{4,3,2,1,0:T(8,128)(2,1)} %bitcast.8), kind=kLoop, calls=%fused_computation.2 | loop fusion | flops 524288 | bytes 2097152 | tf_op jit(solution)/shard_map/stack | solution.py:204
  63.9 0.1 pad_maximum_fusion.1.x1
  64.0 1.7 %pad_maximum_fusion.x0 = bf16[2,4,16,16,256]{4,3,2,1,0:T(8,128)(2,1)S(1)} fusion(bf16[1,4,16,16,256]{4,3,2,1,0:T(8,128)(2,1)} %bitcast.5, bf16[1,4,16,16,256]{4,3,2,1,0:T(8,128)(2,1)} %bitcast.36), kind=kLoop, calls=%fused_computation | loop fusion | flops 524288 | bytes 2097152 | tf_op jit(solution)/shard_map/stack | solution.py:199
  65.7 2.4 %collective-permute-done.10.far = bf16[3,512,256]{2,1,0:T(8,128)(2,1)} collective-permute-done((bf16[3,512,256]{2,1,0:T(8,128)(2,1)}, bf16[3,512,256]{2,1,0:T(8,128)(2,1)}, u32[]{:S(2)}, u32[]{:S(2)}) %collective-permute-start.10) | collective-permute-done | bytes 786464 | tf_op jit(solution)/shard_map/ppermute | solution.py:28
  68.1 2.6 %collective-permute-done.8.a1 = bf16[512,768]{1,0:T(8,128)(2,1)} collective-permute-done((bf16[512,768]{1,0:T(8,128)(2,1)}, bf16[512,768]{1,0:T(8,128)(2,1)}, u32[]{:S(2)}, u32[]{:S(2)}) %collective-permute-start.8) | collective-permute-done | bytes 786464 | tf_op jit(solution)/shard_map/ppermute | solution.py:28
  70.7 0.0 collective-permute-start.14
  70.7 0.5 collective-permute-start.13
  71.2 0.1 collective-permute-start.19
  71.3 0.2 select_reduce_fusion.3
  71.5 0.1 copy.14
  71.6 0.2 convert_reduce_fusion
  71.8 0.3 collective-permute-done.17.r3
  72.1 0.1 select_reduce_fusion
  72.3 3.5 %shard_map.95.sv.sv_in = bf16[32,512,256]{2,1,0:T(8,128)(2,1)S(1)} custom-call(bf16[512,1024]{1,0:T(8,128)(2,1)} %s.1, bf16[512,1024]{1,0:T(8,128)(2,1)} %copy-done.5, bf16[512,1024]{1,0:T(8,128)(2,1)} %copy-done.6, bf16[512,1024]{1,0:T(8,128)(2,1)} %copy-done.7, bf16[512,1024]{1,0:T(8,128)(2,1)} %copy-done.3, bf16[512,768]{1,0:T(8,128)(2,1)} %collective-permute-done.8.a1, ...), custom_call_target="tpu_custom_call" | custom-call | tf_op jit(solution)/shard_map/pallas_call | solution.py:221
  75.9 3.7 %shard_map.96.lv_in = bf16[4,16,256,256]{3,2,1,0:T(8,128)(2,1)S(1)} custom-call(s32[16]{0:T(128)S(1)} %fusion.17.place_ref, bf16[2,4,16,16,256]{4,3,2,1,0:T(8,128)(2,1)} %copy-done.2, bf16[2,4,16,16,256]{4,3,2,1,0:T(8,128)(2,1)} %copy-done.1, bf16[4,16,16,256]{3,2,1,0:T(8,128)(2,1)} %collective-permute-done.6.lh, ...), custom_call_target="tpu_custom_call" | custom-call | tf_op jit(solution)/shard_map/pallas_call | solution.py:229
  79.6 4.5 %shard_map.97 = (bf16[4,16,256,256]{3,2,1,0:T(8,128)(2,1)S(1)}, f32[4,512,256]{2,1,0:T(8,128)S(1)}) custom-call(s32[4,16]{1,0:T(4,128)S(1)} %get-tuple-element.43.slot_ref, s32[4,16]{1,0:T(4,128)S(1)} %get-tuple-element.42.block_ref, s32[16]{0:T(128)S(1)} %fusion.17.place_ref, ...), custom_call_target="tpu_custom_call", output_to_operand_aliasing={{0}: (4, {})} | custom-call | tf_op jit(solution)/shard_map/pallas_call | solution.py:238
  84.1 0.6 collective-permute-done.19.a3
  84.7 2.6 %shard_map.98 = (bf16[512,1024]{1,0:T(8,128)(2,1)}, f32[8,4,16,256]{3,2,1,0:T(8,128)S(1)}, bf16[8,4,16,256]{3,2,1,0:T(8,128)(2,1)S(1)}, bf16[32,512,256]{2,1,0:T(8,128)(2,1)S(1)}) custom-call(s32[4,16]{1,0:T(4,128)S(1)} %get-tuple-element.43.slot_ref, s32[4,16]{1,0:T(4,128)S(1)} %get-tuple-element.42.block_ref, ...), custom_call_target="tpu_custom_call", output_to_operand_aliasing={{3}: (4, {})} | custom-call | tf_op jit(solution)/shard_map/pallas_call | solution.py:248
  87.3 0.1 collective-permute-start.20
  87.4 1.5 %collective-permute-done.20 = bf16[8,4,16,256]{3,2,1,0:T(8,128)(2,1)S(1)} collective-permute-done((bf16[8,4,16,256]{3,2,1,0:T(8,128)(2,1)S(1)}, bf16[8,4,16,256]{3,2,1,0:T(8,128)(2,1)S(1)}, u32[]{:S(2)}, u32[]{:S(2)}) %collective-permute-start.20) | collective-permute-done | bytes 262176 | tf_op jit(solution)/shard_map/ppermute | solution.py:28
  89.0 0.1 convert_add_fusion
  89.1 0.6 collective-permute-start.21
  89.7 6.5 %collective-permute-done.21 = bf16[4,4,16,256]{3,2,1,0:T(8,128)(2,1)S(1)} collective-permute-done((bf16[4,4,16,256]{3,2,1,0:T(8,128)(2,1)S(1)}, bf16[4,4,16,256]{3,2,1,0:T(8,128)(2,1)S(1)}, u32[]{:S(2)}, u32[]{:S(2)}) %collective-permute-start.21) | collective-permute-done | bytes 131104 | tf_op jit(solution)/shard_map/ppermute | solution.py:28
  96.3 1.6 %collective-permute-start.22 = (bf16[4,16,256]{2,1,0:T(8,128)(2,1)S(1)}, bf16[4,16,256]{2,1,0:T(8,128)(2,1)S(1)}, u32[]{:S(2)}, u32[]{:S(2)}) collective-permute-start(bf16[4,16,256]{2,1,0:T(8,128)(2,1)S(1)} %get-tuple-element.46), channel_id=1, source_target_pairs={{0,64},{1,65},{2,66},{3,67},{4,68},{5,69},{6,70},{7,71},{8,72},{9,... | collective-permute-start | bytes 98312 | tf_op jit(solution)/shard_map/ppermute | solution.py:28
  97.9 1.4 %collective-permute-start.23 = (bf16[4,16,256]{2,1,0:T(8,128)(2,1)S(1)}, bf16[4,16,256]{2,1,0:T(8,128)(2,1)S(1)}, u32[]{:S(2)}, u32[]{:S(2)}) collective-permute-start(bf16[4,16,256]{2,1,0:T(8,128)(2,1)S(1)} %get-tuple-element.48), channel_id=1, source_target_pairs={{0,32},{1,33},{2,34},{3,35},{4,36},{5,37},{6,38},{7,39},{8,40},{9,... | collective-permute-start | bytes 98312 | tf_op jit(solution)/shard_map/ppermute | solution.py:28
  99.3 1.8 %collective-permute-start.24 = (bf16[4,16,256]{2,1,0:T(8,128)(2,1)S(1)}, bf16[4,16,256]{2,1,0:T(8,128)(2,1)S(1)}, u32[]{:S(2)}, u32[]{:S(2)}) collective-permute-start(bf16[4,16,256]{2,1,0:T(8,128)(2,1)S(1)} %get-tuple-element.47), channel_id=1, source_target_pairs={{0,96},{1,97},{2,98},{3,99},{4,100},{5,101},{6,102},{7,103},{8,104... | collective-permute-start | bytes 98312 | tf_op jit(solution)/shard_map/ppermute | solution.py:28
  101.1 0.6 collective-permute-done.22
  101.8 1.2 %collective-permute-done.23 = bf16[4,16,256]{2,1,0:T(8,128)(2,1)S(1)} collective-permute-done((bf16[4,16,256]{2,1,0:T(8,128)(2,1)S(1)}, bf16[4,16,256]{2,1,0:T(8,128)(2,1)S(1)}, u32[]{:S(2)}, u32[]{:S(2)}) %collective-permute-start.23) | collective-permute-done | bytes 32800 | tf_op jit(solution)/shard_map/ppermute | solution.py:28
  103.0 0.2 collective-permute-done.24
  103.3 0.6 fusion.3
  (38 shorter events, 0.3 us)
Async XLA Ops:
  0.6 52.8 %copy-start = (s32[32,16]{0,1:T(8,128)S(1)}, s32[32,16]{0,1:T(8,128)}, u32[]{:S(2)}) copy-start(s32[32,16]{0,1:T(8,128)} %param.10) | copy-start | bytes 6148
  0.6 71.6 %copy-start.9 = (s32[16]{0:T(128)S(1)}, s32[16]{0:T(128)}, u32[]{:S(2)}) copy-start(s32[16]{0:T(128)} %constant.187.clone) | copy-start | bytes 196
  0.7 71.6 %copy-start.10 = (s32[16]{0:T(128)S(1)}, s32[16]{0:T(128)}, u32[]{:S(2)}) copy-start(s32[16]{0:T(128)} %constant.188.clone) | copy-start | bytes 196
  0.7 71.6 %copy-start.11 = (s32[16]{0:T(128)S(1)}, s32[16]{0:T(128)}, u32[]{:S(2)}) copy-start(s32[16]{0:T(128)} %constant.189.clone) | copy-start | bytes 196
  0.7 22.6 %collective-permute-start = (bf16[512,1024]{1,0:T(8,128)(2,1)}, bf16[512,1024]{1,0:T(8,128)(2,1)S(1)}, u32[]{:S(2)}, u32[]{:S(2)}) collective-permute-start(bf16[512,1024]{1,0:T(8,128)(2,1)} %s.1), channel_id=1, source_target_pairs={{0,2},{1,3},{2,4},{3,5},{4,6},{5,7},{6,0},{7,1},{8,14},{9,15},{10,... | collective-permute-start | bytes 3145736 | tf_op jit(solution)/shard_map/ppermute | solution.py:28
  2.8 12.8 %collective-permute-start.1 = (bf16[4,16,16,256]{3,2,1,0:T(8,128)(2,1)}, bf16[4,16,16,256]{3,2,1,0:T(8,128)(2,1)}, u32[]{:S(2)}, u32[]{:S(2)}) collective-permute-start(bf16[4,16,16,256]{3,2,1,0:T(8,128)(2,1)} %param.9), channel_id=1, source_target_pairs={{0,32},{1,33},{2,34},{3,35},{4,36},{5,37},{6,38},{7,39},{8,104},{9... | collective-permute-start | bytes 1572872 | tf_op jit(solution)/shard_map/ppermute | solution.py:28
  4.3 14.1 %collective-permute-start.2 = (bf16[4,16,16,256]{3,2,1,0:T(8,128)(2,1)}, bf16[4,16,16,256]{3,2,1,0:T(8,128)(2,1)S(1)}, u32[]{:S(2)}, u32[]{:S(2)}) collective-permute-start(bf16[4,16,16,256]{3,2,1,0:T(8,128)(2,1)} %param.9), channel_id=1, source_target_pairs={{0,96},{1,97},{2,98},{3,99},{4,100},{5,101},{6,102},{7,103},{8,40}... | collective-permute-start | bytes 1572872 | tf_op jit(solution)/shard_map/ppermute | solution.py:28
  6.0 26.0 %collective-permute-start.5 = (bf16[512,1024]{1,0:T(8,128)(2,1)}, bf16[512,1024]{1,0:T(8,128)(2,1)S(1)}, u32[]{:S(2)}, u32[]{:S(2)}) collective-permute-start(bf16[512,1024]{1,0:T(8,128)(2,1)} %s.1), channel_id=1, source_target_pairs={{0,1},{1,0},{2,3},{3,2},{4,5},{5,4},{6,7},{7,6},{8,9},{9,8},{10,11... | collective-permute-start | bytes 3145736 | tf_op jit(solution)/shard_map/ppermute | solution.py:28
  7.5 38.1 %collective-permute-start.3 = (bf16[512,1024]{1,0:T(8,128)(2,1)}, bf16[512,1024]{1,0:T(8,128)(2,1)S(1)}, u32[]{:S(2)}, u32[]{:S(2)}) collective-permute-start(bf16[512,1024]{1,0:T(8,128)(2,1)} %s.1), channel_id=1, source_target_pairs={{0,6},{1,7},{2,0},{3,1},{4,2},{5,3},{6,4},{7,5},{8,10},{9,11},{10,... | collective-permute-start | bytes 3145736 | tf_op jit(solution)/shard_map/ppermute | solution.py:28
  23.3 22.3 %copy-start.5 = (bf16[512,1024]{1,0:T(8,128)(2,1)}, bf16[512,1024]{1,0:T(8,128)(2,1)S(1)}, u32[]{:S(2)}) copy-start(bf16[512,1024]{1,0:T(8,128)(2,1)S(1)} %collective-permute-done.p1) | copy-start | bytes 3145732
  23.3 22.3 %collective-permute-start.4 = (bf16[512,1024]{1,0:T(8,128)(2,1)S(1)}, bf16[512,1024]{1,0:T(8,128)(2,1)S(1)}, u32[]{:S(2)}, u32[]{:S(2)}) collective-permute-start(bf16[512,1024]{1,0:T(8,128)(2,1)S(1)} %collective-permute-done.p1), channel_id=1, source_target_pairs={{0,2},{1,3},{2,4},{3,5},{4,6},{5,7},{6,0},{7,1},{8,14},{9,15},{10,... | collective-permute-start | bytes 3145736 | tf_op jit(solution)/shard_map/ppermute | solution.py:28
  25.6 20.0 %collective-permute-start.6 = (bf16[4,16,16,256]{3,2,1,0:T(8,128)(2,1)}, bf16[4,16,16,256]{3,2,1,0:T(8,128)(2,1)}, u32[]{:S(2)}, u32[]{:S(2)}) collective-permute-start(bf16[4,16,16,256]{3,2,1,0:T(8,128)(2,1)} %param.9), channel_id=1, source_target_pairs={{0,16},{1,17},{2,18},{3,19},{4,20},{5,21},{6,22},{7,23},{8,24},{9,... | collective-permute-start | bytes 1572872 | tf_op jit(solution)/shard_map/ppermute | solution.py:28
  28.9 16.7 %collective-permute-start.7 = (bf16[4,16,16,256]{3,2,1,0:T(8,128)(2,1)}, bf16[4,16,16,256]{3,2,1,0:T(8,128)(2,1)S(1)}, u32[]{:S(2)}, u32[]{:S(2)}) collective-permute-start(bf16[4,16,16,256]{3,2,1,0:T(8,128)(2,1)} %collective-permute-done.1), channel_id=1, source_target_pairs={{0,32},{1,33},{2,34},{3,35},{4,36},{5,37},{6,38},{7,39},{8,104},{9... | collective-permute-start | bytes 1572872 | tf_op jit(solution)/shard_map/ppermute | solution.py:28
  32.0 1.0 copy-start.3
  45.6 3.3 %copy-start.6 = (bf16[512,1024]{1,0:T(8,128)(2,1)}, bf16[512,1024]{1,0:T(8,128)(2,1)S(1)}, u32[]{:S(2)}) copy-start(bf16[512,1024]{1,0:T(8,128)(2,1)S(1)} %collective-permute-done.3.p2) | copy-start | bytes 3145732
  45.6 3.4 %copy-start.7 = (bf16[512,1024]{1,0:T(8,128)(2,1)}, bf16[512,1024]{1,0:T(8,128)(2,1)S(1)}, u32[]{:S(2)}) copy-start(bf16[512,1024]{1,0:T(8,128)(2,1)S(1)} %collective-permute-done.4.p3) | copy-start | bytes 3145732
  45.6 15.8 %collective-permute-start.11 = (bf16[4,16,16,256]{3,2,1,0:T(8,128)(2,1)}, bf16[4,16,16,256]{3,2,1,0:T(8,128)(2,1)}, u32[]{:S(2)}, u32[]{:S(2)}) collective-permute-start(bf16[4,16,16,256]{3,2,1,0:T(8,128)(2,1)} %collective-permute-done.6.lh), channel_id=1, source_target_pairs={{0,32},{1,33},{2,34},{3,35},{4,36},{5,37},{6,38},{7,39},{8,104},{9... | collective-permute-start | bytes 1572872 | tf_op jit(solution)/shard_map/ppermute | solution.py:28
  46.1 15.3 %collective-permute-start.12 = (bf16[4,16,16,256]{3,2,1,0:T(8,128)(2,1)}, bf16[4,16,16,256]{3,2,1,0:T(8,128)(2,1)S(1)}, u32[]{:S(2)}, u32[]{:S(2)}) collective-permute-start(bf16[4,16,16,256]{3,2,1,0:T(8,128)(2,1)} %collective-permute-done.6.lh), channel_id=1, source_target_pairs={{0,96},{1,97},{2,98},{3,99},{4,100},{5,101},{6,102},{7,103},{8,40}... | collective-permute-start | bytes 1572872 | tf_op jit(solution)/shard_map/ppermute | solution.py:28
  50.0 18.1 %collective-permute-start.10 = (bf16[3,512,256]{2,1,0:T(8,128)(2,1)}, bf16[3,512,256]{2,1,0:T(8,128)(2,1)}, u32[]{:S(2)}, u32[]{:S(2)}) collective-permute-start(bf16[3,512,256]{2,1,0:T(8,128)(2,1)} %pad_maximum_fusion.3), channel_id=1, source_target_pairs={{0,1},{1,0},{2,3},{3,2},{4,5},{5,4},{6,7},{7,6},{8,9},{9,8},{10,11... | collective-permute-start | bytes 2359304 | tf_op jit(solution)/shard_map/ppermute | solution.py:28
  50.2 20.5 %collective-permute-start.8 = (bf16[512,768]{1,0:T(8,128)(2,1)}, bf16[512,768]{1,0:T(8,128)(2,1)}, u32[]{:S(2)}, u32[]{:S(2)}) collective-permute-start(bf16[512,768]{1,0:T(8,128)(2,1)} %slice.16), channel_id=1, source_target_pairs={{0,2},{1,3},{2,4},{3,5},{4,6},{5,7},{6,0},{7,1},{8,14},{9,15},{10,... | collective-permute-start | bytes 2359304 | tf_op jit(solution)/shard_map/ppermute | solution.py:28
  50.2 20.5 %collective-permute-start.9 = (bf16[512,768]{1,0:T(8,128)(2,1)}, bf16[512,768]{1,0:T(8,128)(2,1)}, u32[]{:S(2)}, u32[]{:S(2)}) collective-permute-start(bf16[512,768]{1,0:T(8,128)(2,1)} %slice.16), channel_id=1, source_target_pairs={{0,6},{1,7},{2,0},{3,1},{4,2},{5,3},{6,4},{7,5},{8,10},{9,11},{10,... | collective-permute-start | bytes 2359304 | tf_op jit(solution)/shard_map/ppermute | solution.py:28
  61.4 9.8 %collective-permute-start.15 = (bf16[4,16,16,256]{3,2,1,0:T(8,128)(2,1)}, bf16[4,16,16,256]{3,2,1,0:T(8,128)(2,1)}, u32[]{:S(2)}, u32[]{:S(2)}) collective-permute-start(bf16[4,16,16,256]{3,2,1,0:T(8,128)(2,1)} %collective-permute-done.6.lh), channel_id=1, source_target_pairs={{0,8},{1,9},{2,10},{3,11},{4,12},{5,13},{6,14},{7,15},{8,0},{9,1},... | collective-permute-start | bytes 1572872 | tf_op jit(solution)/shard_map/ppermute | solution.py:28
  61.4 9.8 %copy-start.4 = (bf16[4,16,16,256]{3,2,1,0:T(8,128)(2,1)}, bf16[4,16,16,256]{3,2,1,0:T(8,128)(2,1)S(1)}, u32[]{:S(2)}) copy-start(bf16[4,16,16,256]{3,2,1,0:T(8,128)(2,1)S(1)} %collective-permute-done.12.r2) | copy-start | bytes 1572868
  61.4 10.7 %collective-permute-start.17 = (bf16[4,16,16,256]{3,2,1,0:T(8,128)(2,1)}, bf16[4,16,16,256]{3,2,1,0:T(8,128)(2,1)S(1)}, u32[]{:S(2)}, u32[]{:S(2)}) collective-permute-start(bf16[4,16,16,256]{3,2,1,0:T(8,128)(2,1)} %collective-permute-done.11.r1), channel_id=1, source_target_pairs={{0,32},{1,33},{2,34},{3,35},{4,36},{5,37},{6,38},{7,39},{8,104},{9... | collective-permute-start | bytes 1572872 | tf_op jit(solution)/shard_map/ppermute | solution.py:28
  64.0 11.8 %copy-start.1 = (bf16[2,4,16,16,256]{4,3,2,1,0:T(8,128)(2,1)}, bf16[2,4,16,16,256]{4,3,2,1,0:T(8,128)(2,1)S(1)}, u32[]{:S(2)}) copy-start(bf16[2,4,16,16,256]{4,3,2,1,0:T(8,128)(2,1)S(1)} %pad_maximum_fusion.1.x1) | copy-start | bytes 3145732
  65.6 10.2 %copy-start.2 = (bf16[2,4,16,16,256]{4,3,2,1,0:T(8,128)(2,1)}, bf16[2,4,16,16,256]{4,3,2,1,0:T(8,128)(2,1)S(1)}, u32[]{:S(2)}) copy-start(bf16[2,4,16,16,256]{4,3,2,1,0:T(8,128)(2,1)S(1)} %pad_maximum_fusion.x0) | copy-start | bytes 3145732
  68.1 7.7 %collective-permute-start.16 = (bf16[2,4,16,16,256]{4,3,2,1,0:T(8,128)(2,1)}, bf16[2,4,16,16,256]{4,3,2,1,0:T(8,128)(2,1)}, u32[]{:S(2)}, u32[]{:S(2)}) collective-permute-start(bf16[2,4,16,16,256]{4,3,2,1,0:T(8,128)(2,1)} %pad_maximum_fusion.2), channel_id=1, source_target_pairs={{0,8},{1,9},{2,10},{3,11},{4,12},{5,13},{6,14},{7,15},{8,0},{9,1},... | collective-permute-start | bytes 3145736 | tf_op jit(solution)/shard_map/ppermute | solution.py:28
  70.7 5.2 %collective-permute-start.14 = (bf16[2,4,16,16,256]{4,3,2,1,0:T(8,128)(2,1)S(1)}, bf16[2,4,16,16,256]{4,3,2,1,0:T(8,128)(2,1)}, u32[]{:S(2)}, u32[]{:S(2)}) collective-permute-start(bf16[2,4,16,16,256]{4,3,2,1,0:T(8,128)(2,1)S(1)} %pad_maximum_fusion.1.x1), channel_id=1, source_target_pairs={{0,8},{1,9},{2,10},{3,11},{4,12},{5,13},{6,14},{7,15},{8,0},{9,1},... | collective-permute-start | bytes 3145736 | tf_op jit(solution)/shard_map/ppermute | solution.py:28
  70.7 5.2 %collective-permute-start.13 = (bf16[2,4,16,16,256]{4,3,2,1,0:T(8,128)(2,1)S(1)}, bf16[2,4,16,16,256]{4,3,2,1,0:T(8,128)(2,1)}, u32[]{:S(2)}, u32[]{:S(2)}) collective-permute-start(bf16[2,4,16,16,256]{4,3,2,1,0:T(8,128)(2,1)S(1)} %pad_maximum_fusion.x0), channel_id=1, source_target_pairs={{0,8},{1,9},{2,10},{3,11},{4,12},{5,13},{6,14},{7,15},{8,0},{9,1},... | collective-permute-start | bytes 3145736 | tf_op jit(solution)/shard_map/ppermute | solution.py:28
  71.2 13.5 %collective-permute-start.19 = (bf16[512,768]{1,0:T(8,128)(2,1)}, bf16[512,768]{1,0:T(8,128)(2,1)S(1)}, u32[]{:S(2)}, u32[]{:S(2)}) collective-permute-start(bf16[512,768]{1,0:T(8,128)(2,1)} %collective-permute-done.8.a1), channel_id=1, source_target_pairs={{0,2},{1,3},{2,4},{3,5},{4,6},{5,7},{6,0},{7,1},{8,14},{9,15},{10,... | collective-permute-start | bytes 2359304 | tf_op jit(solution)/shard_map/ppermute | solution.py:28
  72.1 7.5 %collective-permute-start.18 = (bf16[4,16,16,256]{3,2,1,0:T(8,128)(2,1)S(1)}, bf16[4,16,16,256]{3,2,1,0:T(8,128)(2,1)S(1)}, u32[]{:S(2)}, u32[]{:S(2)}) collective-permute-start(bf16[4,16,16,256]{3,2,1,0:T(8,128)(2,1)S(1)} %collective-permute-done.17.r3), channel_id=1, source_target_pairs={{0,8},{1,9},{2,10},{3,11},{4,12},{5,13},{6,14},{7,15},{8,0},{9,1},... | collective-permute-start | bytes 1572872 | tf_op jit(solution)/shard_map/ppermute | solution.py:28
  84.7 18.5 %copy-start.8 = (f32[4,16,256]{2,1,0:T(8,128)S(1)}, f32[4,16,256]{2,1,0:T(8,128)}, u32[]{:S(2)}) copy-start(f32[4,16,256]{2,1,0:T(8,128)} %param.12) | copy-start | bytes 196612
  87.3 1.6 %collective-permute-start.20 = (bf16[8,4,16,256]{3,2,1,0:T(8,128)(2,1)S(1)}, bf16[8,4,16,256]{3,2,1,0:T(8,128)(2,1)S(1)}, u32[]{:S(2)}, u32[]{:S(2)}) collective-permute-start(bf16[8,4,16,256]{3,2,1,0:T(8,128)(2,1)S(1)} %get-tuple-element.41), channel_id=1, source_target_pairs={{0,8},{1,9},{2,10},{3,11},{4,12},{5,13},{6,14},{7,15},{8,0},{9,1},... | collective-permute-start | bytes 786440 | tf_op jit(solution)/shard_map/ppermute | solution.py:28
  89.1 7.1 %collective-permute-start.21 = (bf16[4,4,16,256]{3,2,1,0:T(8,128)(2,1)S(1)}, bf16[4,4,16,256]{3,2,1,0:T(8,128)(2,1)S(1)}, u32[]{:S(2)}, u32[]{:S(2)}) collective-permute-start(bf16[4,4,16,256]{3,2,1,0:T(8,128)(2,1)S(1)} %fusion), channel_id=1, source_target_pairs={{0,16},{1,17},{2,18},{3,19},{4,20},{5,21},{6,22},{7,23},{8,24},{9,... | collective-permute-start | bytes 393224 | tf_op jit(solution)/shard_map/ppermute | solution.py:28
  96.3 5.5 %collective-permute-start.22 = (bf16[4,16,256]{2,1,0:T(8,128)(2,1)S(1)}, bf16[4,16,256]{2,1,0:T(8,128)(2,1)S(1)}, u32[]{:S(2)}, u32[]{:S(2)}) collective-permute-start(bf16[4,16,256]{2,1,0:T(8,128)(2,1)S(1)} %get-tuple-element.46), channel_id=1, source_target_pairs={{0,64},{1,65},{2,66},{3,67},{4,68},{5,69},{6,70},{7,71},{8,72},{9,... | collective-permute-start | bytes 98312 | tf_op jit(solution)/shard_map/ppermute | solution.py:28
  97.9 5.1 %collective-permute-start.23 = (bf16[4,16,256]{2,1,0:T(8,128)(2,1)S(1)}, bf16[4,16,256]{2,1,0:T(8,128)(2,1)S(1)}, u32[]{:S(2)}, u32[]{:S(2)}) collective-permute-start(bf16[4,16,256]{2,1,0:T(8,128)(2,1)S(1)} %get-tuple-element.48), channel_id=1, source_target_pairs={{0,32},{1,33},{2,34},{3,35},{4,36},{5,37},{6,38},{7,39},{8,40},{9,... | collective-permute-start | bytes 98312 | tf_op jit(solution)/shard_map/ppermute | solution.py:28
  99.3 3.9 %collective-permute-start.24 = (bf16[4,16,256]{2,1,0:T(8,128)(2,1)S(1)}, bf16[4,16,256]{2,1,0:T(8,128)(2,1)S(1)}, u32[]{:S(2)}, u32[]{:S(2)}) collective-permute-start(bf16[4,16,256]{2,1,0:T(8,128)(2,1)S(1)} %get-tuple-element.47), channel_id=1, source_target_pairs={{0,96},{1,97},{2,98},{3,99},{4,100},{5,101},{6,102},{7,103},{8,104... | collective-permute-start | bytes 98312 | tf_op jit(solution)/shard_map/ppermute | solution.py:28

commit v6 on v4

--- a/solution.py
+++ b/solution.py
@@ -83,7 +83,8 @@
     return [src.at[:, pl.ds(j * B, B)] for j in range(count)]
 
 
-def hold_kernel(s, p1, p2, p3, sw, a1, a2, far, sv, sem):
+def hold_kernel(s, p1, p2, p3, sw, a1, a2, far, sv, done, sem):
+    done[...] = jnp.zeros_like(done)
     parts = []
     for src in (s, p1, p2, p3, sw):
         parts += columns(src, 4)
@@ -112,7 +113,7 @@
     return jnp.dot(left, right, preferred_element_type=jnp.float32)
 
 
-def main_kernel(slot_ref, block_ref, place_ref, sv, lv_in, r3, t3, lv, acc, sem):
+def main_kernel(slot_ref, block_ref, place_ref, sv, lv_in, r3, t3, done, lv, acc, sem):
     start_wait(row_copies([r3, t3], 14, place_ref, lv, sem))
     for k in range(SUP):
         acc[k] = product(slot_ref, block_ref, k, 0, EARLY, sv, lv)
@@ -204,13 +205,9 @@
     t2 = swap_core(jnp.stack([r1, r2]))
     a1, a2, far = tie(a1, a2, far)
     a3 = z_first(a1)
-    t3 = swap_core(r3)
-    s, p1, p2, p3, sw, a1, a2, far = in_hbm(s, p1, p2, p3, sw, a1, a2, far)
+    s, p1, p2, p3, sw = in_hbm(s, p1, p2, p3, sw)
+    a1, a2, far = [pltpu.with_memory_space_constraint(v, pltpu.VMEM) for v in (a1, a2, far)]
     a3 = pltpu.with_memory_space_constraint(a3, pltpu.VMEM)
-    lh, r1, r2, x0, x1 = in_hbm(lh, r1, r2, x0, x1)
-    t0, tx0, tx1, t2 = in_hbm(t0, tx0, tx1, t2)
-    r3, t3 = [pltpu.with_memory_space_constraint(v, pltpu.VMEM) for v in (r3, t3)]
-
     hbm = pl.BlockSpec(memory_space=pltpu.HBM)
     smem = pl.BlockSpec(memory_space=pltpu.SMEM)
     vmem = pl.BlockSpec(memory_space=pltpu.VMEM)
@@ -218,14 +215,20 @@
     panel_shape = pltpu.VMEM((SUP, NR, B, B), jnp.bfloat16)
     held_shape = pltpu.VMEM((NA, ROWS, B), jnp.bfloat16)
     acc_shape = pltpu.VMEM((SUP, ROWS, B), jnp.float32)
-    held = pl.pallas_call(
+    held, done = pl.pallas_call(
         hold_kernel,
-        out_shape=held_shape,
-        in_specs=[hbm] * 8,
-        out_specs=vmem,
+        out_shape=(held_shape, jax.ShapeDtypeStruct((8, 128), jnp.float32)),
+        in_specs=[hbm] * 5 + [vmem] * 3,
+        out_specs=(vmem, vmem),
         scratch_shapes=[pltpu.SemaphoreType.DMA((29,))],
         compiler_params=params,
     )(s, p1, p2, p3, sw, a1, a2, far)
+    r3, done = tie(r3, done)
+    t3 = swap_core(r3)
+    lh, r1, r2, x0, x1 = in_hbm(lh, r1, r2, x0, x1)
+    t0, tx0, tx1, t2 = in_hbm(t0, tx0, tx1, t2)
+    r3, t3 = [pltpu.with_memory_space_constraint(v, pltpu.VMEM) for v in (r3, t3)]
+
     blocks = pl.pallas_call(
         panel_kernel,
         out_shape=panel_shape,
@@ -238,12 +241,12 @@
     blocks, acc = pl.pallas_call(
         main_kernel,
         out_shape=(panel_shape, acc_shape),
-        in_specs=[smem] * 3 + [vmem] * 4,
+        in_specs=[smem] * 3 + [vmem] * 5,
         out_specs=(vmem, vmem),
         input_output_aliases={4: 0},
         scratch_shapes=[pltpu.SemaphoreType.DMA((2,))],
         compiler_params=params,
-    )(sorted_slots, sorted_blocks, place, held, blocks, r3, t3)
+    )(sorted_slots, sorted_blocks, place, held, blocks, r3, t3, done)
     blocks, acc = [pltpu.with_memory_space_constraint(v, pltpu.VMEM) for v in (blocks, acc)]
     sigma_off, keep, send, _ = pl.pallas_call(
         late_kernel,

time: 103 us -> 103 us (level)
  waiting for transfers between devices: 40.5 us -> 37.6 us
  other arithmetic: 7.57 us -> 9.97 us
  starting transfers between devices: 24.9 us -> 26.1 us
    ppermute x21, waiting for transfers between devices: 40.5 us -> 37.6 us  [permute(): return lax.ppermute(x, AXES, pairs)]
    another operation x1, other arithmetic: 0.1 us -> 2.29 us  [per_device(): x1 = jnp.stack([q2, q3])]
    ppermute x21, starting transfers between devices: 24.9 us -> 26.1 us  [permute(): return lax.ppermute(x, AXES, pairs)]
  transfers between devices with their start and end apart: 21 -> 21, of which waited for: 10 -> 9; matrix products, arithmetic and copies ran while one was open for 8% -> 10% of each run, Pallas kernels for 11% -> 11%
where the time goes in v6:
time: 103 us
  waiting for transfers between devices  37.6 us (37%)
  starting transfers between devices  26.1 us (25%)
  Pallas kernels  14.1 us (14%)
  blocking collectives  12.5 us (12%)
  other arithmetic  9.97 us (10%)
  local copies, waits for them, and re-layouts  1.47 us (1%)
    ppermute x21, waiting for transfers between devices, permute(): return lax.ppermute(x, AXES, pairs)  37.6 us
    ppermute x21, starting transfers between devices, permute(): return lax.ppermute(x, AXES, pairs)  26.1 us
    all_to_all x1, blocking collectives, per_device(): lax.all_to_all(halves, 'prow', split_axis=0, concat_axis=0, tiled=True, a...  12.5 us
    pallas_call x1, Pallas kernels, per_device(): pl.pallas_call(main_kernel, out_shape=(panel_shape, acc_shape), in_specs=...  4.92 us
    pallas_call x1, Pallas kernels, per_device(): pl.pallas_call(panel_kernel, out_shape=panel_shape, in_specs=[smem] + [hb...  3.75 us
    pallas_call x1, Pallas kernels, per_device(): pl.pallas_call(hold_kernel, out_shape=(held_shape, jax.ShapeDtypeStruct((...  2.81 us
    pallas_call x1, Pallas kernels, per_device(): pl.pallas_call(late_kernel, out_shape=(jax.ShapeDtypeStruct((ROWS, SUP *...  2.64 us
    another operation x1, other arithmetic, per_device(): x1 = jnp.stack([q2, q3])  2.29 us
  transfers between devices with their start and end apart: 21, of which 9 were waited for; matrix products, arithmetic and copies ran while one was open for 10% of the time, Pallas kernels for 11%

profile of v6, /device:TPU:0, one launch (start us, length us, event | category | flops | bytes accessed | tf_op | source)
XLA Modules:
  0.0 102.6 jit_solution(1940632022350446674)
XLA Ops:
  0.6 0.0 copy-start
  0.6 2.1 %collective-permute-start = (bf16[512,1024]{1,0:T(8,128)(2,1)}, bf16[512,1024]{1,0:T(8,128)(2,1)S(1)}, u32[]{:S(2)}, u32[]{:S(2)}) collective-permute-start(bf16[512,1024]{1,0:T(8,128)(2,1)} %s.1), channel_id=1, source_target_pairs={{0,2},{1,3},{2,4},{3,5},{4,6},{5,7},{6,0},{7,1},{8,14},{9,15},{10,... | collective-permute-start | bytes 3145736 | tf_op jit(solution)/shard_map/ppermute | solution.py:28
  2.7 3.0 %collective-permute-start.2 = (bf16[4,16,16,256]{3,2,1,0:T(8,128)(2,1)}, bf16[4,16,16,256]{3,2,1,0:T(8,128)(2,1)}, u32[]{:S(2)}, u32[]{:S(2)}) collective-permute-start(bf16[4,16,16,256]{3,2,1,0:T(8,128)(2,1)} %param.9), channel_id=1, source_target_pairs={{0,96},{1,97},{2,98},{3,99},{4,100},{5,101},{6,102},{7,103},{8,40}... | collective-permute-start | bytes 1572872 | tf_op jit(solution)/shard_map/ppermute | solution.py:28
  5.7 0.0 collective-permute-start.1
  5.7 1.5 %collective-permute-start.5 = (bf16[512,1024]{1,0:T(8,128)(2,1)}, bf16[512,1024]{1,0:T(8,128)(2,1)S(1)}, u32[]{:S(2)}, u32[]{:S(2)}) collective-permute-start(bf16[512,1024]{1,0:T(8,128)(2,1)} %s.1), channel_id=1, source_target_pairs={{0,1},{1,0},{2,3},{3,2},{4,5},{5,4},{6,7},{7,6},{8,9},{9,8},{10,11... | collective-permute-start | bytes 3145736 | tf_op jit(solution)/shard_map/ppermute | solution.py:28
  7.2 2.2 %collective-permute-start.3 = (bf16[512,1024]{1,0:T(8,128)(2,1)}, bf16[512,1024]{1,0:T(8,128)(2,1)S(1)}, u32[]{:S(2)}, u32[]{:S(2)}) collective-permute-start(bf16[512,1024]{1,0:T(8,128)(2,1)} %s.1), channel_id=1, source_target_pairs={{0,6},{1,7},{2,0},{3,1},{4,2},{5,3},{6,4},{7,5},{8,10},{9,11},{10,... | collective-permute-start | bytes 3145736 | tf_op jit(solution)/shard_map/ppermute | solution.py:28
  9.4 8.3 %collective-permute-done.2 = bf16[4,16,16,256]{3,2,1,0:T(8,128)(2,1)} collective-permute-done((bf16[4,16,16,256]{3,2,1,0:T(8,128)(2,1)}, bf16[4,16,16,256]{3,2,1,0:T(8,128)(2,1)}, u32[]{:S(2)}, u32[]{:S(2)}) %collective-permute-start.2) | collective-permute-done | bytes 524320 | tf_op jit(solution)/shard_map/ppermute | solution.py:28
  17.7 2.0 %collective-permute-done.1 = bf16[4,16,16,256]{3,2,1,0:T(8,128)(2,1)S(1)} collective-permute-done((bf16[4,16,16,256]{3,2,1,0:T(8,128)(2,1)}, bf16[4,16,16,256]{3,2,1,0:T(8,128)(2,1)S(1)}, u32[]{:S(2)}, u32[]{:S(2)}) %collective-permute-start.1) | collective-permute-done | bytes 524320 | tf_op jit(solution)/shard_map/ppermute | solution.py:28
  19.7 3.5 %collective-permute-done.p1 = bf16[512,1024]{1,0:T(8,128)(2,1)S(1)} collective-permute-done((bf16[512,1024]{1,0:T(8,128)(2,1)}, bf16[512,1024]{1,0:T(8,128)(2,1)S(1)}, u32[]{:S(2)}, u32[]{:S(2)}) %collective-permute-start) | collective-permute-done | bytes 1048608 | tf_op jit(solution)/shard_map/ppermute | solution.py:28
  23.2 2.2 %collective-permute-start.4 = (bf16[512,1024]{1,0:T(8,128)(2,1)S(1)}, bf16[512,1024]{1,0:T(8,128)(2,1)S(1)}, u32[]{:S(2)}, u32[]{:S(2)}) collective-permute-start(bf16[512,1024]{1,0:T(8,128)(2,1)S(1)} %collective-permute-done.p1), channel_id=1, source_target_pairs={{0,2},{1,3},{2,4},{3,5},{4,6},{5,7},{6,0},{7,1},{8,14},{9,15},{10,... | collective-permute-start | bytes 3145736 | tf_op jit(solution)/shard_map/ppermute | solution.py:28
  25.5 3.3 %collective-permute-start.6 = (bf16[4,16,16,256]{3,2,1,0:T(8,128)(2,1)}, bf16[4,16,16,256]{3,2,1,0:T(8,128)(2,1)}, u32[]{:S(2)}, u32[]{:S(2)}) collective-permute-start(bf16[4,16,16,256]{3,2,1,0:T(8,128)(2,1)} %param.9), channel_id=1, source_target_pairs={{0,16},{1,17},{2,18},{3,19},{4,20},{5,21},{6,22},{7,23},{8,24},{9,... | collective-permute-start | bytes 1572872 | tf_op jit(solution)/shard_map/ppermute | solution.py:28
  28.8 2.9 %collective-permute-start.7 = (bf16[4,16,16,256]{3,2,1,0:T(8,128)(2,1)S(1)}, bf16[4,16,16,256]{3,2,1,0:T(8,128)(2,1)}, u32[]{:S(2)}, u32[]{:S(2)}) collective-permute-start(bf16[4,16,16,256]{3,2,1,0:T(8,128)(2,1)S(1)} %collective-permute-done.1), channel_id=1, source_target_pairs={{0,32},{1,33},{2,34},{3,35},{4,36},{5,37},{6,38},{7,39},{8,104},{9... | collective-permute-start | bytes 1572872 | tf_op jit(solution)/shard_map/ppermute | solution.py:28
  31.7 0.0 collective-permute-done.5.sw
  31.7 1.1 %slice.16 = bf16[512,768]{1,0:T(8,128)(2,1)} slice(bf16[512,1024]{1,0:T(8,128)(2,1)S(1)} %collective-permute-done.5.sw), slice={[0:512], [0:768]} | slice | bytes 1572864 | tf_op jit(solution)/shard_map/slice | solution.py:185
  32.8 0.0 copy-start.8
  32.8 0.0 copy-start.9
  32.9 0.0 copy-start.10
  32.9 12.3 %collective-permute-done.6.lh = bf16[4,16,16,256]{3,2,1,0:T(8,128)(2,1)} collective-permute-done((bf16[4,16,16,256]{3,2,1,0:T(8,128)(2,1)}, bf16[4,16,16,256]{3,2,1,0:T(8,128)(2,1)}, u32[]{:S(2)}, u32[]{:S(2)}) %collective-permute-start.6) | collective-permute-done | bytes 524320 | tf_op jit(solution)/shard_map/ppermute | solution.py:28
  45.2 0.0 collective-permute-done.3.p2
  45.2 0.0 collective-permute-done.7
  45.2 0.0 collective-permute-done.4.p3
  45.2 2.6 %collective-permute-start.12 = (bf16[4,16,16,256]{3,2,1,0:T(8,128)(2,1)}, bf16[4,16,16,256]{3,2,1,0:T(8,128)(2,1)S(1)}, u32[]{:S(2)}, u32[]{:S(2)}) collective-permute-start(bf16[4,16,16,256]{3,2,1,0:T(8,128)(2,1)} %collective-permute-done.6.lh), channel_id=1, source_target_pairs={{0,96},{1,97},{2,98},{3,99},{4,100},{5,101},{6,102},{7,103},{8,40}... | collective-permute-start | bytes 1572872 | tf_op jit(solution)/shard_map/ppermute | solution.py:28
  47.8 0.0 collective-permute-start.11
  47.8 0.1 slice_bitcast_fusion
  47.9 1.0 pad_maximum_fusion.3
  48.8 0.2 collective-permute-start.10
  49.1 1.7 %collective-permute-start.9 = (bf16[512,768]{1,0:T(8,128)(2,1)}, bf16[512,768]{1,0:T(8,128)(2,1)S(1)}, u32[]{:S(2)}, u32[]{:S(2)}) collective-permute-start(bf16[512,768]{1,0:T(8,128)(2,1)} %slice.16), channel_id=1, source_target_pairs={{0,6},{1,7},{2,0},{3,1},{4,2},{5,3},{6,4},{7,5},{8,10},{9,11},{10,... | collective-permute-start | bytes 2359304 | tf_op jit(solution)/shard_map/ppermute | solution.py:28
  50.8 0.3 collective-permute-start.8
  51.1 0.1 constant_dynamic-slice_fusion
  51.2 0.1 copy.13
  51.3 0.9 select_reduce_fusion.2
  52.1 7.9 %collective-permute-done.12.r2 = bf16[4,16,16,256]{3,2,1,0:T(8,128)(2,1)S(1)} collective-permute-done((bf16[4,16,16,256]{3,2,1,0:T(8,128)(2,1)}, bf16[4,16,16,256]{3,2,1,0:T(8,128)(2,1)S(1)}, u32[]{:S(2)}, u32[]{:S(2)}) %collective-permute-start.12) | collective-permute-done | bytes 524320 | tf_op jit(solution)/shard_map/ppermute | solution.py:28
  60.1 0.0 collective-permute-start.15
  60.1 0.7 collective-permute-done.11.r1
  60.8 0.0 collective-permute-start.17
  60.8 2.3 %pad_maximum_fusion.1.x1 = bf16[2,4,16,16,256]{4,3,2,1,0:T(8,128)(2,1)} fusion(bf16[1,4,16,16,256]{4,3,2,1,0:T(8,128)(2,1)} %bitcast.7, bf16[1,4,16,16,256]{4,3,2,1,0:T(8,128)(2,1)} %bitcast.6), kind=kLoop, calls=%fused_computation.1 | loop fusion | flops 524288 | bytes 2097152 | tf_op jit(solution)/shard_map/stack | solution.py:201
  63.1 2.3 %pad_maximum_fusion.x0 = bf16[2,4,16,16,256]{4,3,2,1,0:T(8,128)(2,1)} fusion(bf16[1,4,16,16,256]{4,3,2,1,0:T(8,128)(2,1)} %bitcast.15, bf16[1,4,16,16,256]{4,3,2,1,0:T(8,128)(2,1)} %bitcast.14), kind=kLoop, calls=%fused_computation | loop fusion | flops 524288 | bytes 2097152 | tf_op jit(solution)/shard_map/stack | solution.py:200
  65.4 2.2 %pad_maximum_fusion.2 = bf16[2,4,16,16,256]{4,3,2,1,0:T(8,128)(2,1)} fusion(bf16[1,4,16,16,256]{4,3,2,1,0:T(8,128)(2,1)S(1)} %bitcast.13, bf16[1,4,16,16,256]{4,3,2,1,0:T(8,128)(2,1)} %bitcast.8), kind=kLoop, calls=%fused_computation.2 | loop fusion | flops 524288 | bytes 2097152 | tf_op jit(solution)/shard_map/stack | solution.py:205
  67.5 1.3 %collective-permute-done.10.far = bf16[3,512,256]{2,1,0:T(8,128)(2,1)S(1)} collective-permute-done((bf16[3,512,256]{2,1,0:T(8,128)(2,1)}, bf16[3,512,256]{2,1,0:T(8,128)(2,1)S(1)}, u32[]{:S(2)}, u32[]{:S(2)}) %collective-permute-start.10) | collective-permute-done | bytes 786464 | tf_op jit(solution)/shard_map/ppermute | solution.py:28
  68.8 1.8 %collective-permute-start.16 = (bf16[2,4,16,16,256]{4,3,2,1,0:T(8,128)(2,1)}, bf16[2,4,16,16,256]{4,3,2,1,0:T(8,128)(2,1)}, u32[]{:S(2)}, u32[]{:S(2)}) collective-permute-start(bf16[2,4,16,16,256]{4,3,2,1,0:T(8,128)(2,1)} %pad_maximum_fusion.2), channel_id=1, source_target_pairs={{0,8},{1,9},{2,10},{3,11},{4,12},{5,13},{6,14},{7,15},{8,0},{9,1},... | collective-permute-start | bytes 3145736 | tf_op jit(solution)/shard_map/ppermute | solution.py:28
  70.6 0.0 collective-permute-done.9.a2
  70.6 0.1 collective-permute-start.13
  70.7 0.0 collective-permute-done.8.a1
  70.7 0.4 collective-permute-start.14
  71.2 0.3 collective-permute-done.17.r3
  71.5 0.0 collective-permute-start.19
  71.5 0.2 select_reduce_fusion.3
  71.7 0.1 copy.14
  71.8 0.2 convert_reduce_fusion.1
  72.0 2.8 %shard_map.95 = (bf16[32,512,256]{2,1,0:T(8,128)(2,1)S(1)}, f32[8,128]{1,0:T(8,128)S(1)}) custom-call(bf16[512,1024]{1,0:T(8,128)(2,1)} %s.1, bf16[512,1024]{1,0:T(8,128)(2,1)} %copy-done.3, bf16[512,1024]{1,0:T(8,128)(2,1)} %copy-done.4, bf16[512,1024]{1,0:T(8,128)(2,1)} %copy-done.5, bf16[512,1024]{1,0:T(8,128)(2,1)} %copy-done.1, ...), custom_call_target="tpu_custom_call" | custom-call | tf_op jit(solution)/shard_map/pallas_call | solution.py:218
  74.8 1.3 %collective-permute-start.18 = (bf16[4,16,16,256]{3,2,1,0:T(8,128)(2,1)}, bf16[4,16,16,256]{3,2,1,0:T(8,128)(2,1)S(1)}, u32[]{:S(2)}, u32[]{:S(2)}) collective-permute-start(bf16[4,16,16,256]{3,2,1,0:T(8,128)(2,1)} %collective-permute-done.17.r3), channel_id=1, source_target_pairs={{0,8},{1,9},{2,10},{3,11},{4,12},{5,13},{6,14},{7,15},{8,0},{9,1},... | collective-permute-start | bytes 1572872 | tf_op jit(solution)/shard_map/ppermute | solution.py:28
  76.2 0.1 select_reduce_fusion
  76.3 0.0 collective-permute-done.16.t2
  76.4 0.0 collective-permute-done.13.tx0
  76.4 3.7 %shard_map.96.lv_in = bf16[4,16,256,256]{3,2,1,0:T(8,128)(2,1)S(1)} custom-call(s32[16]{0:T(128)S(1)} %fusion.13.place_ref, bf16[2,4,16,16,256]{4,3,2,1,0:T(8,128)(2,1)} %pad_maximum_fusion.x0, bf16[2,4,16,16,256]{4,3,2,1,0:T(8,128)(2,1)} %pad_maximum_fusion.1.x1, bf16[4,16,16,256]{3,2,1,0:T(8,128)(2,1)} %collective-permute-done.6.lh, ...), custom_call_target="tpu_custom_call" | custom-call | tf_op jit(solution)/shard_map/pallas_call | solution.py:232
  80.1 4.9 %shard_map.97 = (bf16[4,16,256,256]{3,2,1,0:T(8,128)(2,1)S(1)}, f32[4,512,256]{2,1,0:T(8,128)S(1)}) custom-call(s32[4,16]{1,0:T(4,128)S(1)} %get-tuple-element.51.slot_ref, s32[4,16]{1,0:T(4,128)S(1)} %get-tuple-element.50.block_ref, s32[16]{0:T(128)S(1)} %fusion.13.place_ref, ...), custom_call_target="tpu_custom_call", output_to_operand_aliasing={{0}: (4, {})} | custom-call | tf_op jit(solution)/shard_map/pallas_call | solution.py:241
  85.1 0.0 collective-permute-done.19.a3
  85.1 0.0 copy-start.7
  85.1 2.6 %shard_map.98 = (bf16[512,1024]{1,0:T(8,128)(2,1)}, f32[8,4,16,256]{3,2,1,0:T(8,128)S(1)}, bf16[8,4,16,256]{3,2,1,0:T(8,128)(2,1)S(1)}, bf16[32,512,256]{2,1,0:T(8,128)(2,1)S(1)}) custom-call(s32[4,16]{1,0:T(4,128)S(1)} %get-tuple-element.51.slot_ref, s32[4,16]{1,0:T(4,128)S(1)} %get-tuple-element.50.block_ref, ...), custom_call_target="tpu_custom_call", output_to_operand_aliasing={{3}: (4, {})} | custom-call | tf_op jit(solution)/shard_map/pallas_call | solution.py:251
  87.7 0.3 collective-permute-start.20
  88.1 1.3 %collective-permute-done.20 = bf16[8,4,16,256]{3,2,1,0:T(8,128)(2,1)S(1)} collective-permute-done((bf16[8,4,16,256]{3,2,1,0:T(8,128)(2,1)S(1)}, bf16[8,4,16,256]{3,2,1,0:T(8,128)(2,1)S(1)}, u32[]{:S(2)}, u32[]{:S(2)}) %collective-permute-start.20) | collective-permute-done | bytes 262176 | tf_op jit(solution)/shard_map/ppermute | solution.py:28
  89.4 0.1 add_convert_fusion
  89.4 12.5 %all_to_all.5 = bf16[8,4,16,256]{3,2,1,0:T(8,128)(2,1)S(1)} all-to-all(bf16[8,4,16,256]{3,2,1,0:T(8,128)(2,1)S(1)} %add_convert_fusion), channel_id=1, replica_groups={{0,16,32,48,64,80,96,112},{8,24,40,56,72,88,104,120},{1,17,33,49,65,81,..., dimensions={0} | all-to-all | bytes 524288 | tf_op jit(solution)/shard_map/all_to_all | solution.py:271
  102.0 0.6 sub.52
  (27 shorter events, 0.2 us)
Async XLA Ops:
  0.6 50.5 %copy-start = (s32[32,16]{0,1:T(8,128)S(1)}, s32[32,16]{0,1:T(8,128)}, u32[]{:S(2)}) copy-start(s32[32,16]{0,1:T(8,128)} %param.10) | copy-start | bytes 6148
  0.6 22.6 %collective-permute-start = (bf16[512,1024]{1,0:T(8,128)(2,1)}, bf16[512,1024]{1,0:T(8,128)(2,1)S(1)}, u32[]{:S(2)}, u32[]{:S(2)}) collective-permute-start(bf16[512,1024]{1,0:T(8,128)(2,1)} %s.1), channel_id=1, source_target_pairs={{0,2},{1,3},{2,4},{3,5},{4,6},{5,7},{6,0},{7,1},{8,14},{9,15},{10,... | collective-permute-start | bytes 3145736 | tf_op jit(solution)/shard_map/ppermute | solution.py:28
  2.7 15.0 %collective-permute-start.2 = (bf16[4,16,16,256]{3,2,1,0:T(8,128)(2,1)}, bf16[4,16,16,256]{3,2,1,0:T(8,128)(2,1)}, u32[]{:S(2)}, u32[]{:S(2)}) collective-permute-start(bf16[4,16,16,256]{3,2,1,0:T(8,128)(2,1)} %param.9), channel_id=1, source_target_pairs={{0,96},{1,97},{2,98},{3,99},{4,100},{5,101},{6,102},{7,103},{8,40}... | collective-permute-start | bytes 1572872 | tf_op jit(solution)/shard_map/ppermute | solution.py:28
  5.7 14.0 %collective-permute-start.1 = (bf16[4,16,16,256]{3,2,1,0:T(8,128)(2,1)}, bf16[4,16,16,256]{3,2,1,0:T(8,128)(2,1)S(1)}, u32[]{:S(2)}, u32[]{:S(2)}) collective-permute-start(bf16[4,16,16,256]{3,2,1,0:T(8,128)(2,1)} %param.9), channel_id=1, source_target_pairs={{0,32},{1,33},{2,34},{3,35},{4,36},{5,37},{6,38},{7,39},{8,104},{9... | collective-permute-start | bytes 1572872 | tf_op jit(solution)/shard_map/ppermute | solution.py:28
  5.7 26.0 %collective-permute-start.5 = (bf16[512,1024]{1,0:T(8,128)(2,1)}, bf16[512,1024]{1,0:T(8,128)(2,1)S(1)}, u32[]{:S(2)}, u32[]{:S(2)}) collective-permute-start(bf16[512,1024]{1,0:T(8,128)(2,1)} %s.1), channel_id=1, source_target_pairs={{0,1},{1,0},{2,3},{3,2},{4,5},{5,4},{6,7},{7,6},{8,9},{9,8},{10,11... | collective-permute-start | bytes 3145736 | tf_op jit(solution)/shard_map/ppermute | solution.py:28
  7.2 37.9 %collective-permute-start.3 = (bf16[512,1024]{1,0:T(8,128)(2,1)}, bf16[512,1024]{1,0:T(8,128)(2,1)S(1)}, u32[]{:S(2)}, u32[]{:S(2)}) collective-permute-start(bf16[512,1024]{1,0:T(8,128)(2,1)} %s.1), channel_id=1, source_target_pairs={{0,6},{1,7},{2,0},{3,1},{4,2},{5,3},{6,4},{7,5},{8,10},{9,11},{10,... | collective-permute-start | bytes 3145736 | tf_op jit(solution)/shard_map/ppermute | solution.py:28
  19.7 28.1 %copy-start.6 = (bf16[4,16,16,256]{3,2,1,0:T(8,128)(2,1)}, bf16[4,16,16,256]{3,2,1,0:T(8,128)(2,1)S(1)}, u32[]{:S(2)}) copy-start(bf16[4,16,16,256]{3,2,1,0:T(8,128)(2,1)S(1)} %collective-permute-done.1) | copy-start | bytes 1572868
  23.2 27.6 %copy-start.3 = (bf16[512,1024]{1,0:T(8,128)(2,1)}, bf16[512,1024]{1,0:T(8,128)(2,1)S(1)}, u32[]{:S(2)}) copy-start(bf16[512,1024]{1,0:T(8,128)(2,1)S(1)} %collective-permute-done.p1) | copy-start | bytes 3145732
  23.2 21.9 %collective-permute-start.4 = (bf16[512,1024]{1,0:T(8,128)(2,1)S(1)}, bf16[512,1024]{1,0:T(8,128)(2,1)S(1)}, u32[]{:S(2)}, u32[]{:S(2)}) collective-permute-start(bf16[512,1024]{1,0:T(8,128)(2,1)S(1)} %collective-permute-done.p1), channel_id=1, source_target_pairs={{0,2},{1,3},{2,4},{3,5},{4,6},{5,7},{6,0},{7,1},{8,14},{9,15},{10,... | collective-permute-start | bytes 3145736 | tf_op jit(solution)/shard_map/ppermute | solution.py:28
  25.5 19.7 %collective-permute-start.6 = (bf16[4,16,16,256]{3,2,1,0:T(8,128)(2,1)}, bf16[4,16,16,256]{3,2,1,0:T(8,128)(2,1)}, u32[]{:S(2)}, u32[]{:S(2)}) collective-permute-start(bf16[4,16,16,256]{3,2,1,0:T(8,128)(2,1)} %param.9), channel_id=1, source_target_pairs={{0,16},{1,17},{2,18},{3,19},{4,20},{5,21},{6,22},{7,23},{8,24},{9,... | collective-permute-start | bytes 1572872 | tf_op jit(solution)/shard_map/ppermute | solution.py:28
  28.8 16.4 %collective-permute-start.7 = (bf16[4,16,16,256]{3,2,1,0:T(8,128)(2,1)S(1)}, bf16[4,16,16,256]{3,2,1,0:T(8,128)(2,1)}, u32[]{:S(2)}, u32[]{:S(2)}) collective-permute-start(bf16[4,16,16,256]{3,2,1,0:T(8,128)(2,1)S(1)} %collective-permute-done.1), channel_id=1, source_target_pairs={{0,32},{1,33},{2,34},{3,35},{4,36},{5,37},{6,38},{7,39},{8,104},{9... | collective-permute-start | bytes 1572872 | tf_op jit(solution)/shard_map/ppermute | solution.py:28
  31.7 17.3 %copy-start.1 = (bf16[512,1024]{1,0:T(8,128)(2,1)}, bf16[512,1024]{1,0:T(8,128)(2,1)S(1)}, u32[]{:S(2)}) copy-start(bf16[512,1024]{1,0:T(8,128)(2,1)S(1)} %collective-permute-done.5.sw) | copy-start | bytes 3145732
  32.8 43.4 %copy-start.8 = (s32[16]{0:T(128)S(1)}, s32[16]{0:T(128)}, u32[]{:S(2)}) copy-start(s32[16]{0:T(128)} %constant.159.clone) | copy-start | bytes 196
  32.8 43.4 %copy-start.9 = (s32[16]{0:T(128)S(1)}, s32[16]{0:T(128)}, u32[]{:S(2)}) copy-start(s32[16]{0:T(128)} %constant.158.clone) | copy-start | bytes 196
  32.9 43.4 %copy-start.10 = (s32[16]{0:T(128)S(1)}, s32[16]{0:T(128)}, u32[]{:S(2)}) copy-start(s32[16]{0:T(128)} %constant.157.clone) | copy-start | bytes 196
  45.2 5.9 %copy-start.4 = (bf16[512,1024]{1,0:T(8,128)(2,1)}, bf16[512,1024]{1,0:T(8,128)(2,1)S(1)}, u32[]{:S(2)}) copy-start(bf16[512,1024]{1,0:T(8,128)(2,1)S(1)} %collective-permute-done.3.p2) | copy-start | bytes 3145732
  45.2 5.9 %copy-start.5 = (bf16[512,1024]{1,0:T(8,128)(2,1)}, bf16[512,1024]{1,0:T(8,128)(2,1)S(1)}, u32[]{:S(2)}) copy-start(bf16[512,1024]{1,0:T(8,128)(2,1)S(1)} %collective-permute-done.4.p3) | copy-start | bytes 3145732
  45.2 14.9 %collective-permute-start.12 = (bf16[4,16,16,256]{3,2,1,0:T(8,128)(2,1)}, bf16[4,16,16,256]{3,2,1,0:T(8,128)(2,1)S(1)}, u32[]{:S(2)}, u32[]{:S(2)}) collective-permute-start(bf16[4,16,16,256]{3,2,1,0:T(8,128)(2,1)} %collective-permute-done.6.lh), channel_id=1, source_target_pairs={{0,96},{1,97},{2,98},{3,99},{4,100},{5,101},{6,102},{7,103},{8,40}... | collective-permute-start | bytes 1572872 | tf_op jit(solution)/shard_map/ppermute | solution.py:28
  47.8 13.0 %collective-permute-start.11 = (bf16[4,16,16,256]{3,2,1,0:T(8,128)(2,1)}, bf16[4,16,16,256]{3,2,1,0:T(8,128)(2,1)}, u32[]{:S(2)}, u32[]{:S(2)}) collective-permute-start(bf16[4,16,16,256]{3,2,1,0:T(8,128)(2,1)} %collective-permute-done.6.lh), channel_id=1, source_target_pairs={{0,32},{1,33},{2,34},{3,35},{4,36},{5,37},{6,38},{7,39},{8,104},{9... | collective-permute-start | bytes 1572872 | tf_op jit(solution)/shard_map/ppermute | solution.py:28
  48.8 20.0 %collective-permute-start.10 = (bf16[3,512,256]{2,1,0:T(8,128)(2,1)}, bf16[3,512,256]{2,1,0:T(8,128)(2,1)S(1)}, u32[]{:S(2)}, u32[]{:S(2)}) collective-permute-start(bf16[3,512,256]{2,1,0:T(8,128)(2,1)} %pad_maximum_fusion.3), channel_id=1, source_target_pairs={{0,1},{1,0},{2,3},{3,2},{4,5},{5,4},{6,7},{7,6},{8,9},{9,8},{10,11... | collective-permute-start | bytes 2359304 | tf_op jit(solution)/shard_map/ppermute | solution.py:28
  49.1 21.6 %collective-permute-start.9 = (bf16[512,768]{1,0:T(8,128)(2,1)}, bf16[512,768]{1,0:T(8,128)(2,1)S(1)}, u32[]{:S(2)}, u32[]{:S(2)}) collective-permute-start(bf16[512,768]{1,0:T(8,128)(2,1)} %slice.16), channel_id=1, source_target_pairs={{0,6},{1,7},{2,0},{3,1},{4,2},{5,3},{6,4},{7,5},{8,10},{9,11},{10,... | collective-permute-start | bytes 2359304 | tf_op jit(solution)/shard_map/ppermute | solution.py:28
  50.8 19.9 %collective-permute-start.8 = (bf16[512,768]{1,0:T(8,128)(2,1)}, bf16[512,768]{1,0:T(8,128)(2,1)S(1)}, u32[]{:S(2)}, u32[]{:S(2)}) collective-permute-start(bf16[512,768]{1,0:T(8,128)(2,1)} %slice.16), channel_id=1, source_target_pairs={{0,2},{1,3},{2,4},{3,5},{4,6},{5,7},{6,0},{7,1},{8,14},{9,15},{10,... | collective-permute-start | bytes 2359304 | tf_op jit(solution)/shard_map/ppermute | solution.py:28
  60.1 11.1 %copy-start.2 = (bf16[4,16,16,256]{3,2,1,0:T(8,128)(2,1)}, bf16[4,16,16,256]{3,2,1,0:T(8,128)(2,1)S(1)}, u32[]{:S(2)}) copy-start(bf16[4,16,16,256]{3,2,1,0:T(8,128)(2,1)S(1)} %collective-permute-done.12.r2) | copy-start | bytes 1572868
  60.1 14.8 %collective-permute-start.15 = (bf16[4,16,16,256]{3,2,1,0:T(8,128)(2,1)}, bf16[4,16,16,256]{3,2,1,0:T(8,128)(2,1)}, u32[]{:S(2)}, u32[]{:S(2)}) collective-permute-start(bf16[4,16,16,256]{3,2,1,0:T(8,128)(2,1)} %collective-permute-done.6.lh), channel_id=1, source_target_pairs={{0,8},{1,9},{2,10},{3,11},{4,12},{5,13},{6,14},{7,15},{8,0},{9,1},... | collective-permute-start | bytes 1572872 | tf_op jit(solution)/shard_map/ppermute | solution.py:28
  60.8 10.7 %collective-permute-start.17 = (bf16[4,16,16,256]{3,2,1,0:T(8,128)(2,1)}, bf16[4,16,16,256]{3,2,1,0:T(8,128)(2,1)}, u32[]{:S(2)}, u32[]{:S(2)}) collective-permute-start(bf16[4,16,16,256]{3,2,1,0:T(8,128)(2,1)} %collective-permute-done.11.r1), channel_id=1, source_target_pairs={{0,32},{1,33},{2,34},{3,35},{4,36},{5,37},{6,38},{7,39},{8,104},{9... | collective-permute-start | bytes 1572872 | tf_op jit(solution)/shard_map/ppermute | solution.py:28
  68.8 7.5 %collective-permute-start.16 = (bf16[2,4,16,16,256]{4,3,2,1,0:T(8,128)(2,1)}, bf16[2,4,16,16,256]{4,3,2,1,0:T(8,128)(2,1)}, u32[]{:S(2)}, u32[]{:S(2)}) collective-permute-start(bf16[2,4,16,16,256]{4,3,2,1,0:T(8,128)(2,1)} %pad_maximum_fusion.2), channel_id=1, source_target_pairs={{0,8},{1,9},{2,10},{3,11},{4,12},{5,13},{6,14},{7,15},{8,0},{9,1},... | collective-permute-start | bytes 3145736 | tf_op jit(solution)/shard_map/ppermute | solution.py:28
  70.6 5.7 %collective-permute-start.13 = (bf16[2,4,16,16,256]{4,3,2,1,0:T(8,128)(2,1)}, bf16[2,4,16,16,256]{4,3,2,1,0:T(8,128)(2,1)}, u32[]{:S(2)}, u32[]{:S(2)}) collective-permute-start(bf16[2,4,16,16,256]{4,3,2,1,0:T(8,128)(2,1)} %pad_maximum_fusion.x0), channel_id=1, source_target_pairs={{0,8},{1,9},{2,10},{3,11},{4,12},{5,13},{6,14},{7,15},{8,0},{9,1},... | collective-permute-start | bytes 3145736 | tf_op jit(solution)/shard_map/ppermute | solution.py:28
  70.7 5.6 %collective-permute-start.14 = (bf16[2,4,16,16,256]{4,3,2,1,0:T(8,128)(2,1)}, bf16[2,4,16,16,256]{4,3,2,1,0:T(8,128)(2,1)}, u32[]{:S(2)}, u32[]{:S(2)}) collective-permute-start(bf16[2,4,16,16,256]{4,3,2,1,0:T(8,128)(2,1)} %pad_maximum_fusion.1.x1), channel_id=1, source_target_pairs={{0,8},{1,9},{2,10},{3,11},{4,12},{5,13},{6,14},{7,15},{8,0},{9,1},... | collective-permute-start | bytes 3145736 | tf_op jit(solution)/shard_map/ppermute | solution.py:28
  71.5 13.6 %collective-permute-start.19 = (bf16[512,768]{1,0:T(8,128)(2,1)S(1)}, bf16[512,768]{1,0:T(8,128)(2,1)S(1)}, u32[]{:S(2)}, u32[]{:S(2)}) collective-permute-start(bf16[512,768]{1,0:T(8,128)(2,1)S(1)} %collective-permute-done.8.a1), channel_id=1, source_target_pairs={{0,2},{1,3},{2,4},{3,5},{4,6},{5,7},{6,0},{7,1},{8,14},{9,15},{10,... | collective-permute-start | bytes 2359304 | tf_op jit(solution)/shard_map/ppermute | solution.py:28
  74.8 5.3 %collective-permute-start.18 = (bf16[4,16,16,256]{3,2,1,0:T(8,128)(2,1)}, bf16[4,16,16,256]{3,2,1,0:T(8,128)(2,1)S(1)}, u32[]{:S(2)}, u32[]{:S(2)}) collective-permute-start(bf16[4,16,16,256]{3,2,1,0:T(8,128)(2,1)} %collective-permute-done.17.r3), channel_id=1, source_target_pairs={{0,8},{1,9},{2,10},{3,11},{4,12},{5,13},{6,14},{7,15},{8,0},{9,1},... | collective-permute-start | bytes 1572872 | tf_op jit(solution)/shard_map/ppermute | solution.py:28
  85.1 16.9 %copy-start.7 = (f32[4,16,256]{2,1,0:T(8,128)S(1)}, f32[4,16,256]{2,1,0:T(8,128)}, u32[]{:S(2)}) copy-start(f32[4,16,256]{2,1,0:T(8,128)} %param.12) | copy-start | bytes 196612
  87.7 1.6 %collective-permute-start.20 = (bf16[8,4,16,256]{3,2,1,0:T(8,128)(2,1)S(1)}, bf16[8,4,16,256]{3,2,1,0:T(8,128)(2,1)S(1)}, u32[]{:S(2)}, u32[]{:S(2)}) collective-permute-start(bf16[8,4,16,256]{3,2,1,0:T(8,128)(2,1)S(1)} %get-tuple-element.49), channel_id=1, source_target_pairs={{0,8},{1,9},{2,10},{3,11},{4,12},{5,13},{6,14},{7,15},{8,0},{9,1},... | collective-permute-start | bytes 786440 | tf_op jit(solution)/shard_map/ppermute | solution.py:28
